TPU v7x, 32 devices: a whole 2x2x4 slice. The times are simulated.
32 devices in a mesh: grid: 8 (over y, x, core), sta: 4 (over z).
Axes of the slice: x: 2, y: 2, z: 4, core: 2. Of those that a mesh axis runs over, the one named last changes fastest.
Arguments:
- spectra: bfloat16 [64, 2, 6144], P(None, None, 'sta'), may hold values from -6 to 6
- lag_samples: int32 [8, 6144], P('grid', 'sta'), may hold values from 0 to 5999
- slowness: bfloat16 [8, 3, 6144], P('grid', None, 'sta'), may hold values from -3 to 3
- spread_taps: float32 [3, 17], replicated, may hold values from 0.02 to 0.2
Outputs:
- stacked: float32 [8, 32, 8, 128], P('grid')
- deblurred: float32 [8, 32, 8, 128], P('grid')
All inputs are finite; a program needn't handle non-finite values.
Results may differ from a plain program's by a relative error of at most 0.0015.
Values may be sent and summed in bfloat16 or wider, within the bound.
No kernel may reach another device: no remote copies, remote signals or barrier semaphores. Data moves between devices by JAX's collectives and lax.ppermute only.
A program may use at most 64 MiB of HBM per device.

v0:
```python
import math

import jax
import jax.numpy as jnp
from jax import lax
from jax.sharding import PartitionSpec as P

STATIONS = 6144
FREQS = 64
F0 = 600
NT = 6000
TAPS = 17
HALF = 8
ITERS = 4
CX = 32
CY = 8
CZ = 128


TWO_PI = 2.0 * math.pi
BACKGROUND = 0.05


def with_halo(array, sides, width):
    for axis, dim in sides:
        size, length = (lax.axis_size(axis), array.shape[dim])
        up = [(i, (i + 1) % size) for i in range(size - 1)]
        down = [(j, i) for i, j in up]
        last = lax.slice_in_dim(array, length - width, length, axis=dim)
        leading = lax.slice_in_dim(array, 0, width, axis=dim)
        before = lax.ppermute(last, axis, up)
        after = lax.ppermute(leading, axis, down)
        array = jnp.concatenate([before, array, after], axis=dim)
    return array


def align_rows(spectra, lag_row):
    bins = F0 + jnp.arange(FREQS, dtype=jnp.int32)
    cycles = bins[:, None] * lag_row[None, :] % NT
    turned = cycles.astype(jnp.float32) * (TWO_PI / NT)
    cosine = jnp.cos(turned)
    sine = jnp.sin(turned)
    real_in = spectra[:, 0, :].astype(jnp.float32)
    imag_in = spectra[:, 1, :].astype(jnp.float32)
    real_out = real_in * cosine + imag_in * sine
    imag_out = imag_in * cosine - real_in * sine
    return jnp.stack([real_out, imag_out], axis=1).astype(jnp.bfloat16)


def beam_freq(freq, aligned_row, slow_rows):
    omega = (F0 + freq).astype(jnp.float32) * (TWO_PI / NT)
    slow = slow_rows.astype(jnp.float32)
    x_coord = jnp.arange(CX, dtype=jnp.float32) - (CX - 1) / 2.0
    y_coord = jnp.arange(CY, dtype=jnp.float32) - (CY - 1) / 2.0
    z_coord = jnp.arange(CZ, dtype=jnp.float32) - (CZ - 1) / 2.0
    phase_x = (omega * slow[0])[None, :] * x_coord[:, None]
    phase_y = (omega * slow[1])[None, :] * y_coord[:, None]
    phase = phase_x[:, None, :] + phase_y[None, :, :]
    cosine = jnp.cos(phase)
    sine = jnp.sin(phase)
    real_in = aligned_row[0].astype(jnp.float32)[None, None, :]
    imag_in = aligned_row[1].astype(jnp.float32)[None, None, :]
    front_real = (real_in * cosine + imag_in * sine).astype(jnp.bfloat16).reshape(CX * CY, -1)
    front_imag = (imag_in * cosine - real_in * sine).astype(jnp.bfloat16).reshape(CX * CY, -1)
    left_side = jnp.concatenate([front_real, front_imag], axis=1)
    phase_z = (omega * slow[2])[:, None] * z_coord[None, :]
    depth_real = jnp.cos(phase_z).astype(jnp.bfloat16)
    depth_imag = jnp.sin(phase_z).astype(jnp.bfloat16)
    upper_rows = jnp.concatenate([depth_real, -depth_imag], axis=1)
    lower_rows = jnp.concatenate([depth_imag, depth_real], axis=1)
    right_side = jnp.concatenate([upper_rows, lower_rows], axis=0)
    return jnp.dot(left_side, right_side, preferred_element_type=jnp.float32)


def freq_beams(freq_ids, aligned_rows, slow_rows):
    return lax.map(lambda pair: beam_freq(pair[0], pair[1], slow_rows), (freq_ids, aligned_rows))


def band_matrix(taps, length):
    rows = jnp.arange(length, dtype=jnp.int32)[:, None]
    columns = jnp.arange(length + 2 * HALF, dtype=jnp.int32)[None, :]
    offset = columns - rows
    picks = jnp.arange(TAPS, dtype=jnp.int32)[:, None, None]
    return jnp.sum(jnp.where(offset[None] == picks, taps[:, None, None], 0.0), axis=0)


def blur(volume, bands):
    band_x, square_y, square_z = bands
    padded = with_halo(volume.astype(jnp.bfloat16), (("grid", 0),), HALF).astype(volume.dtype)
    along_x = jnp.einsum("ip,pyz->iyz", band_x, padded, precision=lax.Precision.HIGHEST)
    along_y = jnp.einsum("jq,xqz->xjz", square_y, along_x, precision=lax.Precision.HIGHEST)
    return jnp.einsum("xyw,kw->xyk", along_y, square_z, precision=lax.Precision.HIGHEST)


def per_device(spectra, lag_samples, slowness, spread_taps):
    groups = lax.axis_size("sta")
    own_count = FREQS // groups
    first_bin = lax.axis_index("sta") * own_count
    aligned = align_rows(spectra, lag_samples[0])
    own_ids = first_bin + jnp.arange(own_count, dtype=jnp.int32)
    rows = lax.dynamic_slice_in_dim(
        lax.all_gather(aligned, "sta", axis=2, tiled=True), first_bin, own_count, 0
    )
    beams = freq_beams(own_ids, rows, lax.all_gather(slowness, "sta", axis=2, tiled=True)[0])
    squares = jnp.sum(beams * beams, axis=0)
    local_power = squares[:, :CZ] + squares[:, CZ:]
    summed = lax.psum(local_power, "sta")
    stacked = (summed / (FREQS * STATIONS) + BACKGROUND).reshape(CX, CY, CZ)
    square_y = band_matrix(spread_taps[1], CY)[:, HALF : HALF + CY]
    square_z = band_matrix(spread_taps[2], CZ)[:, HALF : HALF + CZ]
    bands = (band_matrix(spread_taps[0], CX), square_y, square_z)
    estimate = stacked
    for sweep in range(ITERS):
        blurred = blur(estimate, bands)
        estimate = estimate * blur(stacked / blurred, bands)
    return (stacked[None], estimate[None])


def solution(mesh):
    placed = (P(None, None, "sta"), P("grid", "sta"), P("grid", None, "sta"), P())
    return jax.shard_map(
        per_device,
        mesh=mesh,
        in_specs=placed,
        out_specs=(P("grid", None, None, None), P("grid", None, None, None)),
        check_vma=False,
    )
```

profile of v0, /device:TPU:0, one launch (start us, length us, event | category | flops | bytes accessed | tf_op | source)
XLA Modules:
  0.0 997.1 jit_solution(16841452278687845361)
XLA Ops:
  12.5 15.1 %all_gather.7 = bf16[1,3,6144]{2,1,0:T(4,128)(2,1)S(1)} all-gather(bf16[1,3,1536]{2,1,0:T(4,128)(2,1)} %param.8), channel_id=1, replica_groups=mesh['grid'=8,'sta'=4] {'sta'}, dimensions={2}, use_global_device_ids=true | all-gather | bytes 46080 | tf_op jit(solution)/shard_map/all_gather | solution.py:104
  28.7 23.9 %all-gather.2.cloned.1.call-done = bf16[64,2,6144]{2,0,1:T(8,128)(2,1)} async-done(((bf16[64,2,1536]{2,0,1:T(8,128)(2,1)}), bf16[64,2,6144]{2,0,1:T(8,128)(2,1)}) %all-gather.2.cloned.1.call-update) | async-done | bytes 1572880 | tf_op jit(solution)/shard_map/all_gather | solution.py:102
  54.0 827.8 %while.12 = (s32[]{:T(128)}, f32[16,256,256]{2,1,0:T(8,128)}, bf16[16,2,6144]{2,1,0:T(2,128)(2,1)S(1)}, s32[16]{0:T(128)S(1)}, bf16[3,6144]{1,0:T(4,128)(2,1)S(1...) while((s32[]{:T(128)}, f32[16,256,256]{2,1,0:T(8,128)}, ...), condition=%wide.region_1.2_spmd, body=%wide.region_0.1_spmd.sunk | while | flops 1669103744 | bytes 24730088 | solution.py:76
  55.6 23.7 %fusion.136 = (bf16[256,6144]{1,0:T(8,128)(2,1)S(1)}, bf16[256,6144]{1,0:T(8,128)(2,1)S(1)}) fusion(f32[6144]{0:T(1024)S(1)} %bitcast.160, f32[8,6144]{1,0:T(8,128)S(1)} %broadcast_multiply_fusion.4, f32[32,6144]{1,0:T(8,128)S(1)} %broadcast_multiply_fusion.5, f32[6144]{0:T(1024)S(1)} %bitcast.159), kind=kLoop, calls=%fused_computation.6.clone.1 | loop fusion | flops 14155776 | bytes 7323648 | tf_op jit(solution)/shard_map/while/body/eval_jaxpr/convert_element_type | solution.py:63
  79.4 12.3 %fusion.134 = (bf16[6144,128]{1,0:T(8,128)(2,1)S(1)}, bf16[6144,128]{1,0:T(8,128)(2,1)S(1)}) fusion(f32[128]{0:T(128)S(1)} %iota_add_fusion.8, f32[6144]{0:T(1024)S(1)} %bitcast.157), kind=kLoop, calls=%fused_computation.26.clone.2 | loop fusion | flops 2359296 | bytes 3170816 | tf_op jit(solution)/shard_map/while/body/eval_jaxpr/convert_element_type | solution.py:68
  107.4 23.7 %fusion.136 = (bf16[256,6144]{1,0:T(8,128)(2,1)S(1)}, bf16[256,6144]{1,0:T(8,128)(2,1)S(1)}) fusion(f32[6144]{0:T(1024)S(1)} %bitcast.160, f32[8,6144]{1,0:T(8,128)S(1)} %broadcast_multiply_fusion.4, f32[32,6144]{1,0:T(8,128)S(1)} %broadcast_multiply_fusion.5, f32[6144]{0:T(1024)S(1)} %bitcast.159), kind=kLoop, calls=%fused_computation.6.clone.1 | loop fusion | flops 14155776 | bytes 7323648 | tf_op jit(solution)/shard_map/while/body/eval_jaxpr/convert_element_type | solution.py:63
  131.1 12.3 %fusion.134 = (bf16[6144,128]{1,0:T(8,128)(2,1)S(1)}, bf16[6144,128]{1,0:T(8,128)(2,1)S(1)}) fusion(f32[128]{0:T(128)S(1)} %iota_add_fusion.8, f32[6144]{0:T(1024)S(1)} %bitcast.157), kind=kLoop, calls=%fused_computation.26.clone.2 | loop fusion | flops 2359296 | bytes 3170816 | tf_op jit(solution)/shard_map/while/body/eval_jaxpr/convert_element_type | solution.py:68
  159.1 23.7 %fusion.136 = (bf16[256,6144]{1,0:T(8,128)(2,1)S(1)}, bf16[256,6144]{1,0:T(8,128)(2,1)S(1)}) fusion(f32[6144]{0:T(1024)S(1)} %bitcast.160, f32[8,6144]{1,0:T(8,128)S(1)} %broadcast_multiply_fusion.4, f32[32,6144]{1,0:T(8,128)S(1)} %broadcast_multiply_fusion.5, f32[6144]{0:T(1024)S(1)} %bitcast.159), kind=kLoop, calls=%fused_computation.6.clone.1 | loop fusion | flops 14155776 | bytes 7323648 | tf_op jit(solution)/shard_map/while/body/eval_jaxpr/convert_element_type | solution.py:63
  182.9 12.3 %fusion.134 = (bf16[6144,128]{1,0:T(8,128)(2,1)S(1)}, bf16[6144,128]{1,0:T(8,128)(2,1)S(1)}) fusion(f32[128]{0:T(128)S(1)} %iota_add_fusion.8, f32[6144]{0:T(1024)S(1)} %bitcast.157), kind=kLoop, calls=%fused_computation.26.clone.2 | loop fusion | flops 2359296 | bytes 3170816 | tf_op jit(solution)/shard_map/while/body/eval_jaxpr/convert_element_type | solution.py:68
  210.8 23.7 %fusion.136 = (bf16[256,6144]{1,0:T(8,128)(2,1)S(1)}, bf16[256,6144]{1,0:T(8,128)(2,1)S(1)}) fusion(f32[6144]{0:T(1024)S(1)} %bitcast.160, f32[8,6144]{1,0:T(8,128)S(1)} %broadcast_multiply_fusion.4, f32[32,6144]{1,0:T(8,128)S(1)} %broadcast_multiply_fusion.5, f32[6144]{0:T(1024)S(1)} %bitcast.159), kind=kLoop, calls=%fused_computation.6.clone.1 | loop fusion | flops 14155776 | bytes 7323648 | tf_op jit(solution)/shard_map/while/body/eval_jaxpr/convert_element_type | solution.py:63
  234.6 12.3 %fusion.134 = (bf16[6144,128]{1,0:T(8,128)(2,1)S(1)}, bf16[6144,128]{1,0:T(8,128)(2,1)S(1)}) fusion(f32[128]{0:T(128)S(1)} %iota_add_fusion.8, f32[6144]{0:T(1024)S(1)} %bitcast.157), kind=kLoop, calls=%fused_computation.26.clone.2 | loop fusion | flops 2359296 | bytes 3170816 | tf_op jit(solution)/shard_map/while/body/eval_jaxpr/convert_element_type | solution.py:68
  262.6 23.7 %fusion.136 = (bf16[256,6144]{1,0:T(8,128)(2,1)S(1)}, bf16[256,6144]{1,0:T(8,128)(2,1)S(1)}) fusion(f32[6144]{0:T(1024)S(1)} %bitcast.160, f32[8,6144]{1,0:T(8,128)S(1)} %broadcast_multiply_fusion.4, f32[32,6144]{1,0:T(8,128)S(1)} %broadcast_multiply_fusion.5, f32[6144]{0:T(1024)S(1)} %bitcast.159), kind=kLoop, calls=%fused_computation.6.clone.1 | loop fusion | flops 14155776 | bytes 7323648 | tf_op jit(solution)/shard_map/while/body/eval_jaxpr/convert_element_type | solution.py:63
  314.3 23.7 %fusion.136 = (bf16[256,6144]{1,0:T(8,128)(2,1)S(1)}, bf16[256,6144]{1,0:T(8,128)(2,1)S(1)}) fusion(f32[6144]{0:T(1024)S(1)} %bitcast.160, f32[8,6144]{1,0:T(8,128)S(1)} %broadcast_multiply_fusion.4, f32[32,6144]{1,0:T(8,128)S(1)} %broadcast_multiply_fusion.5, f32[6144]{0:T(1024)S(1)} %bitcast.159), kind=kLoop, calls=%fused_computation.6.clone.1 | loop fusion | flops 14155776 | bytes 7323648 | tf_op jit(solution)/shard_map/while/body/eval_jaxpr/convert_element_type | solution.py:63
  366.0 23.7 %fusion.136 = (bf16[256,6144]{1,0:T(8,128)(2,1)S(1)}, bf16[256,6144]{1,0:T(8,128)(2,1)S(1)}) fusion(f32[6144]{0:T(1024)S(1)} %bitcast.160, f32[8,6144]{1,0:T(8,128)S(1)} %broadcast_multiply_fusion.4, f32[32,6144]{1,0:T(8,128)S(1)} %broadcast_multiply_fusion.5, f32[6144]{0:T(1024)S(1)} %bitcast.159), kind=kLoop, calls=%fused_computation.6.clone.1 | loop fusion | flops 14155776 | bytes 7323648 | tf_op jit(solution)/shard_map/while/body/eval_jaxpr/convert_element_type | solution.py:63
  417.8 23.7 %fusion.136 = (bf16[256,6144]{1,0:T(8,128)(2,1)S(1)}, bf16[256,6144]{1,0:T(8,128)(2,1)S(1)}) fusion(f32[6144]{0:T(1024)S(1)} %bitcast.160, f32[8,6144]{1,0:T(8,128)S(1)} %broadcast_multiply_fusion.4, f32[32,6144]{1,0:T(8,128)S(1)} %broadcast_multiply_fusion.5, f32[6144]{0:T(1024)S(1)} %bitcast.159), kind=kLoop, calls=%fused_computation.6.clone.1 | loop fusion | flops 14155776 | bytes 7323648 | tf_op jit(solution)/shard_map/while/body/eval_jaxpr/convert_element_type | solution.py:63
  469.5 23.7 %fusion.136 = (bf16[256,6144]{1,0:T(8,128)(2,1)S(1)}, bf16[256,6144]{1,0:T(8,128)(2,1)S(1)}) fusion(f32[6144]{0:T(1024)S(1)} %bitcast.160, f32[8,6144]{1,0:T(8,128)S(1)} %broadcast_multiply_fusion.4, f32[32,6144]{1,0:T(8,128)S(1)} %broadcast_multiply_fusion.5, f32[6144]{0:T(1024)S(1)} %bitcast.159), kind=kLoop, calls=%fused_computation.6.clone.1 | loop fusion | flops 14155776 | bytes 7323648 | tf_op jit(solution)/shard_map/while/body/eval_jaxpr/convert_element_type | solution.py:63
  521.3 23.7 %fusion.136 = (bf16[256,6144]{1,0:T(8,128)(2,1)S(1)}, bf16[256,6144]{1,0:T(8,128)(2,1)S(1)}) fusion(f32[6144]{0:T(1024)S(1)} %bitcast.160, f32[8,6144]{1,0:T(8,128)S(1)} %broadcast_multiply_fusion.4, f32[32,6144]{1,0:T(8,128)S(1)} %broadcast_multiply_fusion.5, f32[6144]{0:T(1024)S(1)} %bitcast.159), kind=kLoop, calls=%fused_computation.6.clone.1 | loop fusion | flops 14155776 | bytes 7323648 | tf_op jit(solution)/shard_map/while/body/eval_jaxpr/convert_element_type | solution.py:63
  573.0 23.7 %fusion.136 = (bf16[256,6144]{1,0:T(8,128)(2,1)S(1)}, bf16[256,6144]{1,0:T(8,128)(2,1)S(1)}) fusion(f32[6144]{0:T(1024)S(1)} %bitcast.160, f32[8,6144]{1,0:T(8,128)S(1)} %broadcast_multiply_fusion.4, f32[32,6144]{1,0:T(8,128)S(1)} %broadcast_multiply_fusion.5, f32[6144]{0:T(1024)S(1)} %bitcast.159), kind=kLoop, calls=%fused_computation.6.clone.1 | loop fusion | flops 14155776 | bytes 7323648 | tf_op jit(solution)/shard_map/while/body/eval_jaxpr/convert_element_type | solution.py:63
  624.7 23.7 %fusion.136 = (bf16[256,6144]{1,0:T(8,128)(2,1)S(1)}, bf16[256,6144]{1,0:T(8,128)(2,1)S(1)}) fusion(f32[6144]{0:T(1024)S(1)} %bitcast.160, f32[8,6144]{1,0:T(8,128)S(1)} %broadcast_multiply_fusion.4, f32[32,6144]{1,0:T(8,128)S(1)} %broadcast_multiply_fusion.5, f32[6144]{0:T(1024)S(1)} %bitcast.159), kind=kLoop, calls=%fused_computation.6.clone.1 | loop fusion | flops 14155776 | bytes 7323648 | tf_op jit(solution)/shard_map/while/body/eval_jaxpr/convert_element_type | solution.py:63
  676.5 23.7 %fusion.136 = (bf16[256,6144]{1,0:T(8,128)(2,1)S(1)}, bf16[256,6144]{1,0:T(8,128)(2,1)S(1)}) fusion(f32[6144]{0:T(1024)S(1)} %bitcast.160, f32[8,6144]{1,0:T(8,128)S(1)} %broadcast_multiply_fusion.4, f32[32,6144]{1,0:T(8,128)S(1)} %broadcast_multiply_fusion.5, f32[6144]{0:T(1024)S(1)} %bitcast.159), kind=kLoop, calls=%fused_computation.6.clone.1 | loop fusion | flops 14155776 | bytes 7323648 | tf_op jit(solution)/shard_map/while/body/eval_jaxpr/convert_element_type | solution.py:63
  728.2 23.7 %fusion.136 = (bf16[256,6144]{1,0:T(8,128)(2,1)S(1)}, bf16[256,6144]{1,0:T(8,128)(2,1)S(1)}) fusion(f32[6144]{0:T(1024)S(1)} %bitcast.160, f32[8,6144]{1,0:T(8,128)S(1)} %broadcast_multiply_fusion.4, f32[32,6144]{1,0:T(8,128)S(1)} %broadcast_multiply_fusion.5, f32[6144]{0:T(1024)S(1)} %bitcast.159), kind=kLoop, calls=%fused_computation.6.clone.1 | loop fusion | flops 14155776 | bytes 7323648 | tf_op jit(solution)/shard_map/while/body/eval_jaxpr/convert_element_type | solution.py:63
  779.9 23.7 %fusion.136 = (bf16[256,6144]{1,0:T(8,128)(2,1)S(1)}, bf16[256,6144]{1,0:T(8,128)(2,1)S(1)}) fusion(f32[6144]{0:T(1024)S(1)} %bitcast.160, f32[8,6144]{1,0:T(8,128)S(1)} %broadcast_multiply_fusion.4, f32[32,6144]{1,0:T(8,128)S(1)} %broadcast_multiply_fusion.5, f32[6144]{0:T(1024)S(1)} %bitcast.159), kind=kLoop, calls=%fused_computation.6.clone.1 | loop fusion | flops 14155776 | bytes 7323648 | tf_op jit(solution)/shard_map/while/body/eval_jaxpr/convert_element_type | solution.py:63
  831.7 23.7 %fusion.136 = (bf16[256,6144]{1,0:T(8,128)(2,1)S(1)}, bf16[256,6144]{1,0:T(8,128)(2,1)S(1)}) fusion(f32[6144]{0:T(1024)S(1)} %bitcast.160, f32[8,6144]{1,0:T(8,128)S(1)} %broadcast_multiply_fusion.4, f32[32,6144]{1,0:T(8,128)S(1)} %broadcast_multiply_fusion.5, f32[6144]{0:T(1024)S(1)} %bitcast.159), kind=kLoop, calls=%fused_computation.6.clone.1 | loop fusion | flops 14155776 | bytes 7323648 | tf_op jit(solution)/shard_map/while/body/eval_jaxpr/convert_element_type | solution.py:63
  885.1 33.4 %all-reduce.2.cloned.1.call-done = f32[256,128]{1,0:T(8,128)} async-done(((f32[256,128]{1,0:T(8,128)}), f32[256,128]{1,0:T(8,128)}) %all-reduce.2.cloned.1.call-update) | async-done | bytes 131088 | tf_op jit(solution)/shard_map/psum | solution.py:107
  (286 shorter events, 469.5 us)
Async XLA Ops:
  7.2 45.4 %all-gather.2.cloned.1.call-start = ((), (), s32[]{:S(2)}) async-start(), calls=%async_computation | async-start | bytes 1966080 | tf_op jit(solution)/shard_map/all_gather | solution.py:102
  12.5 906.0 %all-reduce.2.cloned.1.call-start = ((), (), s32[]{:S(2)}) async-start(), calls=%async_computation.1 | async-start | bytes 262144 | tf_op jit(solution)/shard_map/psum | solution.py:107
  918.5 44.7 %copy-start = (f32[256,128]{1,0:T(8,128)S(1)}, f32[256,128]{1,0:T(8,128)}, u32[]{:S(2)}) copy-start(f32[256,128]{1,0:T(8,128)} %all-reduce.2.cloned.1.call-done) | copy-start | bytes 393220
  919.5 2.7 collective-permute-start
  920.8 4.7 collective-permute-start.1
  927.3 5.7 collective-permute-start.2
  931.7 3.1 collective-permute-start.3
  936.5 5.9 collective-permute-start.4
  941.1 3.1 collective-permute-start.5
  945.9 6.3 collective-permute-start.6
  950.8 3.1 collective-permute-start.7
  954.7 6.1 collective-permute-start.8
  959.5 3.1 collective-permute-start.9
  963.4 6.1 collective-permute-start.10
  968.3 3.1 collective-permute-start.11
  972.2 6.1 collective-permute-start.12
  977.0 3.1 collective-permute-start.13
  980.9 6.8 collective-permute-start.14
  985.7 3.1 collective-permute-start.15
Sparse Core Ops, SparseCore 0:
  12.6 39.9 all-gather.1
  885.1 33.3 all-reduce.1
where the time goes:
time: 1000 us; the launch traced here: 997 us
  other arithmetic  776 us (78%)
  waiting for transfers between devices  72.1 us (7%)
  matrix products  49.6 us (5%)
  starting transfers between devices  45 us (4%)
  blocking collectives  15.1 us (2%)
  between operations  14.6 us (1%)
  local copies, waits for them, and re-layouts  13.4 us (1%)
  loops' own time  11.6 us (1%)
    convert_element_type x16, other arithmetic, beam_freq(): (real_in * cosine + imag_in * sine).astype(jnp.bfloat16)  380 us
    convert_element_type x16, other arithmetic, beam_freq(): depth_imag = jnp.sin(phase_z).astype(jnp.bfloat16)  197 us
    neg x16, other arithmetic, beam_freq(): upper_rows = jnp.concatenate([depth_real, -depth_imag], axis=1)  184 us
    dot_general x16, matrix products, beam_freq(): return jnp.dot(left_side, right_side, preferred_element_type=jnp.float32)  40 us
    ppermute x8, starting transfers between devices, with_halo(): before = lax.ppermute(last, axis, up)  34.4 us
    psum x1, waiting for transfers between devices, per_device(): summed = lax.psum(local_power, 'sta')  33.4 us
    all_gather x1, waiting for transfers between devices, per_device(): lax.all_gather(aligned, 'sta', axis=2, tiled=True)  23.9 us
  transfers between devices with their start and end apart: 18, of which 10 were waited for; matrix products, arithmetic and copies ran while one was open for 0% of the time, Pallas kernels for 0%

commit v1 on v0

v1 whole, which is shorter than its diff:
```python
import functools
import math

import jax
import jax.numpy as jnp
from jax import lax
from jax.experimental import pallas as pl
from jax.experimental.pallas import tpu as pltpu
from jax.sharding import PartitionSpec as P

F0 = 600
NT = 6000
TAPS = 17
HALF = 8
ITERS = 4
CX = 32
CY = 8
CZ = 128
LANES = 128

TWO_PI = 2.0 * math.pi
BACKGROUND = 0.05

FA, FB, DA, DB = 0, 16, 32, 64
ENTRIES = 72


def sincos(t):
    u = t * t
    s = t * (1.0 + u * (-1 / 6 + u * (1 / 120 + u * (-1 / 5040 + u * (1 / 362880 - u * (1 / 39916800))))))
    c = 1.0 + u * (-1 / 2 + u * (1 / 24 + u * (-1 / 720 + u * (1 / 40320 - u * (1 / 3628800)))))
    return c, s


def doubled(cs):
    c, s = cs
    t = s + s
    return 1.0 - t * s, t * c


def times(p, q):
    return p[0] * q[0] - p[1] * q[1], p[0] * q[1] + p[1] * q[0]


def beam_kernel(groups, own, width, first_ref, *refs):
    x_refs, (out_ref, xs, com, tab, left, right, acc, work) = refs[:groups], refs[groups:]
    parts = width // LANES
    cols = 2 * width
    for g in range(groups):
        xs[g] = x_refs[g][:, :cols]
        common = x_refs[g][:, cols:].astype(jnp.float32)
        for piece in range(com.shape[1]):
            com[g, piece] = common[:, piece * LANES : (piece + 1) * LANES]
    pieces = com.shape[1]
    bins = (lax.broadcasted_iota(jnp.int32, (own, LANES), 0) + (first_ref[0] + F0)).astype(jnp.float32)
    half_omega = bins * (TWO_PI / NT / 2.0)

    def tables(g, i):
        def common(which):
            index = which * parts + i
            row = com[g, index % pieces, pl.ds(index // pieces, 1), :]
            return jnp.broadcast_to(row, (own, LANES))

        lag = common(0) * 64.0 + common(1)
        turns = bins * lag
        rest = turns - jnp.floor(turns * (1.0 / NT) + 0.5) * float(NT)
        turn = doubled(doubled(sincos(rest * (TWO_PI / NT / 4.0))))
        re = xs[g, :, pl.ds(pl.multiple_of(i * LANES, LANES), LANES)].astype(jnp.float32)
        im = xs[g, :, pl.ds(pl.multiple_of(width + i * LANES, LANES), LANES)].astype(jnp.float32)
        al = re * turn[0] + im * turn[1], im * turn[0] - re * turn[1]

        def put(entry, value):
            tab[i, entry * own : (entry + 1) * own, :] = value

        xl = [sincos(half_omega * common(2))]
        for _ in range(4):
            xl.append(doubled(xl[-1]))
        yl = [sincos(half_omega * common(3))]
        for _ in range(2):
            yl.append(doubled(yl[-1]))

        def products(levels):
            rows = [None]
            for level in levels:
                rows = [level[bit] if row is None else row * level[bit] for bit in range(2) for row in rows]
            return rows

        for entry, value in enumerate(products(yl + xl[:1])):
            put(FA + entry, value)
        for entry, value in enumerate(products(xl[1:])):
            put(FB + entry, value)

        half = sincos(half_omega * common(4))
        rows = [half]
        power = half
        for _ in range(4):
            power = doubled(power)
            rows = rows + [times(row, power) for row in rows]
        for entry, value in enumerate(rows):
            put(DA + entry, value[0])
            put(DA + 16 + entry, value[1])
        e16 = doubled(power)
        e48 = times(e16, doubled(e16))
        for low, high, e in ((0, 3, e48), (1, 2, e16)):
            rc, ms, mc, rs = al[0] * e[0], al[1] * e[1], al[1] * e[0], al[0] * e[1]
            put(DB + high, rc + ms)
            put(DB + 4 + high, mc - rs)
            put(DB + low, rc - ms)
            put(DB + 4 + low, mc + rs)

    def beams(g, f):
        def rows16(entry, i):
            return tab[i, pl.ds(entry * own + f, 16, stride=own), :].astype(jnp.bfloat16)

        def spread(entry, i):
            row = tab[i, pl.ds(entry * own + f, 1), :]
            return jnp.broadcast_to(row, (16, LANES)).astype(jnp.bfloat16)

        for i in range(parts):
            lanes = slice(i * LANES, (i + 1) * LANES)
            a = rows16(FA, i)
            for b in range(16):
                left[b * 16 : (b + 1) * 16, lanes] = a * spread(FB + b, i)
            ar, ai = rows16(DA, i), rows16(DA + 16, i)
            for h in range(4):
                br, bi = spread(DB + h, i), spread(DB + 4 + h, i)
                rr, ii, ri, ir = ar * br, ai * bi, ar * bi, ai * br
                right[h * 32 : h * 32 + 16, lanes] = rr + ii
                right[h * 32 + 16 : h * 32 + 32, lanes] = rr - ii
                right[CZ + h * 32 : CZ + h * 32 + 16, lanes] = ri - ir
                right[CZ + h * 32 + 16 : CZ + h * 32 + 32, lanes] = ri + ir
        got = lax.dot_general(left[...], right[...], (((1,), (1,)), ((), ())), preferred_element_type=jnp.float32)

        @pl.when(g == 0)
        def _():
            acc[f] = got

        @pl.when(g > 0)
        def _():
            acc[f] = acc[f] + got

    def group(g, carry):
        lax.fori_loop(0, parts, lambda i, c: (tables(g, i), c)[1], 0)
        lax.fori_loop(0, own, lambda f, c: (beams(g, f), c)[1], 0)
        return carry

    lax.fori_loop(0, groups, group, 0)

    def butterfly(values, levels):
        for level in range(levels):
            step = 1 << level
            out = list(values)
            for at in range(len(values)):
                if not at & step:
                    (cr, ci), (sr, si) = values[at], values[at + step]
                    out[at] = (cr - si, ci + sr)
                    out[at + step] = (cr + si, ci - sr)
            values = out
        return values

    def power(f, total):
        values = [(acc[f, 8 * x : 8 * x + 8, :CZ], acc[f, 8 * x : 8 * x + 8, CZ:]) for x in range(CX)]
        for x, (re, im) in enumerate(butterfly(values, 5)):
            work[0, 8 * x : 8 * x + 8, :] = re
            work[1, 8 * x : 8 * x + 8, :] = im
        values = [(work[0, pl.ds(y, CX, stride=8), :], work[1, pl.ds(y, CX, stride=8), :]) for y in range(CY)]
        for y, (re, im) in enumerate(butterfly(values, 3)):
            part = re * re + im * im
            prev = out_ref[:, y * CZ : (y + 1) * CZ]
            out_ref[:, y * CZ : (y + 1) * CZ] = jnp.where(f == 0, part, prev + part)
        return total

    lax.fori_loop(0, own, power, 0)
    src = lax.broadcasted_iota(jnp.int32, (CZ, CZ), 0)
    dst = lax.broadcasted_iota(jnp.int32, (CZ, CZ), 1)
    low = src % 16
    place = (src // 32) * 32 + jnp.where((src // 16) % 2 == 0, 16 + low, 15 - low)
    swap = (place == dst).astype(jnp.float32)
    for y in range(CY):
        lanes = slice(y * CZ, (y + 1) * CZ)
        out_ref[:, lanes] = jnp.dot(
            out_ref[:, lanes], swap, precision=lax.Precision.HIGHEST, preferred_element_type=jnp.float32
        )


def split(v):
    high = v.astype(jnp.bfloat16)
    return high, (v - high.astype(jnp.float32)).astype(jnp.bfloat16)


def dot3(a, b):
    dot = functools.partial(jnp.dot, preferred_element_type=jnp.float32)
    return dot(a[0], b[0]) + (dot(a[0], b[1]) + dot(a[1], b[0]))


def deblur_kernel(count, scale, at_ref, taps_ref, own_ref, m2, m1, p1, p2, stacked_ref, est_ref):
    rows, cols = 5 * CX, CY * CZ
    start = (at_ref[0] - 2) * CX

    def inside(first, length):
        x = lax.broadcasted_iota(jnp.int32, (length, cols), 0) + (start + first)
        return (x >= 0) & (x < count * CX)

    stacked = own_ref[...] * scale + BACKGROUND
    halo = [ref[...].astype(jnp.float32) * scale + BACKGROUND for ref in (m2, m1, p1, p2)]
    observed = jnp.concatenate(halo[:2] + [stacked] + halo[2:], axis=0)
    observed = jnp.where(inside(0, rows), observed, 0.0)
    for y in range(CY):
        stacked_ref[:, y, :] = stacked[:, y * CZ : (y + 1) * CZ]

    def band(axis, offset):
        total = jnp.zeros(offset.shape, jnp.float32)
        for tap in range(TAPS):
            total = jnp.where(offset == tap, taps_ref[axis, tap], total)
        return total

    i = lax.broadcasted_iota(jnp.int32, (rows - 2 * HALF, rows), 0)
    p = lax.broadcasted_iota(jnp.int32, (rows - 2 * HALF, rows), 1)
    band_x = split(band(0, p - i))
    w = lax.broadcasted_iota(jnp.int32, (2 * CZ, 2 * CZ), 0)
    k = lax.broadcasted_iota(jnp.int32, (2 * CZ, 2 * CZ), 1)
    band_z = split(band(2, jnp.where(w // CZ == k // CZ, w - k + HALF, -1)))

    def blur(v):
        n = v.shape[0]
        x = dot3(tuple(part[: n - 2 * HALF, :n] for part in band_x), split(v))
        along = []
        for j in range(CY):
            total = None
            for q in range(CY):
                term = taps_ref[1, q - j + HALF] * x[:, q * CZ : (q + 1) * CZ]
                total = term if total is None else total + term
            along.append(total)
        out = []
        for j in range(0, CY, 2):
            out.append(dot3(split(jnp.concatenate(along[j : j + 2], axis=1)), band_z))
        return jnp.concatenate(out, axis=1)

    est, first = observed, 0
    for _ in range(ITERS):
        blurred = blur(est)
        first += HALF
        n = blurred.shape[0]
        ok = inside(first, n)
        ratio = jnp.where(ok, observed[first : first + n] / jnp.where(ok, blurred, 1.0), 0.0)
        change = blur(ratio)
        first += HALF
        est = est[2 * HALF : -2 * HALF] * change
    for y in range(CY):
        est_ref[:, y, :] = est[:, y * CZ : (y + 1) * CZ]


def summed_over(value, axis, size):
    if size & (size - 1):
        return lax.psum(value, axis)
    step = 1
    while step < size:
        value = value + lax.ppermute(value, axis, [(i, i ^ step) for i in range(size)])
        step *= 2
    return value


def per_device(groups, tiles, spectra, lag_samples, slowness, spread_taps):
    freqs, _, width = spectra.shape
    own = freqs // groups
    me = lax.axis_index("sta")
    lag = lag_samples[0]
    common = jnp.concatenate(
        [jnp.stack([lag >> 6, lag & 63]).astype(jnp.bfloat16), slowness[0]], axis=0
    ).reshape(-1)
    room = -(-common.size // (own * LANES)) * own * LANES
    common = jnp.pad(common, (0, room - common.size)).reshape(own, -1)
    flat = spectra.reshape(freqs, 2 * width)

    def bundle(dest):
        return jnp.concatenate([lax.dynamic_slice_in_dim(flat, dest * own, own, 0), common], axis=1)

    blocks = [bundle(me)]
    for k in range(1, groups):
        send = [(i, (i + k) % groups) for i in range(groups)]
        blocks.append(lax.ppermute(bundle((me + k) % groups), "sta", send))

    vmem = pl.BlockSpec(memory_space=pltpu.VMEM)
    smem = pl.BlockSpec(memory_space=pltpu.SMEM)
    pieces = common.shape[1] // LANES
    local = pl.pallas_call(
        functools.partial(beam_kernel, groups, own, width),
        out_shape=jax.ShapeDtypeStruct((CX, CY * CZ), jnp.float32),
        in_specs=[smem] + [vmem] * groups,
        out_specs=vmem,
        scratch_shapes=[
            pltpu.VMEM((groups, own, 2 * width), jnp.bfloat16),
            pltpu.VMEM((groups, pieces, own, LANES), jnp.float32),
            pltpu.VMEM((width // LANES, ENTRIES * own, LANES), jnp.float32),
            pltpu.VMEM((CX * CY, width), jnp.bfloat16),
            pltpu.VMEM((2 * CZ, width), jnp.bfloat16),
            pltpu.VMEM((own, CX * CY, 2 * CZ), jnp.float32),
            pltpu.VMEM((2, CX * CY, CZ), jnp.float32),
        ],
        compiler_params=pltpu.CompilerParams(vmem_limit_bytes=48 * 1024 * 1024),
        name="beams",
    )((me * own).astype(jnp.int32).reshape(1), *blocks)

    total = summed_over(local, "sta", groups)
    narrow = total.astype(jnp.bfloat16)
    halo = []
    for shift in (2, 1, -1, -2):
        moves = [(i, i + shift) for i in range(tiles) if 0 <= i + shift < tiles]
        halo.append(lax.ppermute(narrow, "grid", moves))
    tile = jax.ShapeDtypeStruct((CX, CY, CZ), jnp.float32)
    stacked, deblurred = pl.pallas_call(
        functools.partial(deblur_kernel, tiles, 1.0 / (freqs * width * groups)),
        out_shape=(tile, tile),
        in_specs=[smem, smem] + [vmem] * 5,
        out_specs=(vmem, vmem),
        compiler_params=pltpu.CompilerParams(vmem_limit_bytes=48 * 1024 * 1024),
        name="deblur",
    )(lax.axis_index("grid").astype(jnp.int32).reshape(1), spread_taps, total, *halo)
    return stacked[None], deblurred[None]


def solution(mesh):
    placed = (P(None, None, "sta"), P("grid", "sta"), P("grid", None, "sta"), P())
    return jax.shard_map(
        functools.partial(per_device, mesh.shape["sta"], mesh.shape["grid"]),
        mesh=mesh,
        in_specs=placed,
        out_specs=(P("grid", None, None, None), P("grid", None, None, None)),
        check_vma=False,
    )
```

time: 1000 us -> 104 us (0.10)
  other arithmetic: 776 us -> 0.11 us
  Pallas kernels: 0 us -> 59.2 us
  waiting for transfers between devices: 72.1 us -> 22.3 us
  matrix products: 49.6 us -> 0 us
  starting transfers between devices: 45 us -> 17.1 us
  blocking collectives: 15.1 us -> 0 us
  between operations: 14.6 us -> 0.83 us
  loops' own time: 11.6 us -> 0 us
  local copies, waits for them, and re-layouts: 13.4 us -> 2.52 us
    convert_element_type x48 -> x1, other arithmetic: 577 us -> 0.02 us  [per_device(): narrow = total.astype(jnp.bfloat16)]
    neg x16 -> x0, other arithmetic: 184 us -> none  [beam_freq(): upper_rows = jnp.concatenate([depth_real, -depth_imag], axis=1)]
    pallas_call x0 -> x2, Pallas kernels: none -> 59.2 us  [the longest x1 51.8 us: per_device(): pl.pallas_call(functools.partial(beam_kernel, groups, own, width), out_sh...]
    dot_general x40 -> x0, matrix products: 49.6 us -> none  [the longest x16 40 us: beam_freq(): return jnp.dot(left_side, right_side, preferred_element_type=jnp.float32)]
    psum x1 -> x0, waiting for transfers between devices: 33.4 us -> none  [per_device(): summed = lax.psum(local_power, 'sta')]
    ppermute x16 -> x9, starting transfers between devices: 44.9 us -> 17.1 us  [the longest x4 10.2 us: per_device(): halo.append(lax.ppermute(narrow, 'grid', moves))]
    all_gather x1 -> x0, waiting for transfers between devices: 23.9 us -> none  [per_device(): lax.all_gather(aligned, 'sta', axis=2, tiled=True)]
    all_gather x1 -> x0, blocking collectives: 15.1 us -> none  [per_device(): lax.all_gather(slowness, 'sta', axis=2, tiled=True)[0]]
  transfers between devices with their start and end apart: 18 -> 9, of which waited for: 10 -> 6; matrix products, arithmetic and copies ran while one was open for 0% -> 0% of each run, Pallas kernels for 0% -> 0%
where the time goes in v1:
time: 104 us; the launch traced here: 102 us
  Pallas kernels  59.2 us (57%)
  waiting for transfers between devices  22.3 us (21%)
  starting transfers between devices  17.1 us (16%)
  local copies, waits for them, and re-layouts  2.52 us (2%)
    pallas_call x1, Pallas kernels, per_device(): pl.pallas_call(functools.partial(beam_kernel, groups, own, width), out_sh...  51.8 us
    ppermute x2, waiting for transfers between devices, summed_over(): lax.ppermute(value, axis, [(i, i ^ step) for i in range(size)])  11 us
    ppermute x4, starting transfers between devices, per_device(): halo.append(lax.ppermute(narrow, 'grid', moves))  10.2 us
    ppermute x3, waiting for transfers between devices, per_device(): blocks.append(lax.ppermute(bundle((me + k) % groups), 'sta', send))  9.41 us
    pallas_call x1, Pallas kernels, per_device(): pl.pallas_call(functools.partial(deblur_kernel, tiles, 1.0 / (freqs * wid...  7.34 us
    ppermute x3, starting transfers between devices, per_device(): blocks.append(lax.ppermute(bundle((me + k) % groups), 'sta', send))  6.11 us
    unnamed x7, local copies, waits for them, and re-layouts  2.42 us
  transfers between devices with their start and end apart: 9, of which 6 were waited for; matrix products, arithmetic and copies ran while one was open for 0% of the time, Pallas kernels for 0%

profile of v1, /device:TPU:0, one launch (start us, length us, event | category | flops | bytes accessed | tf_op | source)
XLA Modules:
  0.0 102.1 jit_solution(11129407595412560356)
XLA Ops:
  0.7 0.7 copy-done.2
  1.4 0.7 copy-done.1
  2.2 1.0 %copy.6 = bf16[8,8,2,1536]{3,1,2,0:T(8,128)(2,1)S(1)} copy(bf16[8,8,2,1536]{3,2,1,0:T(2,128)(2,1)} %bitcast.8) | data formatting | bytes 786432
  3.3 5.1 %collective-permute-start.2 = (bf16[16,3584]{1,0:T(8,128)(2,1)S(1)}, bf16[16,3584]{1,0:T(8,128)(2,1)S(1)}, u32[]{:S(2)}, u32[]{:S(2)}) collective-permute-start(bf16[16,3584]{1,0:T(8,128)(2,1)S(1)} %get-tuple-element.12), channel_id=1, source_target_pairs={{0,3},{1,0},{2,1},{3,2},{4,7},{5,4},{6,5},{7,6},{8,11},{9,8},{10,9... | collective-permute-start | bytes 344072 | tf_op jit(solution)/shard_map/ppermute | solution.py:281
  8.4 0.0 collective-permute-start
  8.4 1.0 collective-permute-start.1
  9.5 2.5 %collective-permute-done.2.refs_3_ = bf16[16,3584]{1,0:T(8,128)(2,1)S(1)} collective-permute-done((bf16[16,3584]{1,0:T(8,128)(2,1)S(1)}, bf16[16,3584]{1,0:T(8,128)(2,1)S(1)}, u32[]{:S(2)}, u32[]{:S(2)}) %collective-permute-start.2) | collective-permute-done | bytes 114720 | tf_op jit(solution)/shard_map/ppermute | solution.py:281
  12.0 4.2 %collective-permute-done.refs_1_ = bf16[16,3584]{1,0:T(8,128)(2,1)S(1)} collective-permute-done((bf16[16,3584]{1,0:T(8,128)(2,1)S(1)}, bf16[16,3584]{1,0:T(8,128)(2,1)S(1)}, u32[]{:S(2)}, u32[]{:S(2)}) %collective-permute-start) | collective-permute-done | bytes 114720 | tf_op jit(solution)/shard_map/ppermute | solution.py:281
  16.2 2.7 %collective-permute-done.1.refs_2_ = bf16[16,3584]{1,0:T(8,128)(2,1)S(1)} collective-permute-done((bf16[16,3584]{1,0:T(8,128)(2,1)S(1)}, bf16[16,3584]{1,0:T(8,128)(2,1)S(1)}, u32[]{:S(2)}, u32[]{:S(2)}) %collective-permute-start.1) | collective-permute-done | bytes 114720 | tf_op jit(solution)/shard_map/ppermute | solution.py:281
  18.9 51.8 %beams.1 = f32[32,1024]{1,0:T(8,128)S(1)} custom-call(s32[1]{0:T(128)} %bitcast.1.first_ref, bf16[16,3584]{1,0:T(8,128)(2,1)S(1)} %get-tuple-element.15.refs_0_, bf16[16,3584]{1,0:T(8,128)(2,1)S(1)} %collective-permute-done.refs_1_, bf16[16,3584]{1,0:T(8,128)(2,1)S(1)} %collective-permute-done.1.refs_2_, bf16[16,3584]{1,0:T(8,128)(2,1)S(1)} %collective-permute-done.2.refs_3_), custom_call_target="tpu_custom_call" | custom-call | tf_op jit(solution)/shard_map/beams/pallas_call | solution.py:286
  70.7 0.0 collective-permute-start.3
  70.7 5.0 %collective-permute-done.3 = f32[32,1024]{1,0:T(8,128)S(1)} collective-permute-done((f32[32,1024]{1,0:T(8,128)S(1)}, f32[32,1024]{1,0:T(8,128)S(1)}, u32[]{:S(2)}, u32[]{:S(2)}) %collective-permute-start.3) | collective-permute-done | bytes 131104 | tf_op jit(solution)/shard_map/ppermute | solution.py:258
  75.7 0.9 collective-permute-start.4
  76.6 6.1 %collective-permute-done.4 = f32[32,1024]{1,0:T(8,128)S(1)} collective-permute-done((f32[32,1024]{1,0:T(8,128)S(1)}, f32[32,1024]{1,0:T(8,128)S(1)}, u32[]{:S(2)}, u32[]{:S(2)}) %collective-permute-start.4) | collective-permute-done | bytes 131104 | tf_op jit(solution)/shard_map/ppermute | solution.py:258
  82.7 1.3 %collective-permute-start.8 = (bf16[32,1024]{1,0:T(8,128)(2,1)S(1)}, bf16[32,1024]{1,0:T(8,128)(2,1)S(1)}, u32[]{:S(2)}, u32[]{:S(2)}) collective-permute-start(bf16[32,1024]{1,0:T(8,128)(2,1)S(1)} %get-tuple-element.6), channel_id=1, source_target_pairs={{8,0},{12,4},{16,8},{20,12},{24,16},{28,20},{9,1},{13,5},{17,9},{2... | collective-permute-start | bytes 196616 | tf_op jit(solution)/shard_map/ppermute | solution.py:309
  84.0 1.3 %collective-permute-start.7 = (bf16[32,1024]{1,0:T(8,128)(2,1)S(1)}, bf16[32,1024]{1,0:T(8,128)(2,1)S(1)}, u32[]{:S(2)}, u32[]{:S(2)}) collective-permute-start(bf16[32,1024]{1,0:T(8,128)(2,1)S(1)} %get-tuple-element.6), channel_id=1, source_target_pairs={{4,0},{8,4},{12,8},{16,12},{20,16},{24,20},{28,24},{5,1},{9,5},{13... | collective-permute-start | bytes 196616 | tf_op jit(solution)/shard_map/ppermute | solution.py:309
  85.3 3.0 %collective-permute-start.6 = (bf16[32,1024]{1,0:T(8,128)(2,1)S(1)}, bf16[32,1024]{1,0:T(8,128)(2,1)S(1)}, u32[]{:S(2)}, u32[]{:S(2)}) collective-permute-start(bf16[32,1024]{1,0:T(8,128)(2,1)S(1)} %get-tuple-element.6), channel_id=1, source_target_pairs={{0,4},{4,8},{8,12},{12,16},{16,20},{20,24},{24,28},{1,5},{5,9},{9,... | collective-permute-start | bytes 196616 | tf_op jit(solution)/shard_map/ppermute | solution.py:309
  88.3 4.6 %collective-permute-start.5 = (bf16[32,1024]{1,0:T(8,128)(2,1)S(1)}, bf16[32,1024]{1,0:T(8,128)(2,1)S(1)}, u32[]{:S(2)}, u32[]{:S(2)}) collective-permute-start(bf16[32,1024]{1,0:T(8,128)(2,1)S(1)} %get-tuple-element.6), channel_id=1, source_target_pairs={{0,8},{4,12},{8,16},{12,20},{16,24},{20,28},{1,9},{5,13},{9,17},{1... | collective-permute-start | bytes 196616 | tf_op jit(solution)/shard_map/ppermute | solution.py:309
  92.9 0.0 copy-start
  92.9 0.0 collective-permute-done.8.p2
  92.9 0.0 collective-permute-done.7.p1
  92.9 0.0 collective-permute-done.6.m1
  92.9 1.8 %collective-permute-done.5.m2 = bf16[32,1024]{1,0:T(8,128)(2,1)S(1)} collective-permute-done((bf16[32,1024]{1,0:T(8,128)(2,1)S(1)}, bf16[32,1024]{1,0:T(8,128)(2,1)S(1)}, u32[]{:S(2)}, u32[]{:S(2)}) %collective-permute-start.5) | collective-permute-done | bytes 65568 | tf_op jit(solution)/shard_map/ppermute | solution.py:309
  94.7 7.3 %deblur.1 = (f32[32,8,128]{2,1,0:T(8,128)}, f32[32,8,128]{2,1,0:T(8,128)}) custom-call(s32[1]{0:T(128)} %bitcast.at_ref, f32[3,17]{1,0:T(4,128)S(1)} %copy-done, f32[32,1024]{1,0:T(8,128)S(1)} %get-tuple-element.7.own_ref, bf16[32,1024]{1,0:T(8,128)(2,1)S(1)} %collective-permute-done.5.m2, bf16[32,1024]{1,0:T(8,128)(2,1)S(1)} %collective-permute-done.6.m1, ...), custom_call_target="tpu_custom_call" | custom-call | tf_op jit(solution)/shard_map/deblur/pallas_call | solution.py:311
  (12 shorter events, 0.2 us)
Async XLA Ops:
  0.7 0.7 copy-start.2
  1.4 0.7 copy-start.1
  3.3 8.7 %collective-permute-start.2 = (bf16[16,3584]{1,0:T(8,128)(2,1)S(1)}, bf16[16,3584]{1,0:T(8,128)(2,1)S(1)}, u32[]{:S(2)}, u32[]{:S(2)}) collective-permute-start(bf16[16,3584]{1,0:T(8,128)(2,1)S(1)} %get-tuple-element.12), channel_id=1, source_target_pairs={{0,3},{1,0},{2,1},{3,2},{4,7},{5,4},{6,5},{7,6},{8,11},{9,8},{10,9... | collective-permute-start | bytes 344072 | tf_op jit(solution)/shard_map/ppermute | solution.py:281
  8.4 7.7 %collective-permute-start = (bf16[16,3584]{1,0:T(8,128)(2,1)S(1)}, bf16[16,3584]{1,0:T(8,128)(2,1)S(1)}, u32[]{:S(2)}, u32[]{:S(2)}) collective-permute-start(bf16[16,3584]{1,0:T(8,128)(2,1)S(1)} %get-tuple-element.13), channel_id=1, source_target_pairs={{0,1},{1,2},{2,3},{3,0},{4,5},{5,6},{6,7},{7,4},{8,9},{9,10},{10,1... | collective-permute-start | bytes 344072 | tf_op jit(solution)/shard_map/ppermute | solution.py:281
  8.4 10.4 %collective-permute-start.1 = (bf16[16,3584]{1,0:T(8,128)(2,1)S(1)}, bf16[16,3584]{1,0:T(8,128)(2,1)S(1)}, u32[]{:S(2)}, u32[]{:S(2)}) collective-permute-start(bf16[16,3584]{1,0:T(8,128)(2,1)S(1)} %get-tuple-element.14), channel_id=1, source_target_pairs={{0,2},{1,3},{2,0},{3,1},{4,6},{5,7},{6,4},{7,5},{8,10},{9,11},{10,... | collective-permute-start | bytes 344072 | tf_op jit(solution)/shard_map/ppermute | solution.py:281
  70.7 5.0 %collective-permute-start.3 = (f32[32,1024]{1,0:T(8,128)S(1)}, f32[32,1024]{1,0:T(8,128)S(1)}, u32[]{:S(2)}, u32[]{:S(2)}) collective-permute-start(f32[32,1024]{1,0:T(8,128)S(1)} %beams.1), channel_id=1, source_target_pairs={{0,1},{1,0},{2,3},{3,2},{4,5},{5,4},{6,7},{7,6},{8,9},{9,8},{10,11... | collective-permute-start | bytes 393224 | tf_op jit(solution)/shard_map/ppermute | solution.py:258
  75.7 6.9 %collective-permute-start.4 = (f32[32,1024]{1,0:T(8,128)S(1)}, f32[32,1024]{1,0:T(8,128)S(1)}, u32[]{:S(2)}, u32[]{:S(2)}) collective-permute-start(f32[32,1024]{1,0:T(8,128)S(1)} %add.49), channel_id=1, source_target_pairs={{0,2},{1,3},{2,0},{3,1},{4,6},{5,7},{6,4},{7,5},{8,10},{9,11},{10,... | collective-permute-start | bytes 393224 | tf_op jit(solution)/shard_map/ppermute | solution.py:258
  82.7 10.2 %collective-permute-start.8 = (bf16[32,1024]{1,0:T(8,128)(2,1)S(1)}, bf16[32,1024]{1,0:T(8,128)(2,1)S(1)}, u32[]{:S(2)}, u32[]{:S(2)}) collective-permute-start(bf16[32,1024]{1,0:T(8,128)(2,1)S(1)} %get-tuple-element.6), channel_id=1, source_target_pairs={{8,0},{12,4},{16,8},{20,12},{24,16},{28,20},{9,1},{13,5},{17,9},{2... | collective-permute-start | bytes 196616 | tf_op jit(solution)/shard_map/ppermute | solution.py:309
  84.0 8.9 %collective-permute-start.7 = (bf16[32,1024]{1,0:T(8,128)(2,1)S(1)}, bf16[32,1024]{1,0:T(8,128)(2,1)S(1)}, u32[]{:S(2)}, u32[]{:S(2)}) collective-permute-start(bf16[32,1024]{1,0:T(8,128)(2,1)S(1)} %get-tuple-element.6), channel_id=1, source_target_pairs={{4,0},{8,4},{12,8},{16,12},{20,16},{24,20},{28,24},{5,1},{9,5},{13... | collective-permute-start | bytes 196616 | tf_op jit(solution)/shard_map/ppermute | solution.py:309
  85.3 7.6 %collective-permute-start.6 = (bf16[32,1024]{1,0:T(8,128)(2,1)S(1)}, bf16[32,1024]{1,0:T(8,128)(2,1)S(1)}, u32[]{:S(2)}, u32[]{:S(2)}) collective-permute-start(bf16[32,1024]{1,0:T(8,128)(2,1)S(1)} %get-tuple-element.6), channel_id=1, source_target_pairs={{0,4},{4,8},{8,12},{12,16},{16,20},{20,24},{24,28},{1,5},{5,9},{9,... | collective-permute-start | bytes 196616 | tf_op jit(solution)/shard_map/ppermute | solution.py:309
  88.3 6.4 %collective-permute-start.5 = (bf16[32,1024]{1,0:T(8,128)(2,1)S(1)}, bf16[32,1024]{1,0:T(8,128)(2,1)S(1)}, u32[]{:S(2)}, u32[]{:S(2)}) collective-permute-start(bf16[32,1024]{1,0:T(8,128)(2,1)S(1)} %get-tuple-element.6), channel_id=1, source_target_pairs={{0,8},{4,12},{8,16},{12,20},{16,24},{20,28},{1,9},{5,13},{9,17},{1... | collective-permute-start | bytes 196616 | tf_op jit(solution)/shard_map/ppermute | solution.py:309
  92.9 1.9 %copy-start = (f32[3,17]{1,0:T(4,128)S(1)}, f32[3,17]{1,0:T(4,128)}, u32[]{:S(2)}) copy-start(f32[3,17]{1,0:T(4,128)} %taps_ref.1) | copy-start | bytes 616

commit v2 on v1

--- a/solution.py
+++ b/solution.py
@@ -42,20 +42,40 @@
     return p[0] * q[0] - p[1] * q[1], p[0] * q[1] + p[1] * q[0]
 
 
-def beam_kernel(groups, own, width, first_ref, *refs):
-    x_refs, (out_ref, xs, com, tab, left, right, acc, work) = refs[:groups], refs[groups:]
+def butterfly(values, levels):
+    for level in range(levels):
+        step = 1 << level
+        out = list(values)
+        for at in range(len(values)):
+            if not at & step:
+                (cr, ci), (sr, si) = values[at], values[at + step]
+                out[at] = (cr - si, ci + sr)
+                out[at + step] = (cr + si, ci - sr)
+        values = out
+    return values
+
+
+def beam_kernel(chunks, own, width, first, first_ref, *refs):
+    x_refs, refs = refs[:chunks], refs[chunks:]
+    if first:
+        acc, xs, com, tabs, sides = refs[0], refs[1], refs[2], refs[3:4], refs[4:8]
+    else:
+        acc_in, out_ref, xs, com, tabs, sides = refs[0], refs[1], refs[2], refs[3], refs[4:6], refs[6:10]
+        acc, works, sem = refs[10], refs[11:13], refs[13]
+        fetch = pltpu.make_async_copy(acc_in, acc, sem)
+        fetch.start()
     parts = width // LANES
     cols = 2 * width
-    for g in range(groups):
+    pieces = com.shape[1]
+    for g in range(chunks):
         xs[g] = x_refs[g][:, :cols]
         common = x_refs[g][:, cols:].astype(jnp.float32)
-        for piece in range(com.shape[1]):
+        for piece in range(pieces):
             com[g, piece] = common[:, piece * LANES : (piece + 1) * LANES]
-    pieces = com.shape[1]
     bins = (lax.broadcasted_iota(jnp.int32, (own, LANES), 0) + (first_ref[0] + F0)).astype(jnp.float32)
     half_omega = bins * (TWO_PI / NT / 2.0)
 
-    def tables(g, i):
+    def tables(tab, g, i):
         def common(which):
             index = which * parts + i
             row = com[g, index % pieces, pl.ds(index // pieces, 1), :]
@@ -108,7 +128,9 @@
             put(DB + low, rc - ms)
             put(DB + 4 + low, mc + rs)
 
-    def beams(g, f):
+    def operands(tab, side, f):
+        left, right = side
+
         def rows16(entry, i):
             return tab[i, pl.ds(entry * own + f, 16, stride=own), :].astype(jnp.bfloat16)
 
@@ -129,48 +151,60 @@
                 right[h * 32 + 16 : h * 32 + 32, lanes] = rr - ii
                 right[CZ + h * 32 : CZ + h * 32 + 16, lanes] = ri - ir
                 right[CZ + h * 32 + 16 : CZ + h * 32 + 32, lanes] = ri + ir
-        got = lax.dot_general(left[...], right[...], (((1,), (1,)), ((), ())), preferred_element_type=jnp.float32)
-
-        @pl.when(g == 0)
-        def _():
-            acc[f] = got
-
-        @pl.when(g > 0)
-        def _():
-            acc[f] = acc[f] + got
-
-    def group(g, carry):
-        lax.fori_loop(0, parts, lambda i, c: (tables(g, i), c)[1], 0)
-        lax.fori_loop(0, own, lambda f, c: (beams(g, f), c)[1], 0)
-        return carry
-
-    lax.fori_loop(0, groups, group, 0)
-
-    def butterfly(values, levels):
-        for level in range(levels):
-            step = 1 << level
-            out = list(values)
-            for at in range(len(values)):
-                if not at & step:
-                    (cr, ci), (sr, si) = values[at], values[at + step]
-                    out[at] = (cr - si, ci + sr)
-                    out[at + step] = (cr + si, ci - sr)
-            values = out
-        return values
-
-    def power(f, total):
-        values = [(acc[f, 8 * x : 8 * x + 8, :CZ], acc[f, 8 * x : 8 * x + 8, CZ:]) for x in range(CX)]
+
+    def product(side):
+        return lax.dot_general(
+            side[0][...], side[1][...], (((1,), (1,)), ((), ())), preferred_element_type=jnp.float32
+        )
+
+    def add_power(got, work):
+        values = [(got[8 * x : 8 * x + 8, :CZ], got[8 * x : 8 * x + 8, CZ:]) for x in range(CX)]
         for x, (re, im) in enumerate(butterfly(values, 5)):
             work[0, 8 * x : 8 * x + 8, :] = re
             work[1, 8 * x : 8 * x + 8, :] = im
         values = [(work[0, pl.ds(y, CX, stride=8), :], work[1, pl.ds(y, CX, stride=8), :]) for y in range(CY)]
         for y, (re, im) in enumerate(butterfly(values, 3)):
-            part = re * re + im * im
-            prev = out_ref[:, y * CZ : (y + 1) * CZ]
-            out_ref[:, y * CZ : (y + 1) * CZ] = jnp.where(f == 0, part, prev + part)
-        return total
-
-    lax.fori_loop(0, own, power, 0)
+            out_ref[:, y * CZ : (y + 1) * CZ] += re * re + im * im
+
+    pairs = (sides[:2], sides[2:])
+    batch = 4
+    each = parts * batch // own
+
+    def some(n, fn):
+        lax.fori_loop(0, n, lambda i, c: (fn(i), c)[1], 0)
+
+    def both(i):
+        tables(tabs[0], 0, 2 * i)
+        tables(tabs[0], 0, 2 * i + 1)
+
+    some(parts // 2, both)
+    if not first:
+        out_ref[...] = jnp.zeros_like(out_ref)
+        fetch.wait()
+    for g in range(chunks):
+        last = g == chunks - 1
+        tab = tabs[g % len(tabs)]
+        operands(tab, pairs[0], 0)
+
+        def block(q, g=g, last=last, tab=tab):
+            for j in range(batch):
+                f = q * batch + j
+                got = product(pairs[j % 2])
+                operands(tab, pairs[(j + 1) % 2], jnp.minimum(f + 1, own - 1))
+                if first:
+                    acc[f] = got
+                elif last:
+                    add_power(acc[f] + got, works[j % 2])
+                else:
+                    acc[f] = acc[f] + got
+            if not last:
+                for e in range(each):
+                    tables(tabs[(g + 1) % 2], g + 1, q * each + e)
+
+        some(own // batch, block)
+
+    if first:
+        return
     src = lax.broadcasted_iota(jnp.int32, (CZ, CZ), 0)
     dst = lax.broadcasted_iota(jnp.int32, (CZ, CZ), 1)
     low = src % 16
@@ -181,6 +215,40 @@
         out_ref[:, lanes] = jnp.dot(
             out_ref[:, lanes], swap, precision=lax.Precision.HIGHEST, preferred_element_type=jnp.float32
         )
+
+
+def beams_call(chunks, own, width, pieces, first, *args):
+    vmem = pl.BlockSpec(memory_space=pltpu.VMEM)
+    smem = pl.BlockSpec(memory_space=pltpu.SMEM)
+    rows = CX * CY
+    acc = (own, rows, 2 * CZ)
+    side = [pltpu.VMEM((rows, width), jnp.bfloat16), pltpu.VMEM((2 * CZ, width), jnp.bfloat16)]
+    tab = pltpu.VMEM((width // LANES, ENTRIES * own, LANES), jnp.float32)
+    scratch = [
+        pltpu.VMEM((chunks, own, 2 * width), jnp.bfloat16),
+        pltpu.VMEM((chunks, pieces, own, LANES), jnp.float32),
+    ]
+    if first:
+        scratch += [tab] + side * 2
+        out = jax.ShapeDtypeStruct(acc, jnp.float32)
+        specs = [smem] + [vmem] * chunks
+    else:
+        scratch += [tab] * 2 + side * 2 + [pltpu.VMEM(acc, jnp.float32)]
+        scratch += [pltpu.VMEM((2, rows, CZ), jnp.float32)] * 2 + [pltpu.SemaphoreType.DMA]
+        out = jax.ShapeDtypeStruct((CX, CY * CZ), jnp.float32)
+        specs = [smem] + [vmem] * chunks + [pl.BlockSpec(memory_space=pl.ANY)]
+    return pl.pallas_call(
+        functools.partial(beam_kernel, chunks, own, width, first),
+        out_shape=out,
+        in_specs=specs,
+        out_specs=vmem,
+        scratch_shapes=scratch,
+        compiler_params=pltpu.CompilerParams(vmem_limit_bytes=48 * 1024 * 1024),
+        cost_estimate=pl.CostEstimate(
+            flops=2 * chunks * own * rows * 2 * CZ * width, bytes_accessed=8 * own * rows * CZ, transcendentals=0
+        ),
+        name="beams_own" if first else "beams_rest",
+    )(*args)
 
 
 def split(v):
@@ -283,23 +351,9 @@
     vmem = pl.BlockSpec(memory_space=pltpu.VMEM)
     smem = pl.BlockSpec(memory_space=pltpu.SMEM)
     pieces = common.shape[1] // LANES
-    local = pl.pallas_call(
-        functools.partial(beam_kernel, groups, own, width),
-        out_shape=jax.ShapeDtypeStruct((CX, CY * CZ), jnp.float32),
-        in_specs=[smem] + [vmem] * groups,
-        out_specs=vmem,
-        scratch_shapes=[
-            pltpu.VMEM((groups, own, 2 * width), jnp.bfloat16),
-            pltpu.VMEM((groups, pieces, own, LANES), jnp.float32),
-            pltpu.VMEM((width // LANES, ENTRIES * own, LANES), jnp.float32),
-            pltpu.VMEM((CX * CY, width), jnp.bfloat16),
-            pltpu.VMEM((2 * CZ, width), jnp.bfloat16),
-            pltpu.VMEM((own, CX * CY, 2 * CZ), jnp.float32),
-            pltpu.VMEM((2, CX * CY, CZ), jnp.float32),
-        ],
-        compiler_params=pltpu.CompilerParams(vmem_limit_bytes=48 * 1024 * 1024),
-        name="beams",
-    )((me * own).astype(jnp.int32).reshape(1), *blocks)
+    at = (me * own).astype(jnp.int32).reshape(1)
+    held = beams_call(1, own, width, pieces, True, at, blocks[0])
+    local = beams_call(groups - 1, own, width, pieces, False, at, *blocks[1:], held)
 
     total = summed_over(local, "sta", groups)
     narrow = total.astype(jnp.bfloat16)

time: 104 us -> 87.4 us (0.84)
  waiting for transfers between devices: 22.3 us -> 10.7 us
  Pallas kernels: 59.2 us -> 51.8 us
  starting transfers between devices: 17.1 us -> 19.9 us
  other arithmetic: 0.11 us -> 1.51 us
  local copies, waits for them, and re-layouts: 2.52 us -> 1.15 us
    ppermute x3, waiting for transfers between devices: 9.41 us -> 0.01 us  [per_device(): blocks.append(lax.ppermute(bundle((me + k) % groups), 'sta', send))]
    pallas_call x1 -> x2, Pallas kernels: 51.8 us -> 44.5 us  [beams_call(): pl.pallas_call(functools.partial(beam_kernel, chunks, own, width, first),...]
    ppermute x2, starting transfers between devices: 0.86 us -> 3.4 us  [summed_over(): lax.ppermute(value, axis, [(i, i ^ step) for i in range(size)])]
    ppermute x2, waiting for transfers between devices: 11 us -> 8.97 us  [summed_over(): lax.ppermute(value, axis, [(i, i ^ step) for i in range(size)])]
    unnamed x7 -> x3, local copies, waits for them, and re-layouts: 2.42 us -> 1.05 us
  transfers between devices with their start and end apart: 9 -> 9, of which waited for: 6 -> 3; matrix products, arithmetic and copies ran while one was open for 0% -> 0% of each run, Pallas kernels for 0% -> 12%
where the time goes in v2:
time: 87.4 us; the launch traced here: 85.8 us
  Pallas kernels  51.8 us (59%)
  starting transfers between devices  19.9 us (23%)
  waiting for transfers between devices  10.7 us (12%)
  other arithmetic  1.51 us (2%)
  local copies, waits for them, and re-layouts  1.15 us (1%)
    pallas_call x2, Pallas kernels, beams_call(): pl.pallas_call(functools.partial(beam_kernel, chunks, own, width, first),...  44.5 us
    ppermute x4, starting transfers between devices, per_device(): halo.append(lax.ppermute(narrow, 'grid', moves))  10.3 us
    ppermute x2, waiting for transfers between devices, summed_over(): lax.ppermute(value, axis, [(i, i ^ step) for i in range(size)])  8.97 us
    pallas_call x1, Pallas kernels, per_device(): pl.pallas_call(functools.partial(deblur_kernel, tiles, 1.0 / (freqs * wid...  7.32 us
    ppermute x3, starting transfers between devices, per_device(): blocks.append(lax.ppermute(bundle((me + k) % groups), 'sta', send))  6.13 us
    ppermute x2, starting transfers between devices, summed_over(): lax.ppermute(value, axis, [(i, i ^ step) for i in range(size)])  3.4 us
  transfers between devices with their start and end apart: 9, of which 3 were waited for; matrix products, arithmetic and copies ran while one was open for 0% of the time, Pallas kernels for 12%

profile of v2, /device:TPU:0, one launch (start us, length us, event | category | flops | bytes accessed | tf_op | source)
XLA Modules:
  0.0 85.8 jit_solution(3412885676759600461)
XLA Ops:
  0.7 0.7 shift-right-arithmetic_convert_fusion
  1.4 0.7 pad_maximum_fusion.4
  2.2 1.0 %copy.6 = bf16[8,8,2,1536]{3,1,2,0:T(8,128)(2,1)S(1)} copy(bf16[8,8,2,1536]{3,2,1,0:T(2,128)(2,1)} %bitcast.8) | data formatting | bytes 786432
  3.4 4.1 %collective-permute-start.1 = (bf16[16,3584]{1,0:T(8,128)(2,1)S(1)}, bf16[16,3584]{1,0:T(8,128)(2,1)S(1)}, u32[]{:S(2)}, u32[]{:S(2)}) collective-permute-start(bf16[16,3584]{1,0:T(8,128)(2,1)S(1)} %get-tuple-element.13), channel_id=1, source_target_pairs={{0,2},{1,3},{2,0},{3,1},{4,6},{5,7},{6,4},{7,5},{8,10},{9,11},{10,... | collective-permute-start | bytes 344072 | tf_op jit(solution)/shard_map/ppermute | solution.py:349
  7.5 1.3 %collective-permute-start.2 = (bf16[16,3584]{1,0:T(8,128)(2,1)S(1)}, bf16[16,3584]{1,0:T(8,128)(2,1)S(1)}, u32[]{:S(2)}, u32[]{:S(2)}) collective-permute-start(bf16[16,3584]{1,0:T(8,128)(2,1)S(1)} %get-tuple-element.14), channel_id=1, source_target_pairs={{0,3},{1,0},{2,1},{3,2},{4,7},{5,4},{6,5},{7,6},{8,11},{9,8},{10,9... | collective-permute-start | bytes 344072 | tf_op jit(solution)/shard_map/ppermute | solution.py:349
  8.8 0.7 collective-permute-start
  9.5 10.6 %beams_own.1.refs_3_ = f32[16,256,256]{2,1,0:T(8,128)S(1)} custom-call(s32[1]{0:T(128)} %bitcast.1.first_ref, bf16[16,3584]{1,0:T(8,128)(2,1)S(1)} %get-tuple-element.12.refs_0_), custom_call_target="tpu_custom_call" | custom-call | flops 3221225472 | bytes 4194304 | tf_op jit(solution)/shard_map/beams_own/pallas_call | solution.py:240
  20.1 0.0 copy-start
  20.1 0.0 collective-permute-done.1.refs_1_
  20.1 0.0 collective-permute-done.2.refs_2_
  20.1 0.0 collective-permute-done.refs_0_
  20.1 33.9 %beams_rest.1 = f32[32,1024]{1,0:T(8,128)S(1)} custom-call(s32[1]{0:T(128)} %bitcast.1.first_ref, bf16[16,3584]{1,0:T(8,128)(2,1)S(1)} %collective-permute-done.refs_0_, bf16[16,3584]{1,0:T(8,128)(2,1)S(1)} %collective-permute-done.1.refs_1_, bf16[16,3584]{1,0:T(8,128)(2,1)S(1)} %collective-permute-done.2.refs_2_, f32[16,256,256]{2,1,0:T(8,128)S(1)} %beams_own.1.refs_3_), custom_call_target="tpu_custom_call" | custom-call | flops 9663676416 | bytes 4194304 | tf_op jit(solution)/shard_map/beams_rest/pallas_call | solution.py:240
  54.0 1.6 %collective-permute-start.3 = (f32[32,1024]{1,0:T(8,128)S(1)}, f32[32,1024]{1,0:T(8,128)S(1)}, u32[]{:S(2)}, u32[]{:S(2)}) collective-permute-start(f32[32,1024]{1,0:T(8,128)S(1)} %beams_rest.1), channel_id=1, source_target_pairs={{0,1},{1,0},{2,3},{3,2},{4,5},{5,4},{6,7},{7,6},{8,9},{9,8},{10,11... | collective-permute-start | bytes 393224 | tf_op jit(solution)/shard_map/ppermute | solution.py:326
  55.6 3.4 %collective-permute-done.3 = f32[32,1024]{1,0:T(8,128)S(1)} collective-permute-done((f32[32,1024]{1,0:T(8,128)S(1)}, f32[32,1024]{1,0:T(8,128)S(1)}, u32[]{:S(2)}, u32[]{:S(2)}) %collective-permute-start.3) | collective-permute-done | bytes 131104 | tf_op jit(solution)/shard_map/ppermute | solution.py:326
  59.0 1.8 %collective-permute-start.4 = (f32[32,1024]{1,0:T(8,128)S(1)}, f32[32,1024]{1,0:T(8,128)S(1)}, u32[]{:S(2)}, u32[]{:S(2)}) collective-permute-start(f32[32,1024]{1,0:T(8,128)S(1)} %add.49), channel_id=1, source_target_pairs={{0,2},{1,3},{2,0},{3,1},{4,6},{5,7},{6,4},{7,5},{8,10},{9,11},{10,... | collective-permute-start | bytes 393224 | tf_op jit(solution)/shard_map/ppermute | solution.py:326
  60.8 5.6 %collective-permute-done.4 = f32[32,1024]{1,0:T(8,128)S(1)} collective-permute-done((f32[32,1024]{1,0:T(8,128)S(1)}, f32[32,1024]{1,0:T(8,128)S(1)}, u32[]{:S(2)}, u32[]{:S(2)}) %collective-permute-start.4) | collective-permute-done | bytes 131104 | tf_op jit(solution)/shard_map/ppermute | solution.py:326
  66.4 1.3 %collective-permute-start.8 = (bf16[32,1024]{1,0:T(8,128)(2,1)S(1)}, bf16[32,1024]{1,0:T(8,128)(2,1)S(1)}, u32[]{:S(2)}, u32[]{:S(2)}) collective-permute-start(bf16[32,1024]{1,0:T(8,128)(2,1)S(1)} %get-tuple-element.6), channel_id=1, source_target_pairs={{8,0},{12,4},{16,8},{20,12},{24,16},{28,20},{9,1},{13,5},{17,9},{2... | collective-permute-start | bytes 196616 | tf_op jit(solution)/shard_map/ppermute | solution.py:363
  67.7 1.3 %collective-permute-start.7 = (bf16[32,1024]{1,0:T(8,128)(2,1)S(1)}, bf16[32,1024]{1,0:T(8,128)(2,1)S(1)}, u32[]{:S(2)}, u32[]{:S(2)}) collective-permute-start(bf16[32,1024]{1,0:T(8,128)(2,1)S(1)} %get-tuple-element.6), channel_id=1, source_target_pairs={{4,0},{8,4},{12,8},{16,12},{20,16},{24,20},{28,24},{5,1},{9,5},{13... | collective-permute-start | bytes 196616 | tf_op jit(solution)/shard_map/ppermute | solution.py:363
  69.0 3.0 %collective-permute-start.6 = (bf16[32,1024]{1,0:T(8,128)(2,1)S(1)}, bf16[32,1024]{1,0:T(8,128)(2,1)S(1)}, u32[]{:S(2)}, u32[]{:S(2)}) collective-permute-start(bf16[32,1024]{1,0:T(8,128)(2,1)S(1)} %get-tuple-element.6), channel_id=1, source_target_pairs={{0,4},{4,8},{8,12},{12,16},{16,20},{20,24},{24,28},{1,5},{5,9},{9,... | collective-permute-start | bytes 196616 | tf_op jit(solution)/shard_map/ppermute | solution.py:363
  72.0 4.7 %collective-permute-start.5 = (bf16[32,1024]{1,0:T(8,128)(2,1)S(1)}, bf16[32,1024]{1,0:T(8,128)(2,1)S(1)}, u32[]{:S(2)}, u32[]{:S(2)}) collective-permute-start(bf16[32,1024]{1,0:T(8,128)(2,1)S(1)} %get-tuple-element.6), channel_id=1, source_target_pairs={{0,8},{4,12},{8,16},{12,20},{16,24},{20,28},{1,9},{5,13},{9,17},{1... | collective-permute-start | bytes 196616 | tf_op jit(solution)/shard_map/ppermute | solution.py:363
  76.8 0.0 collective-permute-done.8.p2
  76.8 0.0 collective-permute-done.7.p1
  76.8 1.7 %collective-permute-done.5.m2 = bf16[32,1024]{1,0:T(8,128)(2,1)S(1)} collective-permute-done((bf16[32,1024]{1,0:T(8,128)(2,1)S(1)}, bf16[32,1024]{1,0:T(8,128)(2,1)S(1)}, u32[]{:S(2)}, u32[]{:S(2)}) %collective-permute-start.5) | collective-permute-done | bytes 65568 | tf_op jit(solution)/shard_map/ppermute | solution.py:363
  78.5 7.3 %deblur.1 = (f32[32,8,128]{2,1,0:T(8,128)}, f32[32,8,128]{2,1,0:T(8,128)}) custom-call(s32[1]{0:T(128)} %bitcast.at_ref, f32[3,17]{1,0:T(4,128)S(1)} %copy-done, f32[32,1024]{1,0:T(8,128)S(1)} %get-tuple-element.7.own_ref, bf16[32,1024]{1,0:T(8,128)(2,1)S(1)} %collective-permute-done.5.m2, bf16[32,1024]{1,0:T(8,128)(2,1)S(1)} %collective-permute-done.6.m1, ...), custom_call_target="tpu_custom_call" | custom-call | tf_op jit(solution)/shard_map/deblur/pallas_call | solution.py:365
  (9 shorter events, 0.2 us)
Async XLA Ops:
  3.4 16.7 %collective-permute-start.1 = (bf16[16,3584]{1,0:T(8,128)(2,1)S(1)}, bf16[16,3584]{1,0:T(8,128)(2,1)S(1)}, u32[]{:S(2)}, u32[]{:S(2)}) collective-permute-start(bf16[16,3584]{1,0:T(8,128)(2,1)S(1)} %get-tuple-element.13), channel_id=1, source_target_pairs={{0,2},{1,3},{2,0},{3,1},{4,6},{5,7},{6,4},{7,5},{8,10},{9,11},{10,... | collective-permute-start | bytes 344072 | tf_op jit(solution)/shard_map/ppermute | solution.py:349
  7.5 12.6 %collective-permute-start.2 = (bf16[16,3584]{1,0:T(8,128)(2,1)S(1)}, bf16[16,3584]{1,0:T(8,128)(2,1)S(1)}, u32[]{:S(2)}, u32[]{:S(2)}) collective-permute-start(bf16[16,3584]{1,0:T(8,128)(2,1)S(1)} %get-tuple-element.14), channel_id=1, source_target_pairs={{0,3},{1,0},{2,1},{3,2},{4,7},{5,4},{6,5},{7,6},{8,11},{9,8},{10,9... | collective-permute-start | bytes 344072 | tf_op jit(solution)/shard_map/ppermute | solution.py:349
  8.8 11.3 %collective-permute-start = (bf16[16,3584]{1,0:T(8,128)(2,1)S(1)}, bf16[16,3584]{1,0:T(8,128)(2,1)S(1)}, u32[]{:S(2)}, u32[]{:S(2)}) collective-permute-start(bf16[16,3584]{1,0:T(8,128)(2,1)S(1)} %get-tuple-element.15), channel_id=1, source_target_pairs={{0,1},{1,2},{2,3},{3,0},{4,5},{5,6},{6,7},{7,4},{8,9},{9,10},{10,1... | collective-permute-start | bytes 344072 | tf_op jit(solution)/shard_map/ppermute | solution.py:349
  20.1 58.4 %copy-start = (f32[3,17]{1,0:T(4,128)S(1)}, f32[3,17]{1,0:T(4,128)}, u32[]{:S(2)}) copy-start(f32[3,17]{1,0:T(4,128)} %taps_ref.1) | copy-start | bytes 616
  54.0 5.0 %collective-permute-start.3 = (f32[32,1024]{1,0:T(8,128)S(1)}, f32[32,1024]{1,0:T(8,128)S(1)}, u32[]{:S(2)}, u32[]{:S(2)}) collective-permute-start(f32[32,1024]{1,0:T(8,128)S(1)} %beams_rest.1), channel_id=1, source_target_pairs={{0,1},{1,0},{2,3},{3,2},{4,5},{5,4},{6,7},{7,6},{8,9},{9,8},{10,11... | collective-permute-start | bytes 393224 | tf_op jit(solution)/shard_map/ppermute | solution.py:326
  59.0 7.3 %collective-permute-start.4 = (f32[32,1024]{1,0:T(8,128)S(1)}, f32[32,1024]{1,0:T(8,128)S(1)}, u32[]{:S(2)}, u32[]{:S(2)}) collective-permute-start(f32[32,1024]{1,0:T(8,128)S(1)} %add.49), channel_id=1, source_target_pairs={{0,2},{1,3},{2,0},{3,1},{4,6},{5,7},{6,4},{7,5},{8,10},{9,11},{10,... | collective-permute-start | bytes 393224 | tf_op jit(solution)/shard_map/ppermute | solution.py:326
  66.4 10.4 %collective-permute-start.8 = (bf16[32,1024]{1,0:T(8,128)(2,1)S(1)}, bf16[32,1024]{1,0:T(8,128)(2,1)S(1)}, u32[]{:S(2)}, u32[]{:S(2)}) collective-permute-start(bf16[32,1024]{1,0:T(8,128)(2,1)S(1)} %get-tuple-element.6), channel_id=1, source_target_pairs={{8,0},{12,4},{16,8},{20,12},{24,16},{28,20},{9,1},{13,5},{17,9},{2... | collective-permute-start | bytes 196616 | tf_op jit(solution)/shard_map/ppermute | solution.py:363
  67.7 9.1 %collective-permute-start.7 = (bf16[32,1024]{1,0:T(8,128)(2,1)S(1)}, bf16[32,1024]{1,0:T(8,128)(2,1)S(1)}, u32[]{:S(2)}, u32[]{:S(2)}) collective-permute-start(bf16[32,1024]{1,0:T(8,128)(2,1)S(1)} %get-tuple-element.6), channel_id=1, source_target_pairs={{4,0},{8,4},{12,8},{16,12},{20,16},{24,20},{28,24},{5,1},{9,5},{13... | collective-permute-start | bytes 196616 | tf_op jit(solution)/shard_map/ppermute | solution.py:363
  69.0 7.8 %collective-permute-start.6 = (bf16[32,1024]{1,0:T(8,128)(2,1)S(1)}, bf16[32,1024]{1,0:T(8,128)(2,1)S(1)}, u32[]{:S(2)}, u32[]{:S(2)}) collective-permute-start(bf16[32,1024]{1,0:T(8,128)(2,1)S(1)} %get-tuple-element.6), channel_id=1, source_target_pairs={{0,4},{4,8},{8,12},{12,16},{16,20},{20,24},{24,28},{1,5},{5,9},{9,... | collective-permute-start | bytes 196616 | tf_op jit(solution)/shard_map/ppermute | solution.py:363
  72.0 6.4 %collective-permute-start.5 = (bf16[32,1024]{1,0:T(8,128)(2,1)S(1)}, bf16[32,1024]{1,0:T(8,128)(2,1)S(1)}, u32[]{:S(2)}, u32[]{:S(2)}) collective-permute-start(bf16[32,1024]{1,0:T(8,128)(2,1)S(1)} %get-tuple-element.6), channel_id=1, source_target_pairs={{0,8},{4,12},{8,16},{12,20},{16,24},{20,28},{1,9},{5,13},{9,17},{1... | collective-permute-start | bytes 196616 | tf_op jit(solution)/shard_map/ppermute | solution.py:363

commit v3 on v2

--- a/solution.py
+++ b/solution.py
@@ -20,6 +20,7 @@
 
 TWO_PI = 2.0 * math.pi
 BACKGROUND = 0.05
+SMALLER = 0.25
 
 FA, FB, DA, DB = 0, 16, 32, 64
 ENTRIES = 72
@@ -55,13 +56,14 @@
     return values
 
 
-def beam_kernel(chunks, own, width, first, first_ref, *refs):
+def beam_kernel(chunks, own, width, scale, first_ref, *refs):
     x_refs, refs = refs[:chunks], refs[chunks:]
+    first = scale is None
     if first:
-        acc, xs, com, tabs, sides = refs[0], refs[1], refs[2], refs[3:4], refs[4:8]
+        acc, xs, com, tabs = refs[0], refs[1], refs[2], refs[3:4]
     else:
-        acc_in, out_ref, xs, com, tabs, sides = refs[0], refs[1], refs[2], refs[3], refs[4:6], refs[6:10]
-        acc, works, sem = refs[10], refs[11:13], refs[13]
+        acc_in, out_ref, xs, com, tabs = refs[0], refs[1], refs[2], refs[3], refs[4:6]
+        acc, works, sem = refs[6], refs[7:9], refs[9]
         fetch = pltpu.make_async_copy(acc_in, acc, sem)
         fetch.start()
     parts = width // LANES
@@ -128,9 +130,7 @@
             put(DB + low, rc - ms)
             put(DB + 4 + low, mc + rs)
 
-    def operands(tab, side, f):
-        left, right = side
-
+    def beams(tab, f):
         def rows16(entry, i):
             return tab[i, pl.ds(entry * own + f, 16, stride=own), :].astype(jnp.bfloat16)
 
@@ -138,23 +138,23 @@
             row = tab[i, pl.ds(entry * own + f, 1), :]
             return jnp.broadcast_to(row, (16, LANES)).astype(jnp.bfloat16)
 
+        left, right = [], []
         for i in range(parts):
-            lanes = slice(i * LANES, (i + 1) * LANES)
             a = rows16(FA, i)
-            for b in range(16):
-                left[b * 16 : (b + 1) * 16, lanes] = a * spread(FB + b, i)
+            left.append(jnp.concatenate([a * spread(FB + b, i) for b in range(16)], axis=0))
             ar, ai = rows16(DA, i), rows16(DA + 16, i)
+            real, imag = [], []
             for h in range(4):
                 br, bi = spread(DB + h, i), spread(DB + 4 + h, i)
                 rr, ii, ri, ir = ar * br, ai * bi, ar * bi, ai * br
-                right[h * 32 : h * 32 + 16, lanes] = rr + ii
-                right[h * 32 + 16 : h * 32 + 32, lanes] = rr - ii
-                right[CZ + h * 32 : CZ + h * 32 + 16, lanes] = ri - ir
-                right[CZ + h * 32 + 16 : CZ + h * 32 + 32, lanes] = ri + ir
-
-    def product(side):
+                real += [rr + ii, rr - ii]
+                imag += [ri - ir, ri + ir]
+            right.append(jnp.concatenate(real + imag, axis=0))
         return lax.dot_general(
-            side[0][...], side[1][...], (((1,), (1,)), ((), ())), preferred_element_type=jnp.float32
+            jnp.concatenate(left, axis=1),
+            jnp.concatenate(right, axis=1),
+            (((1,), (1,)), ((), ())),
+            preferred_element_type=jnp.float32,
         )
 
     def add_power(got, work):
@@ -166,7 +166,6 @@
         for y, (re, im) in enumerate(butterfly(values, 3)):
             out_ref[:, y * CZ : (y + 1) * CZ] += re * re + im * im
 
-    pairs = (sides[:2], sides[2:])
     batch = 4
     each = parts * batch // own
 
@@ -184,13 +183,11 @@
     for g in range(chunks):
         last = g == chunks - 1
         tab = tabs[g % len(tabs)]
-        operands(tab, pairs[0], 0)
 
         def block(q, g=g, last=last, tab=tab):
             for j in range(batch):
                 f = q * batch + j
-                got = product(pairs[j % 2])
-                operands(tab, pairs[(j + 1) % 2], jnp.minimum(f + 1, own - 1))
+                got = beams(tab, f)
                 if first:
                     acc[f] = got
                 elif last:
@@ -209,7 +206,7 @@
     dst = lax.broadcasted_iota(jnp.int32, (CZ, CZ), 1)
     low = src % 16
     place = (src // 32) * 32 + jnp.where((src // 16) % 2 == 0, 16 + low, 15 - low)
-    swap = (place == dst).astype(jnp.float32)
+    swap = jnp.where(place == dst, scale, 0.0)
     for y in range(CY):
         lanes = slice(y * CZ, (y + 1) * CZ)
         out_ref[:, lanes] = jnp.dot(
@@ -217,28 +214,28 @@
         )
 
 
-def beams_call(chunks, own, width, pieces, first, *args):
+def beams_call(chunks, own, width, pieces, scale, *args):
+    first = scale is None
     vmem = pl.BlockSpec(memory_space=pltpu.VMEM)
     smem = pl.BlockSpec(memory_space=pltpu.SMEM)
     rows = CX * CY
     acc = (own, rows, 2 * CZ)
-    side = [pltpu.VMEM((rows, width), jnp.bfloat16), pltpu.VMEM((2 * CZ, width), jnp.bfloat16)]
     tab = pltpu.VMEM((width // LANES, ENTRIES * own, LANES), jnp.float32)
     scratch = [
         pltpu.VMEM((chunks, own, 2 * width), jnp.bfloat16),
         pltpu.VMEM((chunks, pieces, own, LANES), jnp.float32),
     ]
     if first:
-        scratch += [tab] + side * 2
+        scratch += [tab]
         out = jax.ShapeDtypeStruct(acc, jnp.float32)
         specs = [smem] + [vmem] * chunks
     else:
-        scratch += [tab] * 2 + side * 2 + [pltpu.VMEM(acc, jnp.float32)]
+        scratch += [tab] * 2 + [pltpu.VMEM(acc, jnp.float32)]
         scratch += [pltpu.VMEM((2, rows, CZ), jnp.float32)] * 2 + [pltpu.SemaphoreType.DMA]
         out = jax.ShapeDtypeStruct((CX, CY * CZ), jnp.float32)
         specs = [smem] + [vmem] * chunks + [pl.BlockSpec(memory_space=pl.ANY)]
     return pl.pallas_call(
-        functools.partial(beam_kernel, chunks, own, width, first),
+        functools.partial(beam_kernel, chunks, own, width, scale),
         out_shape=out,
         in_specs=specs,
         out_specs=vmem,
@@ -261,7 +258,7 @@
     return dot(a[0], b[0]) + (dot(a[0], b[1]) + dot(a[1], b[0]))
 
 
-def deblur_kernel(count, scale, at_ref, taps_ref, own_ref, m2, m1, p1, p2, stacked_ref, est_ref):
+def deblur_kernel(count, at_ref, taps_ref, own_ref, m2, m1, p1, p2, stacked_ref, est_ref):
     rows, cols = 5 * CX, CY * CZ
     start = (at_ref[0] - 2) * CX
 
@@ -269,8 +266,8 @@
         x = lax.broadcasted_iota(jnp.int32, (length, cols), 0) + (start + first)
         return (x >= 0) & (x < count * CX)
 
-    stacked = own_ref[...] * scale + BACKGROUND
-    halo = [ref[...].astype(jnp.float32) * scale + BACKGROUND for ref in (m2, m1, p1, p2)]
+    stacked = own_ref[...] * (1.0 / SMALLER) + BACKGROUND
+    halo = [ref[...].astype(jnp.float32) * (1.0 / SMALLER) + BACKGROUND for ref in (m2, m1, p1, p2)]
     observed = jnp.concatenate(halo[:2] + [stacked] + halo[2:], axis=0)
     observed = jnp.where(inside(0, rows), observed, 0.0)
     for y in range(CY):
@@ -323,7 +320,9 @@
         return lax.psum(value, axis)
     step = 1
     while step < size:
-        value = value + lax.ppermute(value, axis, [(i, i ^ step) for i in range(size)])
+        half = value.astype(jnp.float16)
+        other = lax.ppermute(half, axis, [(i, i ^ step) for i in range(size)])
+        value = half.astype(jnp.float32) + other.astype(jnp.float32)
         step *= 2
     return value
 
@@ -352,8 +351,9 @@
     smem = pl.BlockSpec(memory_space=pltpu.SMEM)
     pieces = common.shape[1] // LANES
     at = (me * own).astype(jnp.int32).reshape(1)
-    held = beams_call(1, own, width, pieces, True, at, blocks[0])
-    local = beams_call(groups - 1, own, width, pieces, False, at, *blocks[1:], held)
+    scale = SMALLER / (freqs * width * groups)
+    held = beams_call(1, own, width, pieces, None, at, blocks[0])
+    local = beams_call(groups - 1, own, width, pieces, scale, at, *blocks[1:], held)
 
     total = summed_over(local, "sta", groups)
     narrow = total.astype(jnp.bfloat16)
@@ -363,7 +363,7 @@
         halo.append(lax.ppermute(narrow, "grid", moves))
     tile = jax.ShapeDtypeStruct((CX, CY, CZ), jnp.float32)
     stacked, deblurred = pl.pallas_call(
-        functools.partial(deblur_kernel, tiles, 1.0 / (freqs * width * groups)),
+        functools.partial(deblur_kernel, tiles),
         out_shape=(tile, tile),
         in_specs=[smem, smem] + [vmem] * 5,
         out_specs=(vmem, vmem),

time: 87.4 us -> 69.5 us (0.80)
  the two profiles are of different devices: /device:TPU:0 before, /device:TPU:4 now
where the time goes in v3:
time: 69.5 us; the launch traced here: 69.2 us
  Pallas kernels  34 us (49%)
  starting transfers between devices  21.1 us (30%)
  waiting for transfers between devices  10.6 us (15%)
  other arithmetic  1.53 us (2%)
  local copies, waits for them, and re-layouts  1.15 us (2%)
  between operations  0.83 us (1%)
    pallas_call x2, Pallas kernels, beams_call(): pl.pallas_call(functools.partial(beam_kernel, chunks, own, width, scale),...  26.6 us
    ppermute x4, starting transfers between devices, per_device(): halo.append(lax.ppermute(narrow, 'grid', moves))  10.3 us
    pallas_call x1, Pallas kernels, per_device(): pl.pallas_call(functools.partial(deblur_kernel, tiles), out_shape=(tile,...  7.33 us
    ppermute x2, starting transfers between devices, summed_over(): other = lax.ppermute(half, axis, [(i, i ^ step) for i in range(size)])  6.07 us
    ppermute x2, waiting for transfers between devices, summed_over(): other = lax.ppermute(half, axis, [(i, i ^ step) for i in range(size)])  5.23 us
    ppermute x3, starting transfers between devices, per_device(): blocks.append(lax.ppermute(bundle((me + k) % groups), 'sta', send))  4.68 us
    ppermute x4, waiting for transfers between devices, per_device(): halo.append(lax.ppermute(narrow, 'grid', moves))  4.35 us
  transfers between devices with their start and end apart: 9, of which 5 were waited for; matrix products, arithmetic and copies ran while one was open for 0% of the time, Pallas kernels for 9%

profile of v3, /device:TPU:4, one launch (start us, length us, event | category | flops | bytes accessed | tf_op | source)
XLA Modules:
  0.0 69.2 jit_solution(1960271979185223559)
XLA Ops:
  0.7 0.7 %shift-right-arithmetic_convert_fusion = (bf16[1,1536]{1,0:T(2,128)(2,1)S(1)}, bf16[1,1536]{1,0:T(2,128)(2,1)S(1)}) fusion(s32[1,1536]{1,0:T(1,128)} %param.5), kind=kLoop, calls=%fused_computation.8 | loop fusion | flops 6144 | bytes 12288 | tf_op jit(solution)/shard_map/convert
  1.4 0.7 %pad_maximum_fusion.4 = bf16[5,1536]{1,0:T(8,128)(2,1)S(1)} fusion(bf16[3,1536]{1,0:T(4,128)(2,1)} %bitcast.9, bf16[1,1536]{1,0:T(2,128)(2,1)S(1)} %get-tuple-element.17, bf16[1,1536]{1,0:T(2,128)(2,1)S(1)} %get-tuple-element.16), kind=kLoop, calls=%fused_computation.6 | loop fusion | flops 46080 | bytes 30720 | tf_op jit(solution)/shard_map/concatenate | solution.py:335
  2.2 1.0 %copy.6 = bf16[8,8,2,1536]{3,1,2,0:T(8,128)(2,1)S(1)} copy(bf16[8,8,2,1536]{3,2,1,0:T(2,128)(2,1)} %bitcast.8) | data formatting | bytes 786432
  3.4 2.7 %collective-permute-start.1 = (bf16[16,3584]{1,0:T(8,128)(2,1)S(1)}, bf16[16,3584]{1,0:T(8,128)(2,1)S(1)}, u32[]{:S(2)}, u32[]{:S(2)}) collective-permute-start(bf16[16,3584]{1,0:T(8,128)(2,1)S(1)} %get-tuple-element.13), channel_id=1, source_target_pairs={{0,2},{1,3},{2,0},{3,1},{4,6},{5,7},{6,4},{7,5},{8,10},{9,11},{10,... | collective-permute-start | bytes 344072 | tf_op jit(solution)/shard_map/ppermute | solution.py:348
  6.0 1.3 %collective-permute-start.2 = (bf16[16,3584]{1,0:T(8,128)(2,1)S(1)}, bf16[16,3584]{1,0:T(8,128)(2,1)S(1)}, u32[]{:S(2)}, u32[]{:S(2)}) collective-permute-start(bf16[16,3584]{1,0:T(8,128)(2,1)S(1)} %get-tuple-element.14), channel_id=1, source_target_pairs={{0,3},{1,0},{2,1},{3,2},{4,7},{5,4},{6,5},{7,6},{8,11},{9,8},{10,9... | collective-permute-start | bytes 344072 | tf_op jit(solution)/shard_map/ppermute | solution.py:348
  7.4 0.7 collective-permute-start
  8.0 6.2 %beams_own.1.refs_3_ = f32[16,256,256]{2,1,0:T(8,128)S(1)} custom-call(s32[1]{0:T(128)} %bitcast.1.first_ref, bf16[16,3584]{1,0:T(8,128)(2,1)S(1)} %get-tuple-element.12.refs_0_), custom_call_target="tpu_custom_call" | custom-call | flops 3221225472 | bytes 4194304 | tf_op jit(solution)/shard_map/beams_own/pallas_call | solution.py:237
  14.2 0.0 copy-start
  14.2 1.0 %collective-permute-done.1.refs_1_ = bf16[16,3584]{1,0:T(8,128)(2,1)S(1)} collective-permute-done((bf16[16,3584]{1,0:T(8,128)(2,1)S(1)}, bf16[16,3584]{1,0:T(8,128)(2,1)S(1)}, u32[]{:S(2)}, u32[]{:S(2)}) %collective-permute-start.1) | collective-permute-done | bytes 114720 | tf_op jit(solution)/shard_map/ppermute | solution.py:348
  15.2 0.0 collective-permute-done.2.refs_2_
  15.2 0.0 collective-permute-done.refs_0_
  15.3 20.5 %beams_rest.1 = f32[32,1024]{1,0:T(8,128)S(1)} custom-call(s32[1]{0:T(128)} %bitcast.1.first_ref, bf16[16,3584]{1,0:T(8,128)(2,1)S(1)} %collective-permute-done.refs_0_, bf16[16,3584]{1,0:T(8,128)(2,1)S(1)} %collective-permute-done.1.refs_1_, bf16[16,3584]{1,0:T(8,128)(2,1)S(1)} %collective-permute-done.2.refs_2_, f32[16,256,256]{2,1,0:T(8,128)S(1)} %beams_own.1.refs_3_), custom_call_target="tpu_custom_call" | custom-call | flops 9663676416 | bytes 4194304 | tf_op jit(solution)/shard_map/beams_rest/pallas_call | solution.py:237
  35.7 2.1 %collective-permute-start.3 = (f16[32,1024]{1,0:T(8,128)(2,1)S(1)}, f16[32,1024]{1,0:T(8,128)(2,1)S(1)}, u32[]{:S(2)}, u32[]{:S(2)}) collective-permute-start(f16[32,1024]{1,0:T(8,128)(2,1)S(1)} %convert_element_type.24), channel_id=1, source_target_pairs={{0,1},{1,0},{2,3},{3,2},{4,5},{5,4},{6,7},{7,6},{8,9},{9,8},{10,11... | collective-permute-start | bytes 196616 | tf_op jit(solution)/shard_map/ppermute | solution.py:324
  37.8 2.3 %collective-permute-done.3 = f16[32,1024]{1,0:T(8,128)(2,1)S(1)} collective-permute-done((f16[32,1024]{1,0:T(8,128)(2,1)S(1)}, f16[32,1024]{1,0:T(8,128)(2,1)S(1)}, u32[]{:S(2)}, u32[]{:S(2)}) %collective-permute-start.3) | collective-permute-done | bytes 65568 | tf_op jit(solution)/shard_map/ppermute | solution.py:324
  40.2 4.0 %collective-permute-start.4 = (f16[32,1024]{1,0:T(8,128)(2,1)S(1)}, f16[32,1024]{1,0:T(8,128)(2,1)S(1)}, u32[]{:S(2)}, u32[]{:S(2)}) collective-permute-start(f16[32,1024]{1,0:T(8,128)(2,1)S(1)} %add_convert_fusion), channel_id=1, source_target_pairs={{0,2},{1,3},{2,0},{3,1},{4,6},{5,7},{6,4},{7,5},{8,10},{9,11},{10,... | collective-permute-start | bytes 196616 | tf_op jit(solution)/shard_map/ppermute | solution.py:324
  44.1 2.9 %collective-permute-done.4 = f16[32,1024]{1,0:T(8,128)(2,1)S(1)} collective-permute-done((f16[32,1024]{1,0:T(8,128)(2,1)S(1)}, f16[32,1024]{1,0:T(8,128)(2,1)S(1)}, u32[]{:S(2)}, u32[]{:S(2)}) %collective-permute-start.4) | collective-permute-done | bytes 65568 | tf_op jit(solution)/shard_map/ppermute | solution.py:324
  47.1 3.3 %collective-permute-start.8 = (bf16[32,1024]{1,0:T(8,128)(2,1)S(1)}, bf16[32,1024]{1,0:T(8,128)(2,1)S(1)}, u32[]{:S(2)}, u32[]{:S(2)}) collective-permute-start(bf16[32,1024]{1,0:T(8,128)(2,1)S(1)} %get-tuple-element.10), channel_id=1, source_target_pairs={{8,0},{12,4},{16,8},{20,12},{24,16},{28,20},{9,1},{13,5},{17,9},{2... | collective-permute-start | bytes 196616 | tf_op jit(solution)/shard_map/ppermute | solution.py:363
  50.4 1.9 %collective-permute-start.7 = (bf16[32,1024]{1,0:T(8,128)(2,1)S(1)}, bf16[32,1024]{1,0:T(8,128)(2,1)S(1)}, u32[]{:S(2)}, u32[]{:S(2)}) collective-permute-start(bf16[32,1024]{1,0:T(8,128)(2,1)S(1)} %get-tuple-element.10), channel_id=1, source_target_pairs={{4,0},{8,4},{12,8},{16,12},{20,16},{24,20},{28,24},{5,1},{9,5},{13... | collective-permute-start | bytes 196616 | tf_op jit(solution)/shard_map/ppermute | solution.py:363
  52.4 2.4 %collective-permute-start.6 = (bf16[32,1024]{1,0:T(8,128)(2,1)S(1)}, bf16[32,1024]{1,0:T(8,128)(2,1)S(1)}, u32[]{:S(2)}, u32[]{:S(2)}) collective-permute-start(bf16[32,1024]{1,0:T(8,128)(2,1)S(1)} %get-tuple-element.10), channel_id=1, source_target_pairs={{0,4},{4,8},{8,12},{12,16},{16,20},{20,24},{24,28},{1,5},{5,9},{9,... | collective-permute-start | bytes 196616 | tf_op jit(solution)/shard_map/ppermute | solution.py:363
  54.8 2.7 %collective-permute-start.5 = (bf16[32,1024]{1,0:T(8,128)(2,1)S(1)}, bf16[32,1024]{1,0:T(8,128)(2,1)S(1)}, u32[]{:S(2)}, u32[]{:S(2)}) collective-permute-start(bf16[32,1024]{1,0:T(8,128)(2,1)S(1)} %get-tuple-element.10), channel_id=1, source_target_pairs={{0,8},{4,12},{8,16},{12,20},{16,24},{20,28},{1,9},{5,13},{9,17},{1... | collective-permute-start | bytes 196616 | tf_op jit(solution)/shard_map/ppermute | solution.py:363
  57.5 0.0 collective-permute-done.8.p2
  57.5 1.4 %collective-permute-done.6.m1 = bf16[32,1024]{1,0:T(8,128)(2,1)S(1)} collective-permute-done((bf16[32,1024]{1,0:T(8,128)(2,1)S(1)}, bf16[32,1024]{1,0:T(8,128)(2,1)S(1)}, u32[]{:S(2)}, u32[]{:S(2)}) %collective-permute-start.6) | collective-permute-done | bytes 65568 | tf_op jit(solution)/shard_map/ppermute | solution.py:363
  58.9 3.0 %collective-permute-done.5.m2 = bf16[32,1024]{1,0:T(8,128)(2,1)S(1)} collective-permute-done((bf16[32,1024]{1,0:T(8,128)(2,1)S(1)}, bf16[32,1024]{1,0:T(8,128)(2,1)S(1)}, u32[]{:S(2)}, u32[]{:S(2)}) %collective-permute-start.5) | collective-permute-done | bytes 65568 | tf_op jit(solution)/shard_map/ppermute | solution.py:363
  61.8 7.3 %deblur.1 = (f32[32,8,128]{2,1,0:T(8,128)}, f32[32,8,128]{2,1,0:T(8,128)}) custom-call(s32[1]{0:T(128)} %bitcast.at_ref, f32[3,17]{1,0:T(4,128)S(1)} %copy-done, f32[32,1024]{1,0:T(8,128)S(1)} %get-tuple-element.11.own_ref, bf16[32,1024]{1,0:T(8,128)(2,1)S(1)} %collective-permute-done.5.m2, bf16[32,1024]{1,0:T(8,128)(2,1)S(1)} %collective-permute-done.6.m1, ...), custom_call_target="tpu_custom_call" | custom-call | tf_op jit(solution)/shard_map/deblur/pallas_call | solution.py:365
  (10 shorter events, 0.2 us)
Async XLA Ops:
  3.4 11.9 %collective-permute-start.1 = (bf16[16,3584]{1,0:T(8,128)(2,1)S(1)}, bf16[16,3584]{1,0:T(8,128)(2,1)S(1)}, u32[]{:S(2)}, u32[]{:S(2)}) collective-permute-start(bf16[16,3584]{1,0:T(8,128)(2,1)S(1)} %get-tuple-element.13), channel_id=1, source_target_pairs={{0,2},{1,3},{2,0},{3,1},{4,6},{5,7},{6,4},{7,5},{8,10},{9,11},{10,... | collective-permute-start | bytes 344072 | tf_op jit(solution)/shard_map/ppermute | solution.py:348
  6.0 9.2 %collective-permute-start.2 = (bf16[16,3584]{1,0:T(8,128)(2,1)S(1)}, bf16[16,3584]{1,0:T(8,128)(2,1)S(1)}, u32[]{:S(2)}, u32[]{:S(2)}) collective-permute-start(bf16[16,3584]{1,0:T(8,128)(2,1)S(1)} %get-tuple-element.14), channel_id=1, source_target_pairs={{0,3},{1,0},{2,1},{3,2},{4,7},{5,4},{6,5},{7,6},{8,11},{9,8},{10,9... | collective-permute-start | bytes 344072 | tf_op jit(solution)/shard_map/ppermute | solution.py:348
  7.4 7.9 %collective-permute-start = (bf16[16,3584]{1,0:T(8,128)(2,1)S(1)}, bf16[16,3584]{1,0:T(8,128)(2,1)S(1)}, u32[]{:S(2)}, u32[]{:S(2)}) collective-permute-start(bf16[16,3584]{1,0:T(8,128)(2,1)S(1)} %get-tuple-element.15), channel_id=1, source_target_pairs={{0,1},{1,2},{2,3},{3,0},{4,5},{5,6},{6,7},{7,4},{8,9},{9,10},{10,1... | collective-permute-start | bytes 344072 | tf_op jit(solution)/shard_map/ppermute | solution.py:348
  14.2 47.6 %copy-start = (f32[3,17]{1,0:T(4,128)S(1)}, f32[3,17]{1,0:T(4,128)}, u32[]{:S(2)}) copy-start(f32[3,17]{1,0:T(4,128)} %taps_ref.1) | copy-start | bytes 616
  35.7 4.4 %collective-permute-start.3 = (f16[32,1024]{1,0:T(8,128)(2,1)S(1)}, f16[32,1024]{1,0:T(8,128)(2,1)S(1)}, u32[]{:S(2)}, u32[]{:S(2)}) collective-permute-start(f16[32,1024]{1,0:T(8,128)(2,1)S(1)} %convert_element_type.24), channel_id=1, source_target_pairs={{0,1},{1,0},{2,3},{3,2},{4,5},{5,4},{6,7},{7,6},{8,9},{9,8},{10,11... | collective-permute-start | bytes 196616 | tf_op jit(solution)/shard_map/ppermute | solution.py:324
  40.2 6.9 %collective-permute-start.4 = (f16[32,1024]{1,0:T(8,128)(2,1)S(1)}, f16[32,1024]{1,0:T(8,128)(2,1)S(1)}, u32[]{:S(2)}, u32[]{:S(2)}) collective-permute-start(f16[32,1024]{1,0:T(8,128)(2,1)S(1)} %add_convert_fusion), channel_id=1, source_target_pairs={{0,2},{1,3},{2,0},{3,1},{4,6},{5,7},{6,4},{7,5},{8,10},{9,11},{10,... | collective-permute-start | bytes 196616 | tf_op jit(solution)/shard_map/ppermute | solution.py:324
  47.1 10.4 %collective-permute-start.8 = (bf16[32,1024]{1,0:T(8,128)(2,1)S(1)}, bf16[32,1024]{1,0:T(8,128)(2,1)S(1)}, u32[]{:S(2)}, u32[]{:S(2)}) collective-permute-start(bf16[32,1024]{1,0:T(8,128)(2,1)S(1)} %get-tuple-element.10), channel_id=1, source_target_pairs={{8,0},{12,4},{16,8},{20,12},{24,16},{28,20},{9,1},{13,5},{17,9},{2... | collective-permute-start | bytes 196616 | tf_op jit(solution)/shard_map/ppermute | solution.py:363
  50.4 7.0 %collective-permute-start.7 = (bf16[32,1024]{1,0:T(8,128)(2,1)S(1)}, bf16[32,1024]{1,0:T(8,128)(2,1)S(1)}, u32[]{:S(2)}, u32[]{:S(2)}) collective-permute-start(bf16[32,1024]{1,0:T(8,128)(2,1)S(1)} %get-tuple-element.10), channel_id=1, source_target_pairs={{4,0},{8,4},{12,8},{16,12},{20,16},{24,20},{28,24},{5,1},{9,5},{13... | collective-permute-start | bytes 196616 | tf_op jit(solution)/shard_map/ppermute | solution.py:363
  52.4 6.5 %collective-permute-start.6 = (bf16[32,1024]{1,0:T(8,128)(2,1)S(1)}, bf16[32,1024]{1,0:T(8,128)(2,1)S(1)}, u32[]{:S(2)}, u32[]{:S(2)}) collective-permute-start(bf16[32,1024]{1,0:T(8,128)(2,1)S(1)} %get-tuple-element.10), channel_id=1, source_target_pairs={{0,4},{4,8},{8,12},{12,16},{16,20},{20,24},{24,28},{1,5},{5,9},{9,... | collective-permute-start | bytes 196616 | tf_op jit(solution)/shard_map/ppermute | solution.py:363
  54.8 7.1 %collective-permute-start.5 = (bf16[32,1024]{1,0:T(8,128)(2,1)S(1)}, bf16[32,1024]{1,0:T(8,128)(2,1)S(1)}, u32[]{:S(2)}, u32[]{:S(2)}) collective-permute-start(bf16[32,1024]{1,0:T(8,128)(2,1)S(1)} %get-tuple-element.10), channel_id=1, source_target_pairs={{0,8},{4,12},{8,16},{12,20},{16,24},{20,28},{1,9},{5,13},{9,17},{1... | collective-permute-start | bytes 196616 | tf_op jit(solution)/shard_map/ppermute | solution.py:363

commit v4 on v3

--- a/solution.py
+++ b/solution.py
@@ -28,8 +28,8 @@
 
 def sincos(t):
     u = t * t
-    s = t * (1.0 + u * (-1 / 6 + u * (1 / 120 + u * (-1 / 5040 + u * (1 / 362880 - u * (1 / 39916800))))))
-    c = 1.0 + u * (-1 / 2 + u * (1 / 24 + u * (-1 / 720 + u * (1 / 40320 - u * (1 / 3628800)))))
+    s = t * (1.0 + u * (-0.16666600108146667 + u * (0.008329673670232296 - u * 0.00019265798619017005)))
+    c = 1.0 + u * (-0.4999999701976776 + u * (0.0416664220392704 + u * (u * 2.4071188818197697e-05 - 0.0013882155762985349)))
     return c, s
 
 
@@ -166,7 +166,7 @@
         for y, (re, im) in enumerate(butterfly(values, 3)):
             out_ref[:, y * CZ : (y + 1) * CZ] += re * re + im * im
 
-    batch = 4
+    batch = 8
     each = parts * batch // own
 
     def some(n, fn):
@@ -185,6 +185,7 @@
         tab = tabs[g % len(tabs)]
 
         def block(q, g=g, last=last, tab=tab):
+            done = 0
             for j in range(batch):
                 f = q * batch + j
                 got = beams(tab, f)
@@ -194,9 +195,9 @@
                     add_power(acc[f] + got, works[j % 2])
                 else:
                     acc[f] = acc[f] + got
-            if not last:
-                for e in range(each):
-                    tables(tabs[(g + 1) % 2], g + 1, q * each + e)
+                while not last and done * batch < (j + 1) * each:
+                    tables(tabs[(g + 1) % 2], g + 1, q * each + done)
+                    done += 1
 
         some(own // batch, block)
 
@@ -315,42 +316,61 @@
         est_ref[:, y, :] = est[:, y * CZ : (y + 1) * CZ]
 
 
+def bundle_kernel(groups, own, me_ref, flat_ref, lag_ref, slow_ref, *refs):
+    outs, common = refs[:groups], refs[groups]
+    cols = flat_ref.shape[1]
+    parts = lag_ref.shape[1] // LANES
+    pieces = common.shape[1] // LANES
+    lag = lag_ref[...]
+    slow = slow_ref[...].astype(jnp.float32)
+    rows = [(lag >> 6).astype(jnp.float32), (lag & 63).astype(jnp.float32)] + [slow[d : d + 1] for d in range(3)]
+    common[...] = jnp.zeros_like(common)
+    for index in range(len(rows) * parts):
+        row, i = rows[index // parts], index % parts
+        at, piece = index // pieces, index % pieces
+        common[at : at + 1, piece * LANES : (piece + 1) * LANES] = row[:, i * LANES : (i + 1) * LANES]
+    shared = common[...].astype(jnp.bfloat16)
+    for k in range(groups):
+        dest = me_ref[0] ^ k if groups & (groups - 1) == 0 else lax.rem(me_ref[0] + k, groups)
+        outs[k][:, :cols] = flat_ref[pl.ds(pl.multiple_of(dest * own, own), own), :]
+        outs[k][:, cols:] = shared
+
+
+def moves(k, size):
+    return [(i, i ^ k if size & (size - 1) == 0 else (i + k) % size) for i in range(size)]
+
+
 def summed_over(value, axis, size):
     if size & (size - 1):
         return lax.psum(value, axis)
-    step = 1
-    while step < size:
-        half = value.astype(jnp.float16)
-        other = lax.ppermute(half, axis, [(i, i ^ step) for i in range(size)])
-        value = half.astype(jnp.float32) + other.astype(jnp.float32)
-        step *= 2
-    return value
+    half = lax.optimization_barrier(value.astype(jnp.float16))
+    terms = [half] + [lax.ppermute(half, axis, moves(k, size)) for k in range(1, size)]
+    terms = [term.astype(jnp.float32) for term in terms]
+    while len(terms) > 1:
+        terms = [a + b for a, b in zip(terms[::2], terms[1::2])]
+    return terms[0]
 
 
 def per_device(groups, tiles, spectra, lag_samples, slowness, spread_taps):
     freqs, _, width = spectra.shape
     own = freqs // groups
-    me = lax.axis_index("sta")
-    lag = lag_samples[0]
-    common = jnp.concatenate(
-        [jnp.stack([lag >> 6, lag & 63]).astype(jnp.bfloat16), slowness[0]], axis=0
-    ).reshape(-1)
-    room = -(-common.size // (own * LANES)) * own * LANES
-    common = jnp.pad(common, (0, room - common.size)).reshape(own, -1)
-    flat = spectra.reshape(freqs, 2 * width)
-
-    def bundle(dest):
-        return jnp.concatenate([lax.dynamic_slice_in_dim(flat, dest * own, own, 0), common], axis=1)
-
-    blocks = [bundle(me)]
-    for k in range(1, groups):
-        send = [(i, (i + k) % groups) for i in range(groups)]
-        blocks.append(lax.ppermute(bundle((me + k) % groups), "sta", send))
-
+    me = lax.axis_index("sta").astype(jnp.int32)
     vmem = pl.BlockSpec(memory_space=pltpu.VMEM)
     smem = pl.BlockSpec(memory_space=pltpu.SMEM)
-    pieces = common.shape[1] // LANES
-    at = (me * own).astype(jnp.int32).reshape(1)
+    parts = width // LANES
+    pieces = -(-5 * parts // own)
+    cols = 2 * width + pieces * LANES
+    blocks = pl.pallas_call(
+        functools.partial(bundle_kernel, groups, own),
+        out_shape=[jax.ShapeDtypeStruct((own, cols), jnp.bfloat16)] * groups,
+        in_specs=[smem] + [vmem] * 3,
+        out_specs=[vmem] * groups,
+        scratch_shapes=[pltpu.VMEM((own, pieces * LANES), jnp.float32)],
+        name="bundles",
+    )(me.reshape(1), spectra.reshape(freqs, 2 * width), lag_samples, slowness[0])
+    blocks = [blocks[0]] + [lax.ppermute(blocks[k], "sta", moves(k, groups)) for k in range(1, groups)]
+
+    at = (me * own).reshape(1)
     scale = SMALLER / (freqs * width * groups)
     held = beams_call(1, own, width, pieces, None, at, blocks[0])
     local = beams_call(groups - 1, own, width, pieces, scale, at, *blocks[1:], held)
@@ -359,8 +379,7 @@
     narrow = total.astype(jnp.bfloat16)
     halo = []
     for shift in (2, 1, -1, -2):
-        moves = [(i, i + shift) for i in range(tiles) if 0 <= i + shift < tiles]
-        halo.append(lax.ppermute(narrow, "grid", moves))
+        halo.append(lax.ppermute(narrow, "grid", [(i, (i + shift) % tiles) for i in range(tiles)]))
     tile = jax.ShapeDtypeStruct((CX, CY, CZ), jnp.float32)
     stacked, deblurred = pl.pallas_call(
         functools.partial(deblur_kernel, tiles),

time: 69.5 us -> 63.8 us (0.918)
  the two profiles are of different devices: /device:TPU:4 before, /device:TPU:0 now
where the time goes in v4:
time: 63.8 us; the launch traced here: 63.6 us
  Pallas kernels  34.8 us (55%)
  starting transfers between devices  13.3 us (21%)
  waiting for transfers between devices  12.1 us (19%)
  local copies, waits for them, and re-layouts  2.68 us (4%)
  between operations  0.69 us (1%)
    pallas_call x2, Pallas kernels, beams_call(): pl.pallas_call(functools.partial(beam_kernel, chunks, own, width, scale),...  25.7 us
    pallas_call x1, Pallas kernels, per_device(): pl.pallas_call(functools.partial(deblur_kernel, tiles), out_shape=(tile,...  7.32 us
    ppermute x3, starting transfers between devices, per_device(): lax.ppermute(blocks[k], 'sta', moves(k, groups))  5.62 us
    ppermute x4, waiting for transfers between devices, per_device(): lax.ppermute(narrow, 'grid', [(i, (i + shift) % tiles) for i in range(til...  5.48 us
    ppermute x3, starting transfers between devices, summed_over(): lax.ppermute(half, axis, moves(k, size))  4.45 us
    ppermute x3, waiting for transfers between devices, summed_over(): lax.ppermute(half, axis, moves(k, size))  3.97 us
    ppermute x4, starting transfers between devices, per_device(): lax.ppermute(narrow, 'grid', [(i, (i + shift) % tiles) for i in range(til...  3.19 us
    ppermute x3, waiting for transfers between devices, per_device(): lax.ppermute(blocks[k], 'sta', moves(k, groups))  2.69 us
  transfers between devices with their start and end apart: 10, of which 7 were waited for; matrix products, arithmetic and copies ran while one was open for 0% of the time, Pallas kernels for 9%

profile of v4, /device:TPU:0, one launch (start us, length us, event | category | flops | bytes accessed | tf_op | source)
XLA Modules:
  0.0 63.6 jit_solution(16969836850361233496)
XLA Ops:
  0.6 1.8 %copy.6 = bf16[8,8,2,1536]{3,1,2,0:T(8,128)(2,1)} copy(bf16[8,8,2,1536]{3,2,1,0:T(2,128)(2,1)} %bitcast.9) | data formatting | bytes 786432
  2.4 1.8 %bundles.1 = (bf16[16,3584]{1,0:T(8,128)(2,1)}, bf16[16,3584]{1,0:T(8,128)(2,1)}, bf16[16,3584]{1,0:T(8,128)(2,1)}, bf16[16,3584]{1,0:T(8,128)(2,1)}) custom-call(s32[1]{0:T(128)} %bitcast.2.me_ref, bf16[64,3072]{1,0:T(8,128)(2,1)} %bitcast.8, s32[1,1536]{1,0:T(1,128)} %lag_ref.1, bf16[3,1536]{1,0:T(4,128)(2,1)} %bitcast.10), custom_call_target="tpu_custom_call" | custom-call | tf_op jit(solution)/shard_map/bundles/pallas_call | solution.py:363
  4.2 3.0 %collective-permute-start = (bf16[16,3584]{1,0:T(8,128)(2,1)}, bf16[16,3584]{1,0:T(8,128)(2,1)S(1)}, u32[]{:S(2)}, u32[]{:S(2)}) collective-permute-start(bf16[16,3584]{1,0:T(8,128)(2,1)} %get-tuple-element.8), channel_id=1, source_target_pairs={{0,1},{1,0},{2,3},{3,2},{4,5},{5,4},{6,7},{7,6},{8,9},{9,8},{10,11... | collective-permute-start | bytes 344072 | tf_op jit(solution)/shard_map/ppermute | solution.py:371
  7.2 2.6 %collective-permute-start.1 = (bf16[16,3584]{1,0:T(8,128)(2,1)}, bf16[16,3584]{1,0:T(8,128)(2,1)S(1)}, u32[]{:S(2)}, u32[]{:S(2)}) collective-permute-start(bf16[16,3584]{1,0:T(8,128)(2,1)} %get-tuple-element.9), channel_id=1, source_target_pairs={{0,2},{1,3},{2,0},{3,1},{4,6},{5,7},{6,4},{7,5},{8,10},{9,11},{10,... | collective-permute-start | bytes 344072 | tf_op jit(solution)/shard_map/ppermute | solution.py:371
  9.8 0.0 collective-permute-start.2
  9.8 0.9 %copy-done.1 = bf16[16,3584]{1,0:T(8,128)(2,1)S(1)} copy-done((bf16[16,3584]{1,0:T(8,128)(2,1)S(1)}, bf16[16,3584]{1,0:T(8,128)(2,1)}, u32[]{:S(2)}) %copy-start.1) | copy-done | bytes 114712
  10.7 5.7 %beams_own.1.refs_3_ = f32[16,256,256]{2,1,0:T(8,128)S(1)} custom-call(s32[1]{0:T(128)} %bitcast.1.first_ref, bf16[16,3584]{1,0:T(8,128)(2,1)S(1)} %copy-done.1), custom_call_target="tpu_custom_call" | custom-call | flops 3221225472 | bytes 4194304 | tf_op jit(solution)/shard_map/beams_own/pallas_call | solution.py:238
  16.4 0.0 copy-start
  16.4 2.7 %collective-permute-done.1.refs_1_ = bf16[16,3584]{1,0:T(8,128)(2,1)S(1)} collective-permute-done((bf16[16,3584]{1,0:T(8,128)(2,1)}, bf16[16,3584]{1,0:T(8,128)(2,1)S(1)}, u32[]{:S(2)}, u32[]{:S(2)}) %collective-permute-start.1) | collective-permute-done | bytes 114720 | tf_op jit(solution)/shard_map/ppermute | solution.py:371
  19.1 20.0 %beams_rest.1 = f32[32,1024]{1,0:T(8,128)S(1)} custom-call(s32[1]{0:T(128)} %bitcast.1.first_ref, bf16[16,3584]{1,0:T(8,128)(2,1)S(1)} %collective-permute-done.refs_0_, bf16[16,3584]{1,0:T(8,128)(2,1)S(1)} %collective-permute-done.1.refs_1_, bf16[16,3584]{1,0:T(8,128)(2,1)S(1)} %collective-permute-done.2.refs_2_, f32[16,256,256]{2,1,0:T(8,128)S(1)} %beams_own.1.refs_3_), custom_call_target="tpu_custom_call" | custom-call | flops 9663676416 | bytes 4194304 | tf_op jit(solution)/shard_map/beams_rest/pallas_call | solution.py:238
  39.2 2.5 %collective-permute-start.5 = (f16[32,1024]{1,0:T(8,128)(2,1)S(1)}, f16[32,1024]{1,0:T(8,128)(2,1)S(1)}, u32[]{:S(2)}, u32[]{:S(2)}) collective-permute-start(f16[32,1024]{1,0:T(8,128)(2,1)S(1)} %convert_element_type.18), channel_id=1, source_target_pairs={{0,3},{1,2},{2,1},{3,0},{4,7},{5,6},{6,5},{7,4},{8,11},{9,10},{10,... | collective-permute-start | bytes 196616 | tf_op jit(solution)/shard_map/ppermute | solution.py:347
  41.7 0.8 %collective-permute-start.4 = (f16[32,1024]{1,0:T(8,128)(2,1)S(1)}, f16[32,1024]{1,0:T(8,128)(2,1)S(1)}, u32[]{:S(2)}, u32[]{:S(2)}) collective-permute-start(f16[32,1024]{1,0:T(8,128)(2,1)S(1)} %convert_element_type.18), channel_id=1, source_target_pairs={{0,2},{1,3},{2,0},{3,1},{4,6},{5,7},{6,4},{7,5},{8,10},{9,11},{10,... | collective-permute-start | bytes 196616 | tf_op jit(solution)/shard_map/ppermute | solution.py:347
  42.5 1.1 %collective-permute-start.3 = (f16[32,1024]{1,0:T(8,128)(2,1)S(1)}, f16[32,1024]{1,0:T(8,128)(2,1)S(1)}, u32[]{:S(2)}, u32[]{:S(2)}) collective-permute-start(f16[32,1024]{1,0:T(8,128)(2,1)S(1)} %convert_element_type.18), channel_id=1, source_target_pairs={{0,1},{1,0},{2,3},{3,2},{4,5},{5,4},{6,7},{7,6},{8,9},{9,8},{10,11... | collective-permute-start | bytes 196616 | tf_op jit(solution)/shard_map/ppermute | solution.py:347
  43.6 2.3 %collective-permute-done.5 = f16[32,1024]{1,0:T(8,128)(2,1)S(1)} collective-permute-done((f16[32,1024]{1,0:T(8,128)(2,1)S(1)}, f16[32,1024]{1,0:T(8,128)(2,1)S(1)}, u32[]{:S(2)}, u32[]{:S(2)}) %collective-permute-start.5) | collective-permute-done | bytes 65568 | tf_op jit(solution)/shard_map/ppermute | solution.py:347
  45.9 1.7 %collective-permute-done.4 = f16[32,1024]{1,0:T(8,128)(2,1)S(1)} collective-permute-done((f16[32,1024]{1,0:T(8,128)(2,1)S(1)}, f16[32,1024]{1,0:T(8,128)(2,1)S(1)}, u32[]{:S(2)}, u32[]{:S(2)}) %collective-permute-start.4) | collective-permute-done | bytes 65568 | tf_op jit(solution)/shard_map/ppermute | solution.py:347
  47.6 2.7 %collective-permute-start.9 = (bf16[32,1024]{1,0:T(8,128)(2,1)S(1)}, bf16[32,1024]{1,0:T(8,128)(2,1)S(1)}, u32[]{:S(2)}, u32[]{:S(2)}) collective-permute-start(bf16[32,1024]{1,0:T(8,128)(2,1)S(1)} %get-tuple-element.14), channel_id=1, source_target_pairs={{0,24},{4,28},{8,0},{12,4},{16,8},{20,12},{24,16},{28,20},{1,25},{... | collective-permute-start | bytes 196616 | tf_op jit(solution)/shard_map/ppermute | solution.py:382
  50.3 0.0 collective-permute-start.8
  50.3 0.5 collective-permute-start.7
  50.8 0.0 collective-permute-start.6
  50.8 1.9 %collective-permute-done.9.p2 = bf16[32,1024]{1,0:T(8,128)(2,1)S(1)} collective-permute-done((bf16[32,1024]{1,0:T(8,128)(2,1)S(1)}, bf16[32,1024]{1,0:T(8,128)(2,1)S(1)}, u32[]{:S(2)}, u32[]{:S(2)}) %collective-permute-start.9) | collective-permute-done | bytes 65568 | tf_op jit(solution)/shard_map/ppermute | solution.py:382
  52.7 1.3 %collective-permute-done.8.p1 = bf16[32,1024]{1,0:T(8,128)(2,1)S(1)} collective-permute-done((bf16[32,1024]{1,0:T(8,128)(2,1)S(1)}, bf16[32,1024]{1,0:T(8,128)(2,1)S(1)}, u32[]{:S(2)}, u32[]{:S(2)}) %collective-permute-start.8) | collective-permute-done | bytes 65568 | tf_op jit(solution)/shard_map/ppermute | solution.py:382
  54.0 0.9 %collective-permute-done.7.m1 = bf16[32,1024]{1,0:T(8,128)(2,1)S(1)} collective-permute-done((bf16[32,1024]{1,0:T(8,128)(2,1)S(1)}, bf16[32,1024]{1,0:T(8,128)(2,1)S(1)}, u32[]{:S(2)}, u32[]{:S(2)}) %collective-permute-start.7) | collective-permute-done | bytes 65568 | tf_op jit(solution)/shard_map/ppermute | solution.py:382
  54.9 1.4 %collective-permute-done.6.m2 = bf16[32,1024]{1,0:T(8,128)(2,1)S(1)} collective-permute-done((bf16[32,1024]{1,0:T(8,128)(2,1)S(1)}, bf16[32,1024]{1,0:T(8,128)(2,1)S(1)}, u32[]{:S(2)}, u32[]{:S(2)}) %collective-permute-start.6) | collective-permute-done | bytes 65568 | tf_op jit(solution)/shard_map/ppermute | solution.py:382
  56.3 7.3 %deblur.1 = (f32[32,8,128]{2,1,0:T(8,128)}, f32[32,8,128]{2,1,0:T(8,128)}) custom-call(s32[1]{0:T(128)} %bitcast.at_ref, f32[3,17]{1,0:T(4,128)S(1)} %copy-done, f32[32,1024]{1,0:T(8,128)S(1)} %get-tuple-element.15.own_ref, bf16[32,1024]{1,0:T(8,128)(2,1)S(1)} %collective-permute-done.6.m2, bf16[32,1024]{1,0:T(8,128)(2,1)S(1)} %collective-permute-done.7.m1, ...), custom_call_target="tpu_custom_call" | custom-call | tf_op jit(solution)/shard_map/deblur/pallas_call | solution.py:384
  (7 shorter events, 0.1 us)
Async XLA Ops:
  4.2 12.2 %collective-permute-start = (bf16[16,3584]{1,0:T(8,128)(2,1)}, bf16[16,3584]{1,0:T(8,128)(2,1)S(1)}, u32[]{:S(2)}, u32[]{:S(2)}) collective-permute-start(bf16[16,3584]{1,0:T(8,128)(2,1)} %get-tuple-element.8), channel_id=1, source_target_pairs={{0,1},{1,0},{2,3},{3,2},{4,5},{5,4},{6,7},{7,6},{8,9},{9,8},{10,11... | collective-permute-start | bytes 344072 | tf_op jit(solution)/shard_map/ppermute | solution.py:371
  7.2 11.9 %collective-permute-start.1 = (bf16[16,3584]{1,0:T(8,128)(2,1)}, bf16[16,3584]{1,0:T(8,128)(2,1)S(1)}, u32[]{:S(2)}, u32[]{:S(2)}) collective-permute-start(bf16[16,3584]{1,0:T(8,128)(2,1)} %get-tuple-element.9), channel_id=1, source_target_pairs={{0,2},{1,3},{2,0},{3,1},{4,6},{5,7},{6,4},{7,5},{8,10},{9,11},{10,... | collective-permute-start | bytes 344072 | tf_op jit(solution)/shard_map/ppermute | solution.py:371
  9.8 9.3 %collective-permute-start.2 = (bf16[16,3584]{1,0:T(8,128)(2,1)}, bf16[16,3584]{1,0:T(8,128)(2,1)S(1)}, u32[]{:S(2)}, u32[]{:S(2)}) collective-permute-start(bf16[16,3584]{1,0:T(8,128)(2,1)} %get-tuple-element.10), channel_id=1, source_target_pairs={{0,3},{1,2},{2,1},{3,0},{4,7},{5,6},{6,5},{7,4},{8,11},{9,10},{10,... | collective-permute-start | bytes 344072 | tf_op jit(solution)/shard_map/ppermute | solution.py:371
  9.8 0.9 %copy-start.1 = (bf16[16,3584]{1,0:T(8,128)(2,1)S(1)}, bf16[16,3584]{1,0:T(8,128)(2,1)}, u32[]{:S(2)}) copy-start(bf16[16,3584]{1,0:T(8,128)(2,1)} %get-tuple-element.11.refs_0_) | copy-start | bytes 344068
  16.4 39.9 %copy-start = (f32[3,17]{1,0:T(4,128)S(1)}, f32[3,17]{1,0:T(4,128)}, u32[]{:S(2)}) copy-start(f32[3,17]{1,0:T(4,128)} %taps_ref.1) | copy-start | bytes 616
  39.2 6.7 %collective-permute-start.5 = (f16[32,1024]{1,0:T(8,128)(2,1)S(1)}, f16[32,1024]{1,0:T(8,128)(2,1)S(1)}, u32[]{:S(2)}, u32[]{:S(2)}) collective-permute-start(f16[32,1024]{1,0:T(8,128)(2,1)S(1)} %convert_element_type.18), channel_id=1, source_target_pairs={{0,3},{1,2},{2,1},{3,0},{4,7},{5,6},{6,5},{7,4},{8,11},{9,10},{10,... | collective-permute-start | bytes 196616 | tf_op jit(solution)/shard_map/ppermute | solution.py:347
  41.7 5.9 %collective-permute-start.4 = (f16[32,1024]{1,0:T(8,128)(2,1)S(1)}, f16[32,1024]{1,0:T(8,128)(2,1)S(1)}, u32[]{:S(2)}, u32[]{:S(2)}) collective-permute-start(f16[32,1024]{1,0:T(8,128)(2,1)S(1)} %convert_element_type.18), channel_id=1, source_target_pairs={{0,2},{1,3},{2,0},{3,1},{4,6},{5,7},{6,4},{7,5},{8,10},{9,11},{10,... | collective-permute-start | bytes 196616 | tf_op jit(solution)/shard_map/ppermute | solution.py:347
  42.5 5.1 %collective-permute-start.3 = (f16[32,1024]{1,0:T(8,128)(2,1)S(1)}, f16[32,1024]{1,0:T(8,128)(2,1)S(1)}, u32[]{:S(2)}, u32[]{:S(2)}) collective-permute-start(f16[32,1024]{1,0:T(8,128)(2,1)S(1)} %convert_element_type.18), channel_id=1, source_target_pairs={{0,1},{1,0},{2,3},{3,2},{4,5},{5,4},{6,7},{7,6},{8,9},{9,8},{10,11... | collective-permute-start | bytes 196616 | tf_op jit(solution)/shard_map/ppermute | solution.py:347
  47.6 5.1 %collective-permute-start.9 = (bf16[32,1024]{1,0:T(8,128)(2,1)S(1)}, bf16[32,1024]{1,0:T(8,128)(2,1)S(1)}, u32[]{:S(2)}, u32[]{:S(2)}) collective-permute-start(bf16[32,1024]{1,0:T(8,128)(2,1)S(1)} %get-tuple-element.14), channel_id=1, source_target_pairs={{0,24},{4,28},{8,0},{12,4},{16,8},{20,12},{24,16},{28,20},{1,25},{... | collective-permute-start | bytes 196616 | tf_op jit(solution)/shard_map/ppermute | solution.py:382
  50.3 3.7 %collective-permute-start.8 = (bf16[32,1024]{1,0:T(8,128)(2,1)S(1)}, bf16[32,1024]{1,0:T(8,128)(2,1)S(1)}, u32[]{:S(2)}, u32[]{:S(2)}) collective-permute-start(bf16[32,1024]{1,0:T(8,128)(2,1)S(1)} %get-tuple-element.14), channel_id=1, source_target_pairs={{0,28},{4,0},{8,4},{12,8},{16,12},{20,16},{24,20},{28,24},{1,29},{... | collective-permute-start | bytes 196616 | tf_op jit(solution)/shard_map/ppermute | solution.py:382
  50.3 4.6 %collective-permute-start.7 = (bf16[32,1024]{1,0:T(8,128)(2,1)S(1)}, bf16[32,1024]{1,0:T(8,128)(2,1)S(1)}, u32[]{:S(2)}, u32[]{:S(2)}) collective-permute-start(bf16[32,1024]{1,0:T(8,128)(2,1)S(1)} %get-tuple-element.14), channel_id=1, source_target_pairs={{0,4},{4,8},{8,12},{12,16},{16,20},{20,24},{24,28},{28,0},{1,5},{5... | collective-permute-start | bytes 196616 | tf_op jit(solution)/shard_map/ppermute | solution.py:382
  50.8 5.5 %collective-permute-start.6 = (bf16[32,1024]{1,0:T(8,128)(2,1)S(1)}, bf16[32,1024]{1,0:T(8,128)(2,1)S(1)}, u32[]{:S(2)}, u32[]{:S(2)}) collective-permute-start(bf16[32,1024]{1,0:T(8,128)(2,1)S(1)} %get-tuple-element.14), channel_id=1, source_target_pairs={{0,8},{4,12},{8,16},{12,20},{16,24},{20,28},{24,0},{28,4},{1,9},{5... | collective-permute-start | bytes 196616 | tf_op jit(solution)/shard_map/ppermute | solution.py:382

commit v5 on v4

--- a/solution.py
+++ b/solution.py
@@ -22,8 +22,9 @@
 BACKGROUND = 0.05
 SMALLER = 0.25
 
-FA, FB, DA, DB = 0, 16, 32, 64
-ENTRIES = 72
+YL, XA, XB, DC, DS, DE, DB = 0, 6, 10, 18, 22, 26, 30
+ENTRIES = 38
+EXTRA = 3
 
 
 def sincos(t):
@@ -60,35 +61,37 @@
     x_refs, refs = refs[:chunks], refs[chunks:]
     first = scale is None
     if first:
-        acc, xs, com, tabs = refs[0], refs[1], refs[2], refs[3:4]
+        acc, xs, tabs = refs[0], refs[1], refs[2:3]
     else:
-        acc_in, out_ref, xs, com, tabs = refs[0], refs[1], refs[2], refs[3], refs[4:6]
-        acc, works, sem = refs[6], refs[7:9], refs[9]
+        acc_in, out_ref, xs, tabs = refs[0], refs[1], refs[2], refs[3:5]
+        acc, works, sem = refs[5], refs[6:8], refs[8]
         fetch = pltpu.make_async_copy(acc_in, acc, sem)
         fetch.start()
     parts = width // LANES
-    cols = 2 * width
-    pieces = com.shape[1]
     for g in range(chunks):
-        xs[g] = x_refs[g][:, :cols]
-        common = x_refs[g][:, cols:].astype(jnp.float32)
-        for piece in range(pieces):
-            com[g, piece] = common[:, piece * LANES : (piece + 1) * LANES]
+        for b in range(own + EXTRA):
+            pair = x_refs[g][b].astype(jnp.float32)
+            for i in range(parts):
+                xs[g, i, 2 * b : 2 * b + 2, :] = pair[:, i * LANES : (i + 1) * LANES]
     bins = (lax.broadcasted_iota(jnp.int32, (own, LANES), 0) + (first_ref[0] + F0)).astype(jnp.float32)
     half_omega = bins * (TWO_PI / NT / 2.0)
+    row = lax.broadcasted_iota(jnp.int32, (8, LANES), 0)
+    bits = [(row & (1 << level)) != 0 for level in range(3)]
+    away = jnp.where(row < 4, 3 - row, row - 4)
+    near = (away & 1) != 0, away >= 2
+    sign = jnp.where(row < 4, -1.0, 1.0)
 
     def tables(tab, g, i):
         def common(which):
-            index = which * parts + i
-            row = com[g, index % pieces, pl.ds(index // pieces, 1), :]
-            return jnp.broadcast_to(row, (own, LANES))
+            at = 2 * own + which
+            return jnp.broadcast_to(xs[g, i, at : at + 1, :], (own, LANES))
 
         lag = common(0) * 64.0 + common(1)
         turns = bins * lag
         rest = turns - jnp.floor(turns * (1.0 / NT) + 0.5) * float(NT)
         turn = doubled(doubled(sincos(rest * (TWO_PI / NT / 4.0))))
-        re = xs[g, :, pl.ds(pl.multiple_of(i * LANES, LANES), LANES)].astype(jnp.float32)
-        im = xs[g, :, pl.ds(pl.multiple_of(width + i * LANES, LANES), LANES)].astype(jnp.float32)
+        re = xs[g, i, pl.ds(0, own, stride=2), :]
+        im = xs[g, i, pl.ds(1, own, stride=2), :]
         al = re * turn[0] + im * turn[1], im * turn[0] - re * turn[1]
 
         def put(entry, value):
@@ -107,21 +110,27 @@
                 rows = [level[bit] if row is None else row * level[bit] for bit in range(2) for row in rows]
             return rows
 
-        for entry, value in enumerate(products(yl + xl[:1])):
-            put(FA + entry, value)
-        for entry, value in enumerate(products(xl[1:])):
-            put(FB + entry, value)
+        for level in range(3):
+            put(YL + 2 * level, yl[level][0])
+            put(YL + 2 * level + 1, yl[level][1])
+        for entry, value in enumerate(products(xl[:2])):
+            put(XA + entry, value)
+        for entry, value in enumerate(products(xl[2:])):
+            put(XB + entry, value)
 
         half = sincos(half_omega * common(4))
-        rows = [half]
-        power = half
-        for _ in range(4):
-            power = doubled(power)
-            rows = rows + [times(row, power) for row in rows]
+        e1 = doubled(half)
+        e2 = doubled(e1)
+        rows = [half, times(half, e1)]
+        rows += [times(e, e2) for e in rows]
         for entry, value in enumerate(rows):
-            put(DA + entry, value[0])
-            put(DA + 16 + entry, value[1])
-        e16 = doubled(power)
+            put(DC + entry, value[0])
+            put(DS + entry, value[1])
+        e4 = doubled(e2)
+        e8 = doubled(e4)
+        for entry, value in enumerate(e4 + times(e4, e8)):
+            put(DE + entry, value)
+        e16 = doubled(e8)
         e48 = times(e16, doubled(e16))
         for low, high, e in ((0, 3, e48), (1, 2, e16)):
             rc, ms, mc, rs = al[0] * e[0], al[1] * e[1], al[1] * e[0], al[0] * e[1]
@@ -131,21 +140,42 @@
             put(DB + 4 + low, mc + rs)
 
     def beams(tab, f):
-        def rows16(entry, i):
-            return tab[i, pl.ds(entry * own + f, 16, stride=own), :].astype(jnp.bfloat16)
-
-        def spread(entry, i):
-            row = tab[i, pl.ds(entry * own + f, 1), :]
-            return jnp.broadcast_to(row, (16, LANES)).astype(jnp.bfloat16)
+        def spread(entry, i, rows=8):
+            return jnp.broadcast_to(tab[i, pl.ds(entry * own + f, 1), :], (rows, LANES))
+
+        def narrow(entry, i):
+            return spread(entry, i, 16).astype(jnp.bfloat16)
+
+        def pack(low, high):
+            return jnp.concatenate([low, high], axis=0).astype(jnp.bfloat16)
 
         left, right = [], []
         for i in range(parts):
-            a = rows16(FA, i)
-            left.append(jnp.concatenate([a * spread(FB + b, i) for b in range(16)], axis=0))
-            ar, ai = rows16(DA, i), rows16(DA + 16, i)
+            y = None
+            for level in range(3):
+                level_y = jnp.where(bits[level], spread(YL + 2 * level + 1, i), spread(YL + 2 * level, i))
+                y = level_y if y is None else y * level_y
+            xy = [y * spread(XA + k, i) for k in range(4)]
+            xy = [pack(xy[0], xy[1]), pack(xy[2], xy[3])]
+            rows = []
+            for b in range(8):
+                by = narrow(XB + b, i)
+                rows += [xy[0] * by, xy[1] * by]
+            left.append(jnp.concatenate(rows, axis=0))
+
+            def middle(entry):
+                e = [spread(entry + k, i) for k in range(4)]
+                return jnp.where(near[1], jnp.where(near[0], e[3], e[2]), jnp.where(near[0], e[1], e[0]))
+
+            mc, ms = middle(DC), middle(DS) * sign
+            turned = []
+            for k in range(2):
+                c, s = spread(DE + 2 * k, i), spread(DE + 2 * k + 1, i)
+                turned.append((c * mc - s * ms, s * mc + c * ms))
+            ar, ai = pack(turned[0][0], turned[1][0]), pack(turned[0][1], turned[1][1])
             real, imag = [], []
             for h in range(4):
-                br, bi = spread(DB + h, i), spread(DB + 4 + h, i)
+                br, bi = narrow(DB + h, i), narrow(DB + 4 + h, i)
                 rr, ii, ri, ir = ar * br, ai * bi, ar * bi, ai * br
                 real += [rr + ii, rr - ii]
                 imag += [ri - ir, ri + ir]
@@ -215,17 +245,14 @@
         )
 
 
-def beams_call(chunks, own, width, pieces, scale, *args):
+def beams_call(chunks, own, width, scale, *args):
     first = scale is None
     vmem = pl.BlockSpec(memory_space=pltpu.VMEM)
     smem = pl.BlockSpec(memory_space=pltpu.SMEM)
     rows = CX * CY
     acc = (own, rows, 2 * CZ)
     tab = pltpu.VMEM((width // LANES, ENTRIES * own, LANES), jnp.float32)
-    scratch = [
-        pltpu.VMEM((chunks, own, 2 * width), jnp.bfloat16),
-        pltpu.VMEM((chunks, pieces, own, LANES), jnp.float32),
-    ]
+    scratch = [pltpu.VMEM((chunks, width // LANES, 2 * (own + EXTRA), LANES), jnp.float32)]
     if first:
         scratch += [tab]
         out = jax.ShapeDtypeStruct(acc, jnp.float32)
@@ -316,24 +343,35 @@
         est_ref[:, y, :] = est[:, y * CZ : (y + 1) * CZ]
 
 
-def bundle_kernel(groups, own, me_ref, flat_ref, lag_ref, slow_ref, *refs):
-    outs, common = refs[:groups], refs[groups]
-    cols = flat_ref.shape[1]
-    parts = lag_ref.shape[1] // LANES
-    pieces = common.shape[1] // LANES
-    lag = lag_ref[...]
-    slow = slow_ref[...].astype(jnp.float32)
-    rows = [(lag >> 6).astype(jnp.float32), (lag & 63).astype(jnp.float32)] + [slow[d : d + 1] for d in range(3)]
-    common[...] = jnp.zeros_like(common)
-    for index in range(len(rows) * parts):
-        row, i = rows[index // parts], index % parts
-        at, piece = index // pieces, index % pieces
-        common[at : at + 1, piece * LANES : (piece + 1) * LANES] = row[:, i * LANES : (i + 1) * LANES]
-    shared = common[...].astype(jnp.bfloat16)
+def bundle_kernel(groups, own, me_ref, spectra_ref, lag_ref, slow_ref, *refs):
+    outs, (lag_in, slow_in, sems) = refs[:groups], refs[groups:]
+    small = [
+        pltpu.make_async_copy(lag_ref, lag_in, sems.at[groups]),
+        pltpu.make_async_copy(slow_ref, slow_in, sems.at[groups + 1]),
+    ]
+    for copy in small:
+        copy.start()
+    slices = []
     for k in range(groups):
         dest = me_ref[0] ^ k if groups & (groups - 1) == 0 else lax.rem(me_ref[0] + k, groups)
-        outs[k][:, :cols] = flat_ref[pl.ds(pl.multiple_of(dest * own, own), own), :]
-        outs[k][:, cols:] = shared
+        slices.append(
+            pltpu.make_async_copy(spectra_ref.at[pl.ds(dest * own, own)], outs[k].at[pl.ds(0, own)], sems.at[k])
+        )
+        slices[k].start()
+    for copy in small:
+        copy.wait()
+    lag = lag_in[...]
+    slow = slow_in[...].astype(jnp.float32)
+    pairs = [
+        jnp.concatenate([(lag >> 6).astype(jnp.float32), (lag & 63).astype(jnp.float32)], axis=0),
+        slow[:2],
+        jnp.concatenate([slow[2:], slow[2:]], axis=0),
+    ]
+    for k in range(groups):
+        for extra, pair in enumerate(pairs):
+            outs[k][own + extra] = pair.astype(jnp.bfloat16)
+    for copy in slices:
+        copy.wait()
 
 
 def moves(k, size):
@@ -357,23 +395,25 @@
     me = lax.axis_index("sta").astype(jnp.int32)
     vmem = pl.BlockSpec(memory_space=pltpu.VMEM)
     smem = pl.BlockSpec(memory_space=pltpu.SMEM)
-    parts = width // LANES
-    pieces = -(-5 * parts // own)
-    cols = 2 * width + pieces * LANES
+    hbm = pl.BlockSpec(memory_space=pl.ANY)
     blocks = pl.pallas_call(
         functools.partial(bundle_kernel, groups, own),
-        out_shape=[jax.ShapeDtypeStruct((own, cols), jnp.bfloat16)] * groups,
-        in_specs=[smem] + [vmem] * 3,
+        out_shape=[jax.ShapeDtypeStruct((own + EXTRA, 2, width), jnp.bfloat16)] * groups,
+        in_specs=[smem] + [hbm] * 3,
         out_specs=[vmem] * groups,
-        scratch_shapes=[pltpu.VMEM((own, pieces * LANES), jnp.float32)],
+        scratch_shapes=[
+            pltpu.VMEM((1, width), jnp.int32),
+            pltpu.VMEM((3, width), jnp.bfloat16),
+            pltpu.SemaphoreType.DMA((groups + 2,)),
+        ],
         name="bundles",
-    )(me.reshape(1), spectra.reshape(freqs, 2 * width), lag_samples, slowness[0])
+    )(me.reshape(1), spectra, lag_samples, slowness[0])
     blocks = [blocks[0]] + [lax.ppermute(blocks[k], "sta", moves(k, groups)) for k in range(1, groups)]
 
     at = (me * own).reshape(1)
     scale = SMALLER / (freqs * width * groups)
-    held = beams_call(1, own, width, pieces, None, at, blocks[0])
-    local = beams_call(groups - 1, own, width, pieces, scale, at, *blocks[1:], held)
+    held = beams_call(1, own, width, None, at, blocks[0])
+    local = beams_call(groups - 1, own, width, scale, at, *blocks[1:], held)
 
     total = summed_over(local, "sta", groups)
     narrow = total.astype(jnp.bfloat16)

time: 63.8 us -> 59.2 us (0.928)
  Pallas kernels: 34.8 us -> 30.9 us
  local copies, waits for them, and re-layouts: 2.68 us -> 0.91 us
  waiting for transfers between devices: 12.1 us -> 13.2 us
    pallas_call x2, Pallas kernels: 25.7 us -> 21.7 us  [beams_call(): pl.pallas_call(functools.partial(beam_kernel, chunks, own, width, scale),...]
    unnamed x5 -> x4, local copies, waits for them, and re-layouts: 2.68 us -> 0.91 us
    ppermute x3, waiting for transfers between devices: 2.69 us -> 3.82 us  [per_device(): lax.ppermute(blocks[k], 'sta', moves(k, groups))]
  transfers between devices with their start and end apart: 10 -> 10, of which waited for: 7 -> 7; matrix products, arithmetic and copies ran while one was open for 0% -> 0% of each run, Pallas kernels for 9% -> 8%
where the time goes in v5:
time: 59.2 us; the launch traced here: 59 us
  Pallas kernels  30.9 us (52%)
  waiting for transfers between devices  13.2 us (22%)
  starting transfers between devices  13.1 us (22%)
  local copies, waits for them, and re-layouts  0.91 us (2%)
  between operations  0.7 us (1%)
    pallas_call x2, Pallas kernels, beams_call(): pl.pallas_call(functools.partial(beam_kernel, chunks, own, width, scale),...  21.7 us
    pallas_call x1, Pallas kernels, per_device(): pl.pallas_call(functools.partial(deblur_kernel, tiles), out_shape=(tile,...  7.32 us
    ppermute x3, starting transfers between devices, per_device(): lax.ppermute(blocks[k], 'sta', moves(k, groups))  5.68 us
    ppermute x4, waiting for transfers between devices, per_device(): lax.ppermute(narrow, 'grid', [(i, (i + shift) % tiles) for i in range(til...  5.48 us
    ppermute x3, starting transfers between devices, summed_over(): lax.ppermute(half, axis, moves(k, size))  4.45 us
    ppermute x3, waiting for transfers between devices, summed_over(): lax.ppermute(half, axis, moves(k, size))  3.94 us
    ppermute x3, waiting for transfers between devices, per_device(): lax.ppermute(blocks[k], 'sta', moves(k, groups))  3.82 us
    ppermute x4, starting transfers between devices, per_device(): lax.ppermute(narrow, 'grid', [(i, (i + shift) % tiles) for i in range(til...  3.01 us
  transfers between devices with their start and end apart: 10, of which 7 were waited for; matrix products, arithmetic and copies ran while one was open for 0% of the time, Pallas kernels for 8%

profile of v5, /device:TPU:0, one launch (start us, length us, event | category | flops | bytes accessed | tf_op | source)
XLA Modules:
  0.0 59.0 jit_solution(1262391258591078242)
XLA Ops:
  0.6 1.9 %bundles.1 = (bf16[19,2,1536]{2,1,0:T(2,128)(2,1)}, bf16[19,2,1536]{2,1,0:T(2,128)(2,1)}, bf16[19,2,1536]{2,1,0:T(2,128)(2,1)}, bf16[19,2,1536]{2,1,0:T(2,128)(2,1)}) custom-call(s32[1]{0:T(128)} %bitcast.2.me_ref, bf16[64,2,1536]{2,1,0:T(2,128)(2,1)} %spectra_ref.1, s32[1,1536]{1,0:T(1,128)} %lag_ref.1, bf16[3,1536]{1,0:T(4,128)(2,1)} %bitcast.6), custom_call_target="tpu_custom_call" | custom-call | tf_op jit(solution)/shard_map/bundles/pallas_call | solution.py:399
  2.5 3.1 %collective-permute-start = (bf16[19,2,1536]{2,1,0:T(2,128)(2,1)}, bf16[19,2,1536]{2,1,0:T(2,128)(2,1)S(1)}, u32[]{:S(2)}, u32[]{:S(2)}) collective-permute-start(bf16[19,2,1536]{2,1,0:T(2,128)(2,1)} %get-tuple-element.8), channel_id=1, source_target_pairs={{0,1},{1,0},{2,3},{3,2},{4,5},{5,4},{6,7},{7,6},{8,9},{9,8},{10,11... | collective-permute-start | bytes 350216 | tf_op jit(solution)/shard_map/ppermute | solution.py:411
  5.6 2.6 %collective-permute-start.1 = (bf16[19,2,1536]{2,1,0:T(2,128)(2,1)}, bf16[19,2,1536]{2,1,0:T(2,128)(2,1)S(1)}, u32[]{:S(2)}, u32[]{:S(2)}) collective-permute-start(bf16[19,2,1536]{2,1,0:T(2,128)(2,1)} %get-tuple-element.9), channel_id=1, source_target_pairs={{0,2},{1,3},{2,0},{3,1},{4,6},{5,7},{6,4},{7,5},{8,10},{9,11},{10,... | collective-permute-start | bytes 350216 | tf_op jit(solution)/shard_map/ppermute | solution.py:411
  8.2 0.9 %copy-done.1 = bf16[19,2,1536]{2,1,0:T(2,128)(2,1)S(1)} copy-done((bf16[19,2,1536]{2,1,0:T(2,128)(2,1)S(1)}, bf16[19,2,1536]{2,1,0:T(2,128)(2,1)}, u32[]{:S(2)}) %copy-start.1) | copy-done | bytes 116760
  9.1 4.7 %beams_own.1.refs_3_ = f32[16,256,256]{2,1,0:T(8,128)S(1)} custom-call(s32[1]{0:T(128)} %bitcast.1.first_ref, bf16[19,2,1536]{2,1,0:T(2,128)(2,1)S(1)} %copy-done.1), custom_call_target="tpu_custom_call" | custom-call | flops 3221225472 | bytes 4194304 | tf_op jit(solution)/shard_map/beams_own/pallas_call | solution.py:265
  13.8 0.0 copy-start
  13.8 0.0 collective-permute-done.refs_0_
  13.9 3.8 %collective-permute-done.1.refs_1_ = bf16[19,2,1536]{2,1,0:T(2,128)(2,1)S(1)} collective-permute-done((bf16[19,2,1536]{2,1,0:T(2,128)(2,1)}, bf16[19,2,1536]{2,1,0:T(2,128)(2,1)S(1)}, u32[]{:S(2)}, u32[]{:S(2)}) %collective-permute-start.1) | collective-permute-done | bytes 116768 | tf_op jit(solution)/shard_map/ppermute | solution.py:411
  17.7 0.0 collective-permute-done.2.refs_2_
  17.7 17.0 %beams_rest.1 = f32[32,1024]{1,0:T(8,128)S(1)} custom-call(s32[1]{0:T(128)} %bitcast.1.first_ref, bf16[19,2,1536]{2,1,0:T(2,128)(2,1)S(1)} %collective-permute-done.refs_0_, bf16[19,2,1536]{2,1,0:T(2,128)(2,1)S(1)} %collective-permute-done.1.refs_1_, bf16[19,2,1536]{2,1,0:T(2,128)(2,1)S(1)} %collective-permute-done.2.refs_2_, ...), custom_call_target="tpu_custom_call" | custom-call | flops 9663676416 | bytes 4194304 | tf_op jit(solution)/shard_map/beams_rest/pallas_call | solution.py:265
  34.7 2.5 %collective-permute-start.5 = (f16[32,1024]{1,0:T(8,128)(2,1)S(1)}, f16[32,1024]{1,0:T(8,128)(2,1)S(1)}, u32[]{:S(2)}, u32[]{:S(2)}) collective-permute-start(f16[32,1024]{1,0:T(8,128)(2,1)S(1)} %convert_element_type.18), channel_id=1, source_target_pairs={{0,3},{1,2},{2,1},{3,0},{4,7},{5,6},{6,5},{7,4},{8,11},{9,10},{10,... | collective-permute-start | bytes 196616 | tf_op jit(solution)/shard_map/ppermute | solution.py:385
  37.2 0.8 %collective-permute-start.4 = (f16[32,1024]{1,0:T(8,128)(2,1)S(1)}, f16[32,1024]{1,0:T(8,128)(2,1)S(1)}, u32[]{:S(2)}, u32[]{:S(2)}) collective-permute-start(f16[32,1024]{1,0:T(8,128)(2,1)S(1)} %convert_element_type.18), channel_id=1, source_target_pairs={{0,2},{1,3},{2,0},{3,1},{4,6},{5,7},{6,4},{7,5},{8,10},{9,11},{10,... | collective-permute-start | bytes 196616 | tf_op jit(solution)/shard_map/ppermute | solution.py:385
  38.0 1.1 %collective-permute-start.3 = (f16[32,1024]{1,0:T(8,128)(2,1)S(1)}, f16[32,1024]{1,0:T(8,128)(2,1)S(1)}, u32[]{:S(2)}, u32[]{:S(2)}) collective-permute-start(f16[32,1024]{1,0:T(8,128)(2,1)S(1)} %convert_element_type.18), channel_id=1, source_target_pairs={{0,1},{1,0},{2,3},{3,2},{4,5},{5,4},{6,7},{7,6},{8,9},{9,8},{10,11... | collective-permute-start | bytes 196616 | tf_op jit(solution)/shard_map/ppermute | solution.py:385
  39.2 2.3 %collective-permute-done.5 = f16[32,1024]{1,0:T(8,128)(2,1)S(1)} collective-permute-done((f16[32,1024]{1,0:T(8,128)(2,1)S(1)}, f16[32,1024]{1,0:T(8,128)(2,1)S(1)}, u32[]{:S(2)}, u32[]{:S(2)}) %collective-permute-start.5) | collective-permute-done | bytes 65568 | tf_op jit(solution)/shard_map/ppermute | solution.py:385
  41.5 1.6 %collective-permute-done.4 = f16[32,1024]{1,0:T(8,128)(2,1)S(1)} collective-permute-done((f16[32,1024]{1,0:T(8,128)(2,1)S(1)}, f16[32,1024]{1,0:T(8,128)(2,1)S(1)}, u32[]{:S(2)}, u32[]{:S(2)}) %collective-permute-start.4) | collective-permute-done | bytes 65568 | tf_op jit(solution)/shard_map/ppermute | solution.py:385
  43.1 2.5 %collective-permute-start.9 = (bf16[32,1024]{1,0:T(8,128)(2,1)S(1)}, bf16[32,1024]{1,0:T(8,128)(2,1)S(1)}, u32[]{:S(2)}, u32[]{:S(2)}) collective-permute-start(bf16[32,1024]{1,0:T(8,128)(2,1)S(1)} %get-tuple-element.14), channel_id=1, source_target_pairs={{0,24},{4,28},{8,0},{12,4},{16,8},{20,12},{24,16},{28,20},{1,25},{... | collective-permute-start | bytes 196616 | tf_op jit(solution)/shard_map/ppermute | solution.py:422
  45.6 0.0 collective-permute-start.8
  45.6 0.5 collective-permute-start.7
  46.2 0.0 collective-permute-start.6
  46.2 1.9 %collective-permute-done.9.p2 = bf16[32,1024]{1,0:T(8,128)(2,1)S(1)} collective-permute-done((bf16[32,1024]{1,0:T(8,128)(2,1)S(1)}, bf16[32,1024]{1,0:T(8,128)(2,1)S(1)}, u32[]{:S(2)}, u32[]{:S(2)}) %collective-permute-start.9) | collective-permute-done | bytes 65568 | tf_op jit(solution)/shard_map/ppermute | solution.py:422
  48.0 1.3 %collective-permute-done.8.p1 = bf16[32,1024]{1,0:T(8,128)(2,1)S(1)} collective-permute-done((bf16[32,1024]{1,0:T(8,128)(2,1)S(1)}, bf16[32,1024]{1,0:T(8,128)(2,1)S(1)}, u32[]{:S(2)}, u32[]{:S(2)}) %collective-permute-start.8) | collective-permute-done | bytes 65568 | tf_op jit(solution)/shard_map/ppermute | solution.py:422
  49.4 0.9 %collective-permute-done.7.m1 = bf16[32,1024]{1,0:T(8,128)(2,1)S(1)} collective-permute-done((bf16[32,1024]{1,0:T(8,128)(2,1)S(1)}, bf16[32,1024]{1,0:T(8,128)(2,1)S(1)}, u32[]{:S(2)}, u32[]{:S(2)}) %collective-permute-start.7) | collective-permute-done | bytes 65568 | tf_op jit(solution)/shard_map/ppermute | solution.py:422
  50.2 1.4 %collective-permute-done.6.m2 = bf16[32,1024]{1,0:T(8,128)(2,1)S(1)} collective-permute-done((bf16[32,1024]{1,0:T(8,128)(2,1)S(1)}, bf16[32,1024]{1,0:T(8,128)(2,1)S(1)}, u32[]{:S(2)}, u32[]{:S(2)}) %collective-permute-start.6) | collective-permute-done | bytes 65568 | tf_op jit(solution)/shard_map/ppermute | solution.py:422
  51.6 7.3 %deblur.1 = (f32[32,8,128]{2,1,0:T(8,128)}, f32[32,8,128]{2,1,0:T(8,128)}) custom-call(s32[1]{0:T(128)} %bitcast.at_ref, f32[3,17]{1,0:T(4,128)S(1)} %copy-done, f32[32,1024]{1,0:T(8,128)S(1)} %get-tuple-element.15.own_ref, bf16[32,1024]{1,0:T(8,128)(2,1)S(1)} %collective-permute-done.6.m2, bf16[32,1024]{1,0:T(8,128)(2,1)S(1)} %collective-permute-done.7.m1, ...), custom_call_target="tpu_custom_call" | custom-call | tf_op jit(solution)/shard_map/deblur/pallas_call | solution.py:424
  (6 shorter events, 0.1 us)
Async XLA Ops:
  2.5 11.3 %collective-permute-start = (bf16[19,2,1536]{2,1,0:T(2,128)(2,1)}, bf16[19,2,1536]{2,1,0:T(2,128)(2,1)S(1)}, u32[]{:S(2)}, u32[]{:S(2)}) collective-permute-start(bf16[19,2,1536]{2,1,0:T(2,128)(2,1)} %get-tuple-element.8), channel_id=1, source_target_pairs={{0,1},{1,0},{2,3},{3,2},{4,5},{5,4},{6,7},{7,6},{8,9},{9,8},{10,11... | collective-permute-start | bytes 350216 | tf_op jit(solution)/shard_map/ppermute | solution.py:411
  5.6 12.1 %collective-permute-start.1 = (bf16[19,2,1536]{2,1,0:T(2,128)(2,1)}, bf16[19,2,1536]{2,1,0:T(2,128)(2,1)S(1)}, u32[]{:S(2)}, u32[]{:S(2)}) collective-permute-start(bf16[19,2,1536]{2,1,0:T(2,128)(2,1)} %get-tuple-element.9), channel_id=1, source_target_pairs={{0,2},{1,3},{2,0},{3,1},{4,6},{5,7},{6,4},{7,5},{8,10},{9,11},{10,... | collective-permute-start | bytes 350216 | tf_op jit(solution)/shard_map/ppermute | solution.py:411
  8.2 9.5 %collective-permute-start.2 = (bf16[19,2,1536]{2,1,0:T(2,128)(2,1)}, bf16[19,2,1536]{2,1,0:T(2,128)(2,1)S(1)}, u32[]{:S(2)}, u32[]{:S(2)}) collective-permute-start(bf16[19,2,1536]{2,1,0:T(2,128)(2,1)} %get-tuple-element.10), channel_id=1, source_target_pairs={{0,3},{1,2},{2,1},{3,0},{4,7},{5,6},{6,5},{7,4},{8,11},{9,10},{10,... | collective-permute-start | bytes 350216 | tf_op jit(solution)/shard_map/ppermute | solution.py:411
  8.2 0.9 %copy-start.1 = (bf16[19,2,1536]{2,1,0:T(2,128)(2,1)S(1)}, bf16[19,2,1536]{2,1,0:T(2,128)(2,1)}, u32[]{:S(2)}) copy-start(bf16[19,2,1536]{2,1,0:T(2,128)(2,1)} %get-tuple-element.11.refs_0_) | copy-start | bytes 350212
  13.8 37.8 %copy-start = (f32[3,17]{1,0:T(4,128)S(1)}, f32[3,17]{1,0:T(4,128)}, u32[]{:S(2)}) copy-start(f32[3,17]{1,0:T(4,128)} %taps_ref.1) | copy-start | bytes 616
  34.7 6.8 %collective-permute-start.5 = (f16[32,1024]{1,0:T(8,128)(2,1)S(1)}, f16[32,1024]{1,0:T(8,128)(2,1)S(1)}, u32[]{:S(2)}, u32[]{:S(2)}) collective-permute-start(f16[32,1024]{1,0:T(8,128)(2,1)S(1)} %convert_element_type.18), channel_id=1, source_target_pairs={{0,3},{1,2},{2,1},{3,0},{4,7},{5,6},{6,5},{7,4},{8,11},{9,10},{10,... | collective-permute-start | bytes 196616 | tf_op jit(solution)/shard_map/ppermute | solution.py:385
  37.2 5.9 %collective-permute-start.4 = (f16[32,1024]{1,0:T(8,128)(2,1)S(1)}, f16[32,1024]{1,0:T(8,128)(2,1)S(1)}, u32[]{:S(2)}, u32[]{:S(2)}) collective-permute-start(f16[32,1024]{1,0:T(8,128)(2,1)S(1)} %convert_element_type.18), channel_id=1, source_target_pairs={{0,2},{1,3},{2,0},{3,1},{4,6},{5,7},{6,4},{7,5},{8,10},{9,11},{10,... | collective-permute-start | bytes 196616 | tf_op jit(solution)/shard_map/ppermute | solution.py:385
  38.0 5.1 %collective-permute-start.3 = (f16[32,1024]{1,0:T(8,128)(2,1)S(1)}, f16[32,1024]{1,0:T(8,128)(2,1)S(1)}, u32[]{:S(2)}, u32[]{:S(2)}) collective-permute-start(f16[32,1024]{1,0:T(8,128)(2,1)S(1)} %convert_element_type.18), channel_id=1, source_target_pairs={{0,1},{1,0},{2,3},{3,2},{4,5},{5,4},{6,7},{7,6},{8,9},{9,8},{10,11... | collective-permute-start | bytes 196616 | tf_op jit(solution)/shard_map/ppermute | solution.py:385
  43.1 4.9 %collective-permute-start.9 = (bf16[32,1024]{1,0:T(8,128)(2,1)S(1)}, bf16[32,1024]{1,0:T(8,128)(2,1)S(1)}, u32[]{:S(2)}, u32[]{:S(2)}) collective-permute-start(bf16[32,1024]{1,0:T(8,128)(2,1)S(1)} %get-tuple-element.14), channel_id=1, source_target_pairs={{0,24},{4,28},{8,0},{12,4},{16,8},{20,12},{24,16},{28,20},{1,25},{... | collective-permute-start | bytes 196616 | tf_op jit(solution)/shard_map/ppermute | solution.py:422
  45.6 3.7 %collective-permute-start.8 = (bf16[32,1024]{1,0:T(8,128)(2,1)S(1)}, bf16[32,1024]{1,0:T(8,128)(2,1)S(1)}, u32[]{:S(2)}, u32[]{:S(2)}) collective-permute-start(bf16[32,1024]{1,0:T(8,128)(2,1)S(1)} %get-tuple-element.14), channel_id=1, source_target_pairs={{0,28},{4,0},{8,4},{12,8},{16,12},{20,16},{24,20},{28,24},{1,29},{... | collective-permute-start | bytes 196616 | tf_op jit(solution)/shard_map/ppermute | solution.py:422
  45.6 4.6 %collective-permute-start.7 = (bf16[32,1024]{1,0:T(8,128)(2,1)S(1)}, bf16[32,1024]{1,0:T(8,128)(2,1)S(1)}, u32[]{:S(2)}, u32[]{:S(2)}) collective-permute-start(bf16[32,1024]{1,0:T(8,128)(2,1)S(1)} %get-tuple-element.14), channel_id=1, source_target_pairs={{0,4},{4,8},{8,12},{12,16},{16,20},{20,24},{24,28},{28,0},{1,5},{5... | collective-permute-start | bytes 196616 | tf_op jit(solution)/shard_map/ppermute | solution.py:422
  46.2 5.5 %collective-permute-start.6 = (bf16[32,1024]{1,0:T(8,128)(2,1)S(1)}, bf16[32,1024]{1,0:T(8,128)(2,1)S(1)}, u32[]{:S(2)}, u32[]{:S(2)}) collective-permute-start(bf16[32,1024]{1,0:T(8,128)(2,1)S(1)} %get-tuple-element.14), channel_id=1, source_target_pairs={{0,8},{4,12},{8,16},{12,20},{16,24},{20,28},{24,0},{28,4},{1,9},{5... | collective-permute-start | bytes 196616 | tf_op jit(solution)/shard_map/ppermute | solution.py:422

commit v6 on v5

--- a/solution.py
+++ b/solution.py
@@ -57,16 +57,13 @@
     return values
 
 
-def beam_kernel(chunks, own, width, scale, first_ref, *refs):
+def beam_kernel(chunks, own, width, scale, more, first_ref, *refs):
     x_refs, refs = refs[:chunks], refs[chunks:]
-    first = scale is None
-    if first:
-        acc, xs, tabs = refs[0], refs[1], refs[2:3]
-    else:
-        acc_in, out_ref, xs, tabs = refs[0], refs[1], refs[2], refs[3:5]
-        acc, works, sem = refs[5], refs[6:8], refs[8]
-        fetch = pltpu.make_async_copy(acc_in, acc, sem)
-        fetch.start()
+    final = scale is not None
+    before = refs[0] if more else None
+    out_ref, xs, *refs = refs[more:]
+    tabs, refs = refs[: min(chunks, 2)], refs[min(chunks, 2) :]
+    works, acc = refs[:2], (refs[2:] if final else [out_ref])
     parts = width // LANES
     for g in range(chunks):
         for b in range(own + EXTRA):
@@ -207,9 +204,8 @@
         tables(tabs[0], 0, 2 * i + 1)
 
     some(parts // 2, both)
-    if not first:
+    if final:
         out_ref[...] = jnp.zeros_like(out_ref)
-        fetch.wait()
     for g in range(chunks):
         last = g == chunks - 1
         tab = tabs[g % len(tabs)]
@@ -219,19 +215,21 @@
             for j in range(batch):
                 f = q * batch + j
                 got = beams(tab, f)
-                if first:
-                    acc[f] = got
-                elif last:
-                    add_power(acc[f] + got, works[j % 2])
+                if g > 0:
+                    got = acc[0][f] + got
+                elif more:
+                    got = before[f] + got
+                if final and last:
+                    add_power(got, works[j % 2])
                 else:
-                    acc[f] = acc[f] + got
+                    acc[0][f] = got
                 while not last and done * batch < (j + 1) * each:
                     tables(tabs[(g + 1) % 2], g + 1, q * each + done)
                     done += 1
 
         some(own // batch, block)
 
-    if first:
+    if not final:
         return
     src = lax.broadcasted_iota(jnp.int32, (CZ, CZ), 0)
     dst = lax.broadcasted_iota(jnp.int32, (CZ, CZ), 1)
@@ -245,35 +243,29 @@
         )
 
 
-def beams_call(chunks, own, width, scale, *args):
-    first = scale is None
+def beams_call(own, width, scale, at, blocks, held):
     vmem = pl.BlockSpec(memory_space=pltpu.VMEM)
     smem = pl.BlockSpec(memory_space=pltpu.SMEM)
+    chunks, more, final = len(blocks), int(held is not None), scale is not None
     rows = CX * CY
     acc = (own, rows, 2 * CZ)
-    tab = pltpu.VMEM((width // LANES, ENTRIES * own, LANES), jnp.float32)
     scratch = [pltpu.VMEM((chunks, width // LANES, 2 * (own + EXTRA), LANES), jnp.float32)]
-    if first:
-        scratch += [tab]
-        out = jax.ShapeDtypeStruct(acc, jnp.float32)
-        specs = [smem] + [vmem] * chunks
-    else:
-        scratch += [tab] * 2 + [pltpu.VMEM(acc, jnp.float32)]
-        scratch += [pltpu.VMEM((2, rows, CZ), jnp.float32)] * 2 + [pltpu.SemaphoreType.DMA]
-        out = jax.ShapeDtypeStruct((CX, CY * CZ), jnp.float32)
-        specs = [smem] + [vmem] * chunks + [pl.BlockSpec(memory_space=pl.ANY)]
+    scratch += [pltpu.VMEM((width // LANES, ENTRIES * own, LANES), jnp.float32)] * min(chunks, 2)
+    if final:
+        scratch += [pltpu.VMEM((2, rows, CZ), jnp.float32)] * 2
+        scratch += [pltpu.VMEM(acc, jnp.float32)] * (chunks > 1)
     return pl.pallas_call(
-        functools.partial(beam_kernel, chunks, own, width, scale),
-        out_shape=out,
-        in_specs=specs,
+        functools.partial(beam_kernel, chunks, own, width, scale, more),
+        out_shape=jax.ShapeDtypeStruct((CX, CY * CZ) if final else acc, jnp.float32),
+        in_specs=[smem] + [vmem] * (chunks + more),
         out_specs=vmem,
         scratch_shapes=scratch,
-        compiler_params=pltpu.CompilerParams(vmem_limit_bytes=48 * 1024 * 1024),
+        compiler_params=pltpu.CompilerParams(vmem_limit_bytes=36 * 1024 * 1024),
         cost_estimate=pl.CostEstimate(
             flops=2 * chunks * own * rows * 2 * CZ * width, bytes_accessed=8 * own * rows * CZ, transcendentals=0
         ),
-        name="beams_own" if first else "beams_rest",
-    )(*args)
+        name="beams_last" if final else "beams_more" if more else "beams_own",
+    )(at, *blocks, *([held] if more else []))
 
 
 def split(v):
@@ -281,42 +273,56 @@
     return high, (v - high.astype(jnp.float32)).astype(jnp.bfloat16)
 
 
-def dot3(a, b):
-    dot = functools.partial(jnp.dot, preferred_element_type=jnp.float32)
-    return dot(a[0], b[0]) + (dot(a[0], b[1]) + dot(a[1], b[0]))
-
-
-def deblur_kernel(count, at_ref, taps_ref, own_ref, m2, m1, p1, p2, stacked_ref, est_ref):
-    rows, cols = 5 * CX, CY * CZ
-    start = (at_ref[0] - 2) * CX
-
-    def inside(first, length):
-        x = lax.broadcasted_iota(jnp.int32, (length, cols), 0) + (start + first)
-        return (x >= 0) & (x < count * CX)
-
-    stacked = own_ref[...] * (1.0 / SMALLER) + BACKGROUND
-    halo = [ref[...].astype(jnp.float32) * (1.0 / SMALLER) + BACKGROUND for ref in (m2, m1, p1, p2)]
-    observed = jnp.concatenate(halo[:2] + [stacked] + halo[2:], axis=0)
-    observed = jnp.where(inside(0, rows), observed, 0.0)
-    for y in range(CY):
-        stacked_ref[:, y, :] = stacked[:, y * CZ : (y + 1) * CZ]
-
-    def band(axis, offset):
+def blur_rows():
+    reach = 2 * ITERS * HALF
+    sizes = [CX + 2 * (reach - HALF * blur) for blur in range(2 * ITERS + 1)]
+    return list(zip(sizes[:-1], sizes[1:]))
+
+
+def band_kernel(taps_ref, *refs):
+    def band(axis, offset, low):
         total = jnp.zeros(offset.shape, jnp.float32)
         for tap in range(TAPS):
             total = jnp.where(offset == tap, taps_ref[axis, tap], total)
-        return total
-
-    i = lax.broadcasted_iota(jnp.int32, (rows - 2 * HALF, rows), 0)
-    p = lax.broadcasted_iota(jnp.int32, (rows - 2 * HALF, rows), 1)
-    band_x = split(band(0, p - i))
-    w = lax.broadcasted_iota(jnp.int32, (2 * CZ, 2 * CZ), 0)
-    k = lax.broadcasted_iota(jnp.int32, (2 * CZ, 2 * CZ), 1)
-    band_z = split(band(2, jnp.where(w // CZ == k // CZ, w - k + HALF, -1)))
-
-    def blur(v):
+        high = total.astype(jnp.bfloat16).astype(jnp.float32)
+        return jnp.where(low, total - high, high).astype(jnp.bfloat16)
+
+    for (n, m), ref in zip(blur_rows(), refs):
+        i = lax.broadcasted_iota(jnp.int32, (m, 3 * n), 0)
+        p = lax.broadcasted_iota(jnp.int32, (m, 3 * n), 1)
+        low = (p >= n) & (p < 2 * n)
+        p = jnp.where(low, p - n, jnp.where(p >= 2 * n, p - 2 * n, p))
+        ref[...] = band(0, p - i, low)
+    pair = 2 * CZ
+    w = lax.broadcasted_iota(jnp.int32, (pair, pair), 0)
+    k = lax.broadcasted_iota(jnp.int32, (pair, pair), 1)
+    offset = jnp.where(w // CZ == k // CZ, w - k + HALF, -1)
+    for part in range(3):
+        refs[-1][part * pair : (part + 1) * pair, :] = band(2, offset, part == 1)
+
+
+def deblur_kernel(count, at_ref, taps_ref, own_ref, m2, m1, p1, p2, *refs):
+    bands, (stacked_ref, est_ref) = refs[:-2], refs[-2:]
+    rows = 5 * CX
+    start = (at_ref[0] - 2) * CX
+    x = lax.broadcasted_iota(jnp.int32, (rows, CZ), 0) + start
+    inside = jnp.where((x >= 0) & (x < count * CX), 1.0, 0.0)
+    outside = jnp.concatenate([1.0 - inside] * CY, axis=1)
+    inside = jnp.concatenate([inside] * CY, axis=1)
+
+    stacked = own_ref[...] * (1.0 / SMALLER) + BACKGROUND
+    halo = [ref[...].astype(jnp.float32) * (1.0 / SMALLER) + BACKGROUND for ref in (m2, m1, p1, p2)]
+    observed = jnp.concatenate(halo[:2] + [stacked] + halo[2:], axis=0) * inside
+    for y in range(CY):
+        stacked_ref[:, y, :] = stacked[:, y * CZ : (y + 1) * CZ]
+
+    def blur(v, which):
         n = v.shape[0]
-        x = dot3(tuple(part[: n - 2 * HALF, :n] for part in band_x), split(v))
+        m = n - 2 * HALF
+        high, low = split(v)
+        x = jnp.dot(
+            bands[which][...], jnp.concatenate([high, high, low], axis=0), preferred_element_type=jnp.float32
+        )
         along = []
         for j in range(CY):
             total = None
@@ -324,19 +330,20 @@
                 term = taps_ref[1, q - j + HALF] * x[:, q * CZ : (q + 1) * CZ]
                 total = term if total is None else total + term
             along.append(total)
-        out = []
-        for j in range(0, CY, 2):
-            out.append(dot3(split(jnp.concatenate(along[j : j + 2], axis=1)), band_z))
-        return jnp.concatenate(out, axis=1)
+        pairs = [jnp.concatenate(along[j : j + 2], axis=1) for j in range(0, CY, 2)]
+        high, low = split(jnp.concatenate(pairs, axis=0))
+        z = jnp.dot(
+            jnp.concatenate([high, high, low], axis=1), bands[-1][...], preferred_element_type=jnp.float32
+        )
+        return jnp.concatenate([z[k * m : (k + 1) * m] for k in range(CY // 2)], axis=1)
 
     est, first = observed, 0
-    for _ in range(ITERS):
-        blurred = blur(est)
+    for sweep in range(ITERS):
+        blurred = blur(est, 2 * sweep)
         first += HALF
         n = blurred.shape[0]
-        ok = inside(first, n)
-        ratio = jnp.where(ok, observed[first : first + n] / jnp.where(ok, blurred, 1.0), 0.0)
-        change = blur(ratio)
+        ratio = observed[first : first + n] / (blurred + outside[first : first + n])
+        change = blur(ratio, 2 * sweep + 1)
         first += HALF
         est = est[2 * HALF : -2 * HALF] * change
     for y in range(CY):
@@ -378,10 +385,9 @@
     return [(i, i ^ k if size & (size - 1) == 0 else (i + k) % size) for i in range(size)]
 
 
-def summed_over(value, axis, size):
+def summed_over(half, axis, size):
     if size & (size - 1):
-        return lax.psum(value, axis)
-    half = lax.optimization_barrier(value.astype(jnp.float16))
+        return lax.psum(half.astype(jnp.float32), axis)
     terms = [half] + [lax.ppermute(half, axis, moves(k, size)) for k in range(1, size)]
     terms = [term.astype(jnp.float32) for term in terms]
     while len(terms) > 1:
@@ -406,16 +412,30 @@
             pltpu.VMEM((3, width), jnp.bfloat16),
             pltpu.SemaphoreType.DMA((groups + 2,)),
         ],
+        compiler_params=pltpu.CompilerParams(vmem_limit_bytes=4 * 1024 * 1024),
         name="bundles",
     )(me.reshape(1), spectra, lag_samples, slowness[0])
     blocks = [blocks[0]] + [lax.ppermute(blocks[k], "sta", moves(k, groups)) for k in range(1, groups)]
 
     at = (me * own).reshape(1)
     scale = SMALLER / (freqs * width * groups)
-    held = beams_call(1, own, width, None, at, blocks[0])
-    local = beams_call(groups - 1, own, width, scale, at, *blocks[1:], held)
-
-    total = summed_over(local, "sta", groups)
+    held = beams_call(own, width, None, at, blocks[:1], None)
+    if groups > 2:
+        held = beams_call(own, width, None, at, blocks[1:2], held)
+    local = beams_call(own, width, scale, at, blocks[2 if groups > 2 else 1 :], held)
+
+    half, taps = lax.optimization_barrier((local.astype(jnp.float16), spread_taps))
+    shapes = [(m, 3 * n) for n, m in blur_rows()] + [(6 * CZ, 2 * CZ)]
+    bands = pl.pallas_call(
+        band_kernel,
+        out_shape=[jax.ShapeDtypeStruct(shape, jnp.bfloat16) for shape in shapes],
+        in_specs=[smem],
+        out_specs=[vmem] * len(shapes),
+        compiler_params=pltpu.CompilerParams(vmem_limit_bytes=8 * 1024 * 1024),
+        cost_estimate=pl.CostEstimate(flops=10**7, bytes_accessed=2 * 10**6, transcendentals=0),
+        name="bands",
+    )(taps)
+    total = summed_over(half, "sta", groups)
     narrow = total.astype(jnp.bfloat16)
     halo = []
     for shift in (2, 1, -1, -2):
@@ -424,11 +444,11 @@
     stacked, deblurred = pl.pallas_call(
         functools.partial(deblur_kernel, tiles),
         out_shape=(tile, tile),
-        in_specs=[smem, smem] + [vmem] * 5,
+        in_specs=[smem, smem] + [vmem] * (5 + len(bands)),
         out_specs=(vmem, vmem),
-        compiler_params=pltpu.CompilerParams(vmem_limit_bytes=48 * 1024 * 1024),
+        compiler_params=pltpu.CompilerParams(vmem_limit_bytes=36 * 1024 * 1024),
         name="deblur",
-    )(lax.axis_index("grid").astype(jnp.int32).reshape(1), spread_taps, total, *halo)
+    )(lax.axis_index("grid").astype(jnp.int32).reshape(1), spread_taps, total, *halo, *bands)
     return stacked[None], deblurred[None]
 
 

time: 59.2 us -> 58.9 us (level)
  waiting for transfers between devices: 13.2 us -> 10.9 us
  local copies, waits for them, and re-layouts: 0.91 us -> 2.39 us
  Pallas kernels: 30.9 us -> 31.5 us
    ppermute x4, waiting for transfers between devices: 5.48 us -> 3 us  [per_device(): lax.ppermute(narrow, 'grid', [(i, (i + shift) % tiles) for i in range(til...]
    pallas_call x2 -> x4, Pallas kernels: 21.7 us -> 24.2 us  [the longest x3 21.7 us: beams_call(): pl.pallas_call(functools.partial(beam_kernel, chunks, own, width, scale,...]
    unnamed x4 -> x8, local copies, waits for them, and re-layouts: 0.91 us -> 2.39 us
    pallas_call x1, Pallas kernels: 1.88 us -> 0.6 us  [per_device(): pl.pallas_call(functools.partial(bundle_kernel, groups, own), out_shape=[...]
    ppermute x3, waiting for transfers between devices: 3.94 us -> 4.63 us  [summed_over(): lax.ppermute(half, axis, moves(k, size))]
    pallas_call x1, Pallas kernels: 7.32 us -> 6.71 us  [per_device(): pl.pallas_call(functools.partial(deblur_kernel, tiles), out_shape=(tile,...]
  transfers between devices with their start and end apart: 10 -> 10, of which waited for: 7 -> 7; matrix products, arithmetic and copies ran while one was open for 0% -> 0% of each run, Pallas kernels for 8% -> 21%
where the time goes in v6:
time: 58.9 us; the launch traced here: 58.7 us
  Pallas kernels  31.5 us (53%)
  starting transfers between devices  13.1 us (22%)
  waiting for transfers between devices  10.9 us (19%)
  local copies, waits for them, and re-layouts  2.39 us (4%)
  between operations  0.72 us (1%)
    pallas_call x3, Pallas kernels, beams_call(): pl.pallas_call(functools.partial(beam_kernel, chunks, own, width, scale,...  21.7 us
    pallas_call x1, Pallas kernels, per_device(): pl.pallas_call(functools.partial(deblur_kernel, tiles), out_shape=(tile,...  6.71 us
    ppermute x3, starting transfers between devices, per_device(): lax.ppermute(blocks[k], 'sta', moves(k, groups))  5.68 us
    ppermute x3, waiting for transfers between devices, summed_over(): lax.ppermute(half, axis, moves(k, size))  4.63 us
    ppermute x3, starting transfers between devices, summed_over(): lax.ppermute(half, axis, moves(k, size))  4.45 us
    ppermute x3, waiting for transfers between devices, per_device(): lax.ppermute(blocks[k], 'sta', moves(k, groups))  3.27 us
    ppermute x4, starting transfers between devices, per_device(): lax.ppermute(narrow, 'grid', [(i, (i + shift) % tiles) for i in range(til...  3 us
    ppermute x4, waiting for transfers between devices, per_device(): lax.ppermute(narrow, 'grid', [(i, (i + shift) % tiles) for i in range(til...  3 us
  transfers between devices with their start and end apart: 10, of which 7 were waited for; matrix products, arithmetic and copies ran while one was open for 0% of the time, Pallas kernels for 21%

profile of v6, /device:TPU:0, one launch (start us, length us, event | category | flops | bytes accessed | tf_op | source)
XLA Modules:
  0.0 58.7 jit_solution(9861162667919129338)
XLA Ops:
  0.6 1.0 %copy-done = bf16[64,2,1536]{2,1,0:T(2,128)(2,1)S(1)} copy-done((bf16[64,2,1536]{2,1,0:T(2,128)(2,1)S(1)}, bf16[64,2,1536]{2,1,0:T(2,128)(2,1)}, u32[]{:S(2)}) %copy-start) | copy-done | bytes 393240
  1.6 0.7 %copy-done.1 = bf16[1,3,1536]{2,1,0:T(4,128)(2,1)S(1)} copy-done((bf16[1,3,1536]{2,1,0:T(4,128)(2,1)S(1)}, bf16[1,3,1536]{2,1,0:T(4,128)(2,1)}, u32[]{:S(2)}) %copy-start.1) | copy-done | bytes 9240
  2.3 0.7 %copy-done.2 = s32[1,1536]{1,0:T(1,128)S(1)} copy-done((s32[1,1536]{1,0:T(1,128)S(1)}, s32[1,1536]{1,0:T(1,128)}, u32[]{:S(2)}) %copy-start.2) | copy-done | bytes 6168
  3.0 0.6 %bundles.1 = (bf16[19,2,1536]{2,1,0:T(2,128)(2,1)S(1)}, bf16[19,2,1536]{2,1,0:T(2,128)(2,1)S(1)}, bf16[19,2,1536]{2,1,0:T(2,128)(2,1)S(1)}, bf16[19,2,1536]{2,1,0:T(2,128)(2,1)S(1)}) custom-call(s32[1]{0:T(128)} %bitcast.2.me_ref, bf16[64,2,1536]{2,1,0:T(2,128)(2,1)S(1)} %copy-done, s32[1,1536]{1,0:T(1,128)S(1)} %copy-done.2, bf16[3,1536]{1,0:T(4,128)(2,1)S(1)} %bitcast.6), custom_call_target="tpu_custom_call" | custom-call | tf_op jit(solution)/shard_map/bundles/pallas_call | solution.py:405
  3.6 4.1 %collective-permute-start = (bf16[19,2,1536]{2,1,0:T(2,128)(2,1)S(1)}, bf16[19,2,1536]{2,1,0:T(2,128)(2,1)S(1)}, u32[]{:S(2)}, u32[]{:S(2)}) collective-permute-start(bf16[19,2,1536]{2,1,0:T(2,128)(2,1)S(1)} %get-tuple-element.19), channel_id=1, source_target_pairs={{0,2},{1,3},{2,0},{3,1},{4,6},{5,7},{6,4},{7,5},{8,10},{9,11},{10,... | collective-permute-start | bytes 350216 | tf_op jit(solution)/shard_map/ppermute | solution.py:418
  7.7 1.3 %collective-permute-start.1 = (bf16[19,2,1536]{2,1,0:T(2,128)(2,1)S(1)}, bf16[19,2,1536]{2,1,0:T(2,128)(2,1)S(1)}, u32[]{:S(2)}, u32[]{:S(2)}) collective-permute-start(bf16[19,2,1536]{2,1,0:T(2,128)(2,1)S(1)} %get-tuple-element.20), channel_id=1, source_target_pairs={{0,3},{1,2},{2,1},{3,0},{4,7},{5,6},{6,5},{7,4},{8,11},{9,10},{10,... | collective-permute-start | bytes 350216 | tf_op jit(solution)/shard_map/ppermute | solution.py:418
  9.1 0.2 collective-permute-start.2
  9.3 4.7 %beams_own.1.refs_1_ = f32[16,256,256]{2,1,0:T(8,128)S(1)} custom-call(s32[1]{0:T(128)} %bitcast.1.first_ref, bf16[19,2,1536]{2,1,0:T(2,128)(2,1)S(1)} %get-tuple-element.22.refs_0_), custom_call_target="tpu_custom_call" | custom-call | flops 3221225472 | bytes 4194304 | tf_op jit(solution)/shard_map/beams_own/pallas_call | solution.py:257
  14.1 3.3 %collective-permute-done.2.refs_0_ = bf16[19,2,1536]{2,1,0:T(2,128)(2,1)S(1)} collective-permute-done((bf16[19,2,1536]{2,1,0:T(2,128)(2,1)S(1)}, bf16[19,2,1536]{2,1,0:T(2,128)(2,1)S(1)}, u32[]{:S(2)}, u32[]{:S(2)}) %collective-permute-start.2) | collective-permute-done | bytes 116768 | tf_op jit(solution)/shard_map/ppermute | solution.py:418
  17.3 4.9 %beams_more.1.refs_2_ = f32[16,256,256]{2,1,0:T(8,128)S(1)} custom-call(s32[1]{0:T(128)} %bitcast.1.first_ref, bf16[19,2,1536]{2,1,0:T(2,128)(2,1)S(1)} %collective-permute-done.2.refs_0_, f32[16,256,256]{2,1,0:T(8,128)S(1)} %beams_own.1.refs_1_), custom_call_target="tpu_custom_call" | custom-call | flops 3221225472 | bytes 4194304 | tf_op jit(solution)/shard_map/beams_more/pallas_call | solution.py:257
  22.2 0.0 copy-start.3
  22.3 12.1 %beams_last.1 = f32[32,1024]{1,0:T(8,128)S(1)} custom-call(s32[1]{0:T(128)} %bitcast.1.first_ref, bf16[19,2,1536]{2,1,0:T(2,128)(2,1)S(1)} %collective-permute-done.refs_0_, bf16[19,2,1536]{2,1,0:T(2,128)(2,1)S(1)} %collective-permute-done.1.refs_1_, f32[16,256,256]{2,1,0:T(8,128)S(1)} %beams_more.1.refs_2_), custom_call_target="tpu_custom_call" | custom-call | flops 6442450944 | bytes 4194304 | tf_op jit(solution)/shard_map/beams_last/pallas_call | solution.py:257
  34.4 3.6 %collective-permute-start.5 = (f16[32,1024]{1,0:T(8,128)(2,1)S(1)}, f16[32,1024]{1,0:T(8,128)(2,1)S(1)}, u32[]{:S(2)}, u32[]{:S(2)}) collective-permute-start(f16[32,1024]{1,0:T(8,128)(2,1)S(1)} %convert_element_type.18), channel_id=1, source_target_pairs={{0,3},{1,2},{2,1},{3,0},{4,7},{5,6},{6,5},{7,4},{8,11},{9,10},{10,... | collective-permute-start | bytes 196616 | tf_op jit(solution)/shard_map/ppermute | solution.py:391
  37.9 0.9 %collective-permute-start.3 = (f16[32,1024]{1,0:T(8,128)(2,1)S(1)}, f16[32,1024]{1,0:T(8,128)(2,1)S(1)}, u32[]{:S(2)}, u32[]{:S(2)}) collective-permute-start(f16[32,1024]{1,0:T(8,128)(2,1)S(1)} %convert_element_type.18), channel_id=1, source_target_pairs={{0,1},{1,0},{2,3},{3,2},{4,5},{5,4},{6,7},{7,6},{8,9},{9,8},{10,11... | collective-permute-start | bytes 196616 | tf_op jit(solution)/shard_map/ppermute | solution.py:391
  38.8 1.8 %collective-permute-done.5 = f16[32,1024]{1,0:T(8,128)(2,1)S(1)} collective-permute-done((f16[32,1024]{1,0:T(8,128)(2,1)S(1)}, f16[32,1024]{1,0:T(8,128)(2,1)S(1)}, u32[]{:S(2)}, u32[]{:S(2)}) %collective-permute-start.5) | collective-permute-done | bytes 65568 | tf_op jit(solution)/shard_map/ppermute | solution.py:391
  40.6 2.6 %collective-permute-done.4 = f16[32,1024]{1,0:T(8,128)(2,1)S(1)} collective-permute-done((f16[32,1024]{1,0:T(8,128)(2,1)S(1)}, f16[32,1024]{1,0:T(8,128)(2,1)S(1)}, u32[]{:S(2)}, u32[]{:S(2)}) %collective-permute-start.4) | collective-permute-done | bytes 65568 | tf_op jit(solution)/shard_map/ppermute | solution.py:391
  43.2 0.3 collective-permute-done.3
  43.5 2.5 %collective-permute-start.9 = (bf16[32,1024]{1,0:T(8,128)(2,1)S(1)}, bf16[32,1024]{1,0:T(8,128)(2,1)S(1)}, u32[]{:S(2)}, u32[]{:S(2)}) collective-permute-start(bf16[32,1024]{1,0:T(8,128)(2,1)S(1)} %get-tuple-element.36), channel_id=1, source_target_pairs={{0,24},{4,28},{8,0},{12,4},{16,8},{20,12},{24,16},{28,20},{1,25},{... | collective-permute-start | bytes 196616 | tf_op jit(solution)/shard_map/ppermute | solution.py:442
  46.0 0.5 collective-permute-start.7
  46.5 2.5 %bands.1 = (bf16[144,480]{1,0:T(8,128)(2,1)S(1)}, bf16[128,432]{1,0:T(8,128)(2,1)S(1)}, bf16[112,384]{1,0:T(8,128)(2,1)S(1)}, bf16[96,336]{1,0:T(8,128)(2,1)S(1)...) custom-call(f32[3,17]{1,0:T(4,128)S(1)} %copy-done.3), custom_call_target="tpu_custom_call" | custom-call | flops 10000000 | bytes 2000000 | tf_op jit(solution)/shard_map/bands/pallas_call | solution.py:429
  49.0 0.7 %collective-permute-done.8.p1 = bf16[32,1024]{1,0:T(8,128)(2,1)S(1)} collective-permute-done((bf16[32,1024]{1,0:T(8,128)(2,1)S(1)}, bf16[32,1024]{1,0:T(8,128)(2,1)S(1)}, u32[]{:S(2)}, u32[]{:S(2)}) %collective-permute-start.8) | collective-permute-done | bytes 65568 | tf_op jit(solution)/shard_map/ppermute | solution.py:442
  49.7 0.9 %collective-permute-done.7.m1 = bf16[32,1024]{1,0:T(8,128)(2,1)S(1)} collective-permute-done((bf16[32,1024]{1,0:T(8,128)(2,1)S(1)}, bf16[32,1024]{1,0:T(8,128)(2,1)S(1)}, u32[]{:S(2)}, u32[]{:S(2)}) %collective-permute-start.7) | collective-permute-done | bytes 65568 | tf_op jit(solution)/shard_map/ppermute | solution.py:442
  50.6 1.4 %collective-permute-done.6.m2 = bf16[32,1024]{1,0:T(8,128)(2,1)S(1)} collective-permute-done((bf16[32,1024]{1,0:T(8,128)(2,1)S(1)}, bf16[32,1024]{1,0:T(8,128)(2,1)S(1)}, u32[]{:S(2)}, u32[]{:S(2)}) %collective-permute-start.6) | collective-permute-done | bytes 65568 | tf_op jit(solution)/shard_map/ppermute | solution.py:442
  52.0 6.7 %deblur.1 = (f32[32,8,128]{2,1,0:T(8,128)}, f32[32,8,128]{2,1,0:T(8,128)}) custom-call(s32[1]{0:T(128)} %bitcast.at_ref, f32[3,17]{1,0:T(4,128)S(1)} %copy-done.3, f32[32,1024]{1,0:T(8,128)S(1)} %get-tuple-element.37.own_ref, bf16[32,1024]{1,0:T(8,128)(2,1)S(1)} %collective-permute-done.6.m2, bf16[32,1024]{1,0:T(8,128)(2,1)S(1)} %collective-permute-done.7.m1, ...), custom_call_target="tpu_custom_call" | custom-call | tf_op jit(solution)/shard_map/deblur/pallas_call | solution.py:444
  (12 shorter events, 0.1 us)
Async XLA Ops:
  0.6 1.0 %copy-start = (bf16[64,2,1536]{2,1,0:T(2,128)(2,1)S(1)}, bf16[64,2,1536]{2,1,0:T(2,128)(2,1)}, u32[]{:S(2)}) copy-start(bf16[64,2,1536]{2,1,0:T(2,128)(2,1)} %spectra_ref.1) | copy-start | bytes 1179652
  1.6 0.7 %copy-start.1 = (bf16[1,3,1536]{2,1,0:T(4,128)(2,1)S(1)}, bf16[1,3,1536]{2,1,0:T(4,128)(2,1)}, u32[]{:S(2)}) copy-start(bf16[1,3,1536]{2,1,0:T(4,128)(2,1)} %param.6) | copy-start | bytes 27652
  2.3 0.7 %copy-start.2 = (s32[1,1536]{1,0:T(1,128)S(1)}, s32[1,1536]{1,0:T(1,128)}, u32[]{:S(2)}) copy-start(s32[1,1536]{1,0:T(1,128)} %lag_ref.1) | copy-start | bytes 18436
  3.6 18.6 %collective-permute-start = (bf16[19,2,1536]{2,1,0:T(2,128)(2,1)S(1)}, bf16[19,2,1536]{2,1,0:T(2,128)(2,1)S(1)}, u32[]{:S(2)}, u32[]{:S(2)}) collective-permute-start(bf16[19,2,1536]{2,1,0:T(2,128)(2,1)S(1)} %get-tuple-element.19), channel_id=1, source_target_pairs={{0,2},{1,3},{2,0},{3,1},{4,6},{5,7},{6,4},{7,5},{8,10},{9,11},{10,... | collective-permute-start | bytes 350216 | tf_op jit(solution)/shard_map/ppermute | solution.py:418
  7.7 14.5 %collective-permute-start.1 = (bf16[19,2,1536]{2,1,0:T(2,128)(2,1)S(1)}, bf16[19,2,1536]{2,1,0:T(2,128)(2,1)S(1)}, u32[]{:S(2)}, u32[]{:S(2)}) collective-permute-start(bf16[19,2,1536]{2,1,0:T(2,128)(2,1)S(1)} %get-tuple-element.20), channel_id=1, source_target_pairs={{0,3},{1,2},{2,1},{3,0},{4,7},{5,6},{6,5},{7,4},{8,11},{9,10},{10,... | collective-permute-start | bytes 350216 | tf_op jit(solution)/shard_map/ppermute | solution.py:418
  9.1 8.2 %collective-permute-start.2 = (bf16[19,2,1536]{2,1,0:T(2,128)(2,1)S(1)}, bf16[19,2,1536]{2,1,0:T(2,128)(2,1)S(1)}, u32[]{:S(2)}, u32[]{:S(2)}) collective-permute-start(bf16[19,2,1536]{2,1,0:T(2,128)(2,1)S(1)} %get-tuple-element.21), channel_id=1, source_target_pairs={{0,1},{1,0},{2,3},{3,2},{4,5},{5,4},{6,7},{7,6},{8,9},{9,8},{10,11... | collective-permute-start | bytes 350216 | tf_op jit(solution)/shard_map/ppermute | solution.py:418
  22.2 24.3 %copy-start.3 = (f32[3,17]{1,0:T(4,128)S(1)}, f32[3,17]{1,0:T(4,128)}, u32[]{:S(2)}) copy-start(f32[3,17]{1,0:T(4,128)} %taps_ref.2) | copy-start | bytes 616
  34.4 6.2 %collective-permute-start.5 = (f16[32,1024]{1,0:T(8,128)(2,1)S(1)}, f16[32,1024]{1,0:T(8,128)(2,1)S(1)}, u32[]{:S(2)}, u32[]{:S(2)}) collective-permute-start(f16[32,1024]{1,0:T(8,128)(2,1)S(1)} %convert_element_type.18), channel_id=1, source_target_pairs={{0,3},{1,2},{2,1},{3,0},{4,7},{5,6},{6,5},{7,4},{8,11},{9,10},{10,... | collective-permute-start | bytes 196616 | tf_op jit(solution)/shard_map/ppermute | solution.py:391
  37.9 5.2 %collective-permute-start.4 = (f16[32,1024]{1,0:T(8,128)(2,1)S(1)}, f16[32,1024]{1,0:T(8,128)(2,1)S(1)}, u32[]{:S(2)}, u32[]{:S(2)}) collective-permute-start(f16[32,1024]{1,0:T(8,128)(2,1)S(1)} %convert_element_type.18), channel_id=1, source_target_pairs={{0,2},{1,3},{2,0},{3,1},{4,6},{5,7},{6,4},{7,5},{8,10},{9,11},{10,... | collective-permute-start | bytes 196616 | tf_op jit(solution)/shard_map/ppermute | solution.py:391
  37.9 5.5 %collective-permute-start.3 = (f16[32,1024]{1,0:T(8,128)(2,1)S(1)}, f16[32,1024]{1,0:T(8,128)(2,1)S(1)}, u32[]{:S(2)}, u32[]{:S(2)}) collective-permute-start(f16[32,1024]{1,0:T(8,128)(2,1)S(1)} %convert_element_type.18), channel_id=1, source_target_pairs={{0,1},{1,0},{2,3},{3,2},{4,5},{5,4},{6,7},{7,6},{8,9},{9,8},{10,11... | collective-permute-start | bytes 196616 | tf_op jit(solution)/shard_map/ppermute | solution.py:391
  43.5 5.5 %collective-permute-start.9 = (bf16[32,1024]{1,0:T(8,128)(2,1)S(1)}, bf16[32,1024]{1,0:T(8,128)(2,1)S(1)}, u32[]{:S(2)}, u32[]{:S(2)}) collective-permute-start(bf16[32,1024]{1,0:T(8,128)(2,1)S(1)} %get-tuple-element.36), channel_id=1, source_target_pairs={{0,24},{4,28},{8,0},{12,4},{16,8},{20,12},{24,16},{28,20},{1,25},{... | collective-permute-start | bytes 196616 | tf_op jit(solution)/shard_map/ppermute | solution.py:442
  46.0 3.7 %collective-permute-start.8 = (bf16[32,1024]{1,0:T(8,128)(2,1)S(1)}, bf16[32,1024]{1,0:T(8,128)(2,1)S(1)}, u32[]{:S(2)}, u32[]{:S(2)}) collective-permute-start(bf16[32,1024]{1,0:T(8,128)(2,1)S(1)} %get-tuple-element.36), channel_id=1, source_target_pairs={{0,28},{4,0},{8,4},{12,8},{16,12},{20,16},{24,20},{28,24},{1,29},{... | collective-permute-start | bytes 196616 | tf_op jit(solution)/shard_map/ppermute | solution.py:442
  46.0 4.6 %collective-permute-start.7 = (bf16[32,1024]{1,0:T(8,128)(2,1)S(1)}, bf16[32,1024]{1,0:T(8,128)(2,1)S(1)}, u32[]{:S(2)}, u32[]{:S(2)}) collective-permute-start(bf16[32,1024]{1,0:T(8,128)(2,1)S(1)} %get-tuple-element.36), channel_id=1, source_target_pairs={{0,4},{4,8},{8,12},{12,16},{16,20},{20,24},{24,28},{28,0},{1,5},{5... | collective-permute-start | bytes 196616 | tf_op jit(solution)/shard_map/ppermute | solution.py:442
  46.5 5.5 %collective-permute-start.6 = (bf16[32,1024]{1,0:T(8,128)(2,1)S(1)}, bf16[32,1024]{1,0:T(8,128)(2,1)S(1)}, u32[]{:S(2)}, u32[]{:S(2)}) collective-permute-start(bf16[32,1024]{1,0:T(8,128)(2,1)S(1)} %get-tuple-element.36), channel_id=1, source_target_pairs={{0,8},{4,12},{8,16},{12,20},{16,24},{20,28},{24,0},{28,4},{1,9},{5... | collective-permute-start | bytes 196616 | tf_op jit(solution)/shard_map/ppermute | solution.py:442

commit v7 on v6

--- a/solution.py
+++ b/solution.py
@@ -77,6 +77,7 @@
     away = jnp.where(row < 4, 3 - row, row - 4)
     near = (away & 1) != 0, away >= 2
     sign = jnp.where(row < 4, -1.0, 1.0)
+    lower = lax.broadcasted_iota(jnp.int32, (CX * CY, CZ), 1) < CZ // 2
 
     def tables(tab, g, i):
         def common(which):
@@ -170,13 +171,11 @@
                 c, s = spread(DE + 2 * k, i), spread(DE + 2 * k + 1, i)
                 turned.append((c * mc - s * ms, s * mc + c * ms))
             ar, ai = pack(turned[0][0], turned[1][0]), pack(turned[0][1], turned[1][1])
-            real, imag = [], []
-            for h in range(4):
-                br, bi = narrow(DB + h, i), narrow(DB + 4 + h, i)
-                rr, ii, ri, ir = ar * br, ai * bi, ar * bi, ai * br
-                real += [rr + ii, rr - ii]
-                imag += [ri - ir, ri + ir]
-            right.append(jnp.concatenate(real + imag, axis=0))
+            na = -ai
+            br = [narrow(DB + h, i) for h in range(4)]
+            bi = [narrow(DB + 4 + h, i) for h in range(4)]
+            rows = [ar * b for b in br] + [ar * b for b in bi] + [ai * b for b in bi] + [na * b for b in br]
+            right.append(jnp.concatenate(rows, axis=0))
         return lax.dot_general(
             jnp.concatenate(left, axis=1),
             jnp.concatenate(right, axis=1),
@@ -185,7 +184,10 @@
         )
 
     def add_power(got, work):
-        values = [(got[8 * x : 8 * x + 8, :CZ], got[8 * x : 8 * x + 8, CZ:]) for x in range(CX)]
+        above, below = got[:, :CZ] + got[:, CZ:], got[:, :CZ] - got[:, CZ:]
+        reals = jnp.where(lower, above, pltpu.roll(below, CZ // 2, 1))
+        imags = jnp.where(lower, pltpu.roll(above, CZ // 2, 1), below)
+        values = [(reals[8 * x : 8 * x + 8], imags[8 * x : 8 * x + 8]) for x in range(CX)]
         for x, (re, im) in enumerate(butterfly(values, 5)):
             work[0, 8 * x : 8 * x + 8, :] = re
             work[1, 8 * x : 8 * x + 8, :] = im
@@ -234,7 +236,7 @@
     src = lax.broadcasted_iota(jnp.int32, (CZ, CZ), 0)
     dst = lax.broadcasted_iota(jnp.int32, (CZ, CZ), 1)
     low = src % 16
-    place = (src // 32) * 32 + jnp.where((src // 16) % 2 == 0, 16 + low, 15 - low)
+    place = (src // 16) % 4 * 32 + jnp.where(src < CZ // 2, 16 + low, 15 - low)
     swap = jnp.where(place == dst, scale, 0.0)
     for y in range(CY):
         lanes = slice(y * CZ, (y + 1) * CZ)
@@ -262,7 +264,7 @@
         scratch_shapes=scratch,
         compiler_params=pltpu.CompilerParams(vmem_limit_bytes=36 * 1024 * 1024),
         cost_estimate=pl.CostEstimate(
-            flops=2 * chunks * own * rows * 2 * CZ * width, bytes_accessed=8 * own * rows * CZ, transcendentals=0
+            flops=(8 if more else 0) * chunks * own * rows * CZ * width, bytes_accessed=8, transcendentals=0
         ),
         name="beams_last" if final else "beams_more" if more else "beams_own",
     )(at, *blocks, *([held] if more else []))
@@ -351,7 +353,7 @@
 
 
 def bundle_kernel(groups, own, me_ref, spectra_ref, lag_ref, slow_ref, *refs):
-    outs, (lag_in, slow_in, sems) = refs[:groups], refs[groups:]
+    outs, (lag_in, slow_in, extra, sems) = refs[:groups], refs[groups:]
     small = [
         pltpu.make_async_copy(lag_ref, lag_in, sems.at[groups]),
         pltpu.make_async_copy(slow_ref, slow_in, sems.at[groups + 1]),
@@ -374,9 +376,11 @@
         slow[:2],
         jnp.concatenate([slow[2:], slow[2:]], axis=0),
     ]
+    for at, pair in enumerate(pairs):
+        extra[at] = pair.astype(jnp.bfloat16)
     for k in range(groups):
-        for extra, pair in enumerate(pairs):
-            outs[k][own + extra] = pair.astype(jnp.bfloat16)
+        slices.append(pltpu.make_async_copy(extra, outs[k].at[pl.ds(own, EXTRA)], sems.at[groups + 2 + k]))
+        slices[-1].start()
     for copy in slices:
         copy.wait()
 
@@ -406,13 +410,14 @@
         functools.partial(bundle_kernel, groups, own),
         out_shape=[jax.ShapeDtypeStruct((own + EXTRA, 2, width), jnp.bfloat16)] * groups,
         in_specs=[smem] + [hbm] * 3,
-        out_specs=[vmem] * groups,
+        out_specs=[hbm] * groups,
         scratch_shapes=[
             pltpu.VMEM((1, width), jnp.int32),
             pltpu.VMEM((3, width), jnp.bfloat16),
-            pltpu.SemaphoreType.DMA((groups + 2,)),
+            pltpu.VMEM((EXTRA, 2, width), jnp.bfloat16),
+            pltpu.SemaphoreType.DMA((2 * groups + 2,)),
         ],
-        compiler_params=pltpu.CompilerParams(vmem_limit_bytes=4 * 1024 * 1024),
+        compiler_params=pltpu.CompilerParams(vmem_limit_bytes=60 * 1024 * 1024),
         name="bundles",
     )(me.reshape(1), spectra, lag_samples, slowness[0])
     blocks = [blocks[0]] + [lax.ppermute(blocks[k], "sta", moves(k, groups)) for k in range(1, groups)]

time: 58.9 us -> 66.6 us (1.13)
  Pallas kernels: 31.5 us -> 43.6 us
  waiting for transfers between devices: 10.9 us -> 7.75 us
  local copies, waits for them, and re-layouts: 2.39 us -> 0.91 us
    pallas_call x1, Pallas kernels: 0.6 us -> 13.1 us  [per_device(): pl.pallas_call(functools.partial(bundle_kernel, groups, own), out_shape=[...]
    ppermute x3, waiting for transfers between devices: 3.27 us -> 0.01 us  [per_device(): lax.ppermute(blocks[k], 'sta', moves(k, groups))]
    unnamed x8 -> x4, local copies, waits for them, and re-layouts: 2.39 us -> 0.91 us
  transfers between devices with their start and end apart: 10 -> 10, of which waited for: 7 -> 6; matrix products, arithmetic and copies ran while one was open for 0% -> 0% of each run, Pallas kernels for 21% -> 18%
where the time goes in v7:
time: 66.6 us; the launch traced here: 66.3 us
  Pallas kernels  43.6 us (65%)
  starting transfers between devices  13.3 us (20%)
  waiting for transfers between devices  7.75 us (12%)
  local copies, waits for them, and re-layouts  0.91 us (1%)
  between operations  0.72 us (1%)
    pallas_call x3, Pallas kernels, beams_call(): pl.pallas_call(functools.partial(beam_kernel, chunks, own, width, scale,...  21.3 us
    pallas_call x1, Pallas kernels, per_device(): pl.pallas_call(functools.partial(bundle_kernel, groups, own), out_shape=[...  13.1 us
    pallas_call x1, Pallas kernels, per_device(): pl.pallas_call(functools.partial(deblur_kernel, tiles), out_shape=(tile,...  6.71 us
    ppermute x3, starting transfers between devices, per_device(): lax.ppermute(blocks[k], 'sta', moves(k, groups))  5.68 us
    ppermute x3, waiting for transfers between devices, summed_over(): lax.ppermute(half, axis, moves(k, size))  4.75 us
    ppermute x3, starting transfers between devices, summed_over(): lax.ppermute(half, axis, moves(k, size))  4.52 us
    ppermute x4, starting transfers between devices, per_device(): lax.ppermute(narrow, 'grid', [(i, (i + shift) % tiles) for i in range(til...  3.09 us
    ppermute x4, waiting for transfers between devices, per_device(): lax.ppermute(narrow, 'grid', [(i, (i + shift) % tiles) for i in range(til...  3 us
  transfers between devices with their start and end apart: 10, of which 6 were waited for; matrix products, arithmetic and copies ran while one was open for 0% of the time, Pallas kernels for 18%

profile of v7, /device:TPU:0, one launch (start us, length us, event | category | flops | bytes accessed | tf_op | source)
XLA Modules:
  0.0 66.3 jit_solution(6485715761327617451)
XLA Ops:
  0.6 13.1 %bundles.1 = (bf16[19,2,1536]{2,1,0:T(2,128)(2,1)}, bf16[19,2,1536]{2,1,0:T(2,128)(2,1)}, bf16[19,2,1536]{2,1,0:T(2,128)(2,1)}, bf16[19,2,1536]{2,1,0:T(2,128)(2,1)}) custom-call(s32[1]{0:T(128)} %bitcast.2.me_ref, bf16[64,2,1536]{2,1,0:T(2,128)(2,1)} %spectra_ref.1, s32[1,1536]{1,0:T(1,128)} %lag_ref.1, bf16[3,1536]{1,0:T(4,128)(2,1)} %bitcast.6), custom_call_target="tpu_custom_call" | custom-call | tf_op jit(solution)/shard_map/bundles/pallas_call | solution.py:409
  13.8 3.1 %collective-permute-start.2 = (bf16[19,2,1536]{2,1,0:T(2,128)(2,1)}, bf16[19,2,1536]{2,1,0:T(2,128)(2,1)S(1)}, u32[]{:S(2)}, u32[]{:S(2)}) collective-permute-start(bf16[19,2,1536]{2,1,0:T(2,128)(2,1)} %get-tuple-element.21), channel_id=1, source_target_pairs={{0,1},{1,0},{2,3},{3,2},{4,5},{5,4},{6,7},{7,6},{8,9},{9,8},{10,11... | collective-permute-start | bytes 350216 | tf_op jit(solution)/shard_map/ppermute | solution.py:423
  16.8 2.6 %collective-permute-start = (bf16[19,2,1536]{2,1,0:T(2,128)(2,1)}, bf16[19,2,1536]{2,1,0:T(2,128)(2,1)S(1)}, u32[]{:S(2)}, u32[]{:S(2)}) collective-permute-start(bf16[19,2,1536]{2,1,0:T(2,128)(2,1)} %get-tuple-element.19), channel_id=1, source_target_pairs={{0,2},{1,3},{2,0},{3,1},{4,6},{5,7},{6,4},{7,5},{8,10},{9,11},{10,... | collective-permute-start | bytes 350216 | tf_op jit(solution)/shard_map/ppermute | solution.py:423
  19.4 0.0 collective-permute-start.1
  19.4 0.9 %copy-done = bf16[19,2,1536]{2,1,0:T(2,128)(2,1)S(1)} copy-done((bf16[19,2,1536]{2,1,0:T(2,128)(2,1)S(1)}, bf16[19,2,1536]{2,1,0:T(2,128)(2,1)}, u32[]{:S(2)}) %copy-start) | copy-done | bytes 116760
  20.3 4.5 %beams_own.1.refs_1_ = f32[16,256,256]{2,1,0:T(8,128)S(1)} custom-call(s32[1]{0:T(128)} %bitcast.1.first_ref, bf16[19,2,1536]{2,1,0:T(2,128)(2,1)S(1)} %copy-done), custom_call_target="tpu_custom_call" | custom-call | bytes 8 | tf_op jit(solution)/shard_map/beams_own/pallas_call | solution.py:259
  24.9 4.7 %beams_more.1.refs_2_ = f32[16,256,256]{2,1,0:T(8,128)S(1)} custom-call(s32[1]{0:T(128)} %bitcast.1.first_ref, bf16[19,2,1536]{2,1,0:T(2,128)(2,1)S(1)} %collective-permute-done.2.refs_0_, f32[16,256,256]{2,1,0:T(8,128)S(1)} %beams_own.1.refs_1_), custom_call_target="tpu_custom_call" | custom-call | flops 6442450944 | bytes 8 | tf_op jit(solution)/shard_map/beams_more/pallas_call | solution.py:259
  29.6 0.0 copy-start.1
  29.6 0.0 collective-permute-done.refs_0_
  29.6 12.1 %beams_last.1 = f32[32,1024]{1,0:T(8,128)S(1)} custom-call(s32[1]{0:T(128)} %bitcast.1.first_ref, bf16[19,2,1536]{2,1,0:T(2,128)(2,1)S(1)} %collective-permute-done.refs_0_, bf16[19,2,1536]{2,1,0:T(2,128)(2,1)S(1)} %collective-permute-done.1.refs_1_, f32[16,256,256]{2,1,0:T(8,128)S(1)} %beams_more.1.refs_2_), custom_call_target="tpu_custom_call" | custom-call | flops 12884901888 | bytes 8 | tf_op jit(solution)/shard_map/beams_last/pallas_call | solution.py:259
  41.7 3.9 %collective-permute-start.5 = (f16[32,1024]{1,0:T(8,128)(2,1)S(1)}, f16[32,1024]{1,0:T(8,128)(2,1)S(1)}, u32[]{:S(2)}, u32[]{:S(2)}) collective-permute-start(f16[32,1024]{1,0:T(8,128)(2,1)S(1)} %convert_element_type.18), channel_id=1, source_target_pairs={{0,3},{1,2},{2,1},{3,0},{4,7},{5,6},{6,5},{7,4},{8,11},{9,10},{10,... | collective-permute-start | bytes 196616 | tf_op jit(solution)/shard_map/ppermute | solution.py:395
  45.6 0.6 collective-permute-start.3
  46.3 1.7 %collective-permute-done.5 = f16[32,1024]{1,0:T(8,128)(2,1)S(1)} collective-permute-done((f16[32,1024]{1,0:T(8,128)(2,1)S(1)}, f16[32,1024]{1,0:T(8,128)(2,1)S(1)}, u32[]{:S(2)}, u32[]{:S(2)}) %collective-permute-start.5) | collective-permute-done | bytes 65568 | tf_op jit(solution)/shard_map/ppermute | solution.py:395
  48.0 2.9 %collective-permute-done.4 = f16[32,1024]{1,0:T(8,128)(2,1)S(1)} collective-permute-done((f16[32,1024]{1,0:T(8,128)(2,1)S(1)}, f16[32,1024]{1,0:T(8,128)(2,1)S(1)}, u32[]{:S(2)}, u32[]{:S(2)}) %collective-permute-start.4) | collective-permute-done | bytes 65568 | tf_op jit(solution)/shard_map/ppermute | solution.py:395
  50.8 0.2 collective-permute-done.3
  51.0 2.6 %collective-permute-start.9 = (bf16[32,1024]{1,0:T(8,128)(2,1)S(1)}, bf16[32,1024]{1,0:T(8,128)(2,1)S(1)}, u32[]{:S(2)}, u32[]{:S(2)}) collective-permute-start(bf16[32,1024]{1,0:T(8,128)(2,1)S(1)} %get-tuple-element.36), channel_id=1, source_target_pairs={{0,24},{4,28},{8,0},{12,4},{16,8},{20,12},{24,16},{28,20},{1,25},{... | collective-permute-start | bytes 196616 | tf_op jit(solution)/shard_map/ppermute | solution.py:447
  53.6 0.0 collective-permute-start.8
  53.6 0.5 collective-permute-start.7
  54.1 0.0 collective-permute-start.6
  54.1 2.5 %bands.1 = (bf16[144,480]{1,0:T(8,128)(2,1)S(1)}, bf16[128,432]{1,0:T(8,128)(2,1)S(1)}, bf16[112,384]{1,0:T(8,128)(2,1)S(1)}, bf16[96,336]{1,0:T(8,128)(2,1)S(1)...) custom-call(f32[3,17]{1,0:T(4,128)S(1)} %copy-done.1), custom_call_target="tpu_custom_call" | custom-call | flops 10000000 | bytes 2000000 | tf_op jit(solution)/shard_map/bands/pallas_call | solution.py:434
  56.6 0.7 %collective-permute-done.8.p1 = bf16[32,1024]{1,0:T(8,128)(2,1)S(1)} collective-permute-done((bf16[32,1024]{1,0:T(8,128)(2,1)S(1)}, bf16[32,1024]{1,0:T(8,128)(2,1)S(1)}, u32[]{:S(2)}, u32[]{:S(2)}) %collective-permute-start.8) | collective-permute-done | bytes 65568 | tf_op jit(solution)/shard_map/ppermute | solution.py:447
  57.3 0.9 %collective-permute-done.7.m1 = bf16[32,1024]{1,0:T(8,128)(2,1)S(1)} collective-permute-done((bf16[32,1024]{1,0:T(8,128)(2,1)S(1)}, bf16[32,1024]{1,0:T(8,128)(2,1)S(1)}, u32[]{:S(2)}, u32[]{:S(2)}) %collective-permute-start.7) | collective-permute-done | bytes 65568 | tf_op jit(solution)/shard_map/ppermute | solution.py:447
  58.2 1.4 %collective-permute-done.6.m2 = bf16[32,1024]{1,0:T(8,128)(2,1)S(1)} collective-permute-done((bf16[32,1024]{1,0:T(8,128)(2,1)S(1)}, bf16[32,1024]{1,0:T(8,128)(2,1)S(1)}, u32[]{:S(2)}, u32[]{:S(2)}) %collective-permute-start.6) | collective-permute-done | bytes 65568 | tf_op jit(solution)/shard_map/ppermute | solution.py:447
  59.6 6.7 %deblur.1 = (f32[32,8,128]{2,1,0:T(8,128)}, f32[32,8,128]{2,1,0:T(8,128)}) custom-call(s32[1]{0:T(128)} %bitcast.at_ref, f32[3,17]{1,0:T(4,128)S(1)} %copy-done.1, f32[32,1024]{1,0:T(8,128)S(1)} %get-tuple-element.37.own_ref, bf16[32,1024]{1,0:T(8,128)(2,1)S(1)} %collective-permute-done.6.m2, bf16[32,1024]{1,0:T(8,128)(2,1)S(1)} %collective-permute-done.7.m1, ...), custom_call_target="tpu_custom_call" | custom-call | tf_op jit(solution)/shard_map/deblur/pallas_call | solution.py:449
  (8 shorter events, 0.1 us)
Async XLA Ops:
  13.8 11.1 %collective-permute-start.2 = (bf16[19,2,1536]{2,1,0:T(2,128)(2,1)}, bf16[19,2,1536]{2,1,0:T(2,128)(2,1)S(1)}, u32[]{:S(2)}, u32[]{:S(2)}) collective-permute-start(bf16[19,2,1536]{2,1,0:T(2,128)(2,1)} %get-tuple-element.21), channel_id=1, source_target_pairs={{0,1},{1,0},{2,3},{3,2},{4,5},{5,4},{6,7},{7,6},{8,9},{9,8},{10,11... | collective-permute-start | bytes 350216 | tf_op jit(solution)/shard_map/ppermute | solution.py:423
  16.8 12.8 %collective-permute-start = (bf16[19,2,1536]{2,1,0:T(2,128)(2,1)}, bf16[19,2,1536]{2,1,0:T(2,128)(2,1)S(1)}, u32[]{:S(2)}, u32[]{:S(2)}) collective-permute-start(bf16[19,2,1536]{2,1,0:T(2,128)(2,1)} %get-tuple-element.19), channel_id=1, source_target_pairs={{0,2},{1,3},{2,0},{3,1},{4,6},{5,7},{6,4},{7,5},{8,10},{9,11},{10,... | collective-permute-start | bytes 350216 | tf_op jit(solution)/shard_map/ppermute | solution.py:423
  19.4 10.2 %collective-permute-start.1 = (bf16[19,2,1536]{2,1,0:T(2,128)(2,1)}, bf16[19,2,1536]{2,1,0:T(2,128)(2,1)S(1)}, u32[]{:S(2)}, u32[]{:S(2)}) collective-permute-start(bf16[19,2,1536]{2,1,0:T(2,128)(2,1)} %get-tuple-element.20), channel_id=1, source_target_pairs={{0,3},{1,2},{2,1},{3,0},{4,7},{5,6},{6,5},{7,4},{8,11},{9,10},{10,... | collective-permute-start | bytes 350216 | tf_op jit(solution)/shard_map/ppermute | solution.py:423
  19.4 0.9 %copy-start = (bf16[19,2,1536]{2,1,0:T(2,128)(2,1)S(1)}, bf16[19,2,1536]{2,1,0:T(2,128)(2,1)}, u32[]{:S(2)}) copy-start(bf16[19,2,1536]{2,1,0:T(2,128)(2,1)} %get-tuple-element.22.refs_0_) | copy-start | bytes 350212
  29.6 24.5 %copy-start.1 = (f32[3,17]{1,0:T(4,128)S(1)}, f32[3,17]{1,0:T(4,128)}, u32[]{:S(2)}) copy-start(f32[3,17]{1,0:T(4,128)} %taps_ref.2) | copy-start | bytes 616
  41.7 6.2 %collective-permute-start.5 = (f16[32,1024]{1,0:T(8,128)(2,1)S(1)}, f16[32,1024]{1,0:T(8,128)(2,1)S(1)}, u32[]{:S(2)}, u32[]{:S(2)}) collective-permute-start(f16[32,1024]{1,0:T(8,128)(2,1)S(1)} %convert_element_type.18), channel_id=1, source_target_pairs={{0,3},{1,2},{2,1},{3,0},{4,7},{5,6},{6,5},{7,4},{8,11},{9,10},{10,... | collective-permute-start | bytes 196616 | tf_op jit(solution)/shard_map/ppermute | solution.py:395
  45.6 5.2 %collective-permute-start.4 = (f16[32,1024]{1,0:T(8,128)(2,1)S(1)}, f16[32,1024]{1,0:T(8,128)(2,1)S(1)}, u32[]{:S(2)}, u32[]{:S(2)}) collective-permute-start(f16[32,1024]{1,0:T(8,128)(2,1)S(1)} %convert_element_type.18), channel_id=1, source_target_pairs={{0,2},{1,3},{2,0},{3,1},{4,6},{5,7},{6,4},{7,5},{8,10},{9,11},{10,... | collective-permute-start | bytes 196616 | tf_op jit(solution)/shard_map/ppermute | solution.py:395
  45.6 5.4 %collective-permute-start.3 = (f16[32,1024]{1,0:T(8,128)(2,1)S(1)}, f16[32,1024]{1,0:T(8,128)(2,1)S(1)}, u32[]{:S(2)}, u32[]{:S(2)}) collective-permute-start(f16[32,1024]{1,0:T(8,128)(2,1)S(1)} %convert_element_type.18), channel_id=1, source_target_pairs={{0,1},{1,0},{2,3},{3,2},{4,5},{5,4},{6,7},{7,6},{8,9},{9,8},{10,11... | collective-permute-start | bytes 196616 | tf_op jit(solution)/shard_map/ppermute | solution.py:395
  51.0 5.6 %collective-permute-start.9 = (bf16[32,1024]{1,0:T(8,128)(2,1)S(1)}, bf16[32,1024]{1,0:T(8,128)(2,1)S(1)}, u32[]{:S(2)}, u32[]{:S(2)}) collective-permute-start(bf16[32,1024]{1,0:T(8,128)(2,1)S(1)} %get-tuple-element.36), channel_id=1, source_target_pairs={{0,24},{4,28},{8,0},{12,4},{16,8},{20,12},{24,16},{28,20},{1,25},{... | collective-permute-start | bytes 196616 | tf_op jit(solution)/shard_map/ppermute | solution.py:447
  53.6 3.7 %collective-permute-start.8 = (bf16[32,1024]{1,0:T(8,128)(2,1)S(1)}, bf16[32,1024]{1,0:T(8,128)(2,1)S(1)}, u32[]{:S(2)}, u32[]{:S(2)}) collective-permute-start(bf16[32,1024]{1,0:T(8,128)(2,1)S(1)} %get-tuple-element.36), channel_id=1, source_target_pairs={{0,28},{4,0},{8,4},{12,8},{16,12},{20,16},{24,20},{28,24},{1,29},{... | collective-permute-start | bytes 196616 | tf_op jit(solution)/shard_map/ppermute | solution.py:447
  53.6 4.6 %collective-permute-start.7 = (bf16[32,1024]{1,0:T(8,128)(2,1)S(1)}, bf16[32,1024]{1,0:T(8,128)(2,1)S(1)}, u32[]{:S(2)}, u32[]{:S(2)}) collective-permute-start(bf16[32,1024]{1,0:T(8,128)(2,1)S(1)} %get-tuple-element.36), channel_id=1, source_target_pairs={{0,4},{4,8},{8,12},{12,16},{16,20},{20,24},{24,28},{28,0},{1,5},{5... | collective-permute-start | bytes 196616 | tf_op jit(solution)/shard_map/ppermute | solution.py:447
  54.1 5.5 %collective-permute-start.6 = (bf16[32,1024]{1,0:T(8,128)(2,1)S(1)}, bf16[32,1024]{1,0:T(8,128)(2,1)S(1)}, u32[]{:S(2)}, u32[]{:S(2)}) collective-permute-start(bf16[32,1024]{1,0:T(8,128)(2,1)S(1)} %get-tuple-element.36), channel_id=1, source_target_pairs={{0,8},{4,12},{8,16},{12,20},{16,24},{20,28},{24,0},{28,4},{1,9},{5... | collective-permute-start | bytes 196616 | tf_op jit(solution)/shard_map/ppermute | solution.py:447

commit v8 on v7

--- a/solution.py
+++ b/solution.py
@@ -195,7 +195,7 @@
         for y, (re, im) in enumerate(butterfly(values, 3)):
             out_ref[:, y * CZ : (y + 1) * CZ] += re * re + im * im
 
-    batch = 8
+    batch = 8 if final else own
     each = parts * batch // own
 
     def some(n, fn):
@@ -238,11 +238,12 @@
     low = src % 16
     place = (src // 16) % 4 * 32 + jnp.where(src < CZ // 2, 16 + low, 15 - low)
     swap = jnp.where(place == dst, scale, 0.0)
+    blocks = [out_ref[:, y * CZ : (y + 1) * CZ] for y in range(CY)]
+    natural = jnp.dot(
+        jnp.concatenate(blocks, axis=0), swap, precision=lax.Precision.HIGHEST, preferred_element_type=jnp.float32
+    )
     for y in range(CY):
-        lanes = slice(y * CZ, (y + 1) * CZ)
-        out_ref[:, lanes] = jnp.dot(
-            out_ref[:, lanes], swap, precision=lax.Precision.HIGHEST, preferred_element_type=jnp.float32
-        )
+        out_ref[:, y * CZ : (y + 1) * CZ] = natural[y * CX : (y + 1) * CX]
 
 
 def beams_call(own, width, scale, at, blocks, held):
@@ -353,7 +354,7 @@
 
 
 def bundle_kernel(groups, own, me_ref, spectra_ref, lag_ref, slow_ref, *refs):
-    outs, (lag_in, slow_in, extra, sems) = refs[:groups], refs[groups:]
+    outs, (lag_in, slow_in, sems) = refs[:groups], refs[groups:]
     small = [
         pltpu.make_async_copy(lag_ref, lag_in, sems.at[groups]),
         pltpu.make_async_copy(slow_ref, slow_in, sems.at[groups + 1]),
@@ -376,11 +377,9 @@
         slow[:2],
         jnp.concatenate([slow[2:], slow[2:]], axis=0),
     ]
-    for at, pair in enumerate(pairs):
-        extra[at] = pair.astype(jnp.bfloat16)
     for k in range(groups):
-        slices.append(pltpu.make_async_copy(extra, outs[k].at[pl.ds(own, EXTRA)], sems.at[groups + 2 + k]))
-        slices[-1].start()
+        for extra, pair in enumerate(pairs):
+            outs[k][own + extra] = pair.astype(jnp.bfloat16)
     for copy in slices:
         copy.wait()
 
@@ -410,12 +409,11 @@
         functools.partial(bundle_kernel, groups, own),
         out_shape=[jax.ShapeDtypeStruct((own + EXTRA, 2, width), jnp.bfloat16)] * groups,
         in_specs=[smem] + [hbm] * 3,
-        out_specs=[hbm] * groups,
+        out_specs=[vmem] * groups,
         scratch_shapes=[
             pltpu.VMEM((1, width), jnp.int32),
             pltpu.VMEM((3, width), jnp.bfloat16),
-            pltpu.VMEM((EXTRA, 2, width), jnp.bfloat16),
-            pltpu.SemaphoreType.DMA((2 * groups + 2,)),
+            pltpu.SemaphoreType.DMA((groups + 2,)),
         ],
         compiler_params=pltpu.CompilerParams(vmem_limit_bytes=60 * 1024 * 1024),
         name="bundles",

time: 66.6 us -> 54.5 us (0.82)
  Pallas kernels: 43.6 us -> 31.8 us
    pallas_call x1, Pallas kernels: 13.1 us -> 1.88 us  [per_device(): pl.pallas_call(functools.partial(bundle_kernel, groups, own), out_shape=[...]
  transfers between devices with their start and end apart: 10 -> 10, of which waited for: 6 -> 5; matrix products, arithmetic and copies ran while one was open for 0% -> 0% of each run, Pallas kernels for 18% -> 21%
where the time goes in v8:
time: 54.5 us; the launch traced here: 54.3 us
  Pallas kernels  31.8 us (58%)
  starting transfers between devices  13.3 us (24%)
  waiting for transfers between devices  7.55 us (14%)
  local copies, waits for them, and re-layouts  0.91 us (2%)
  between operations  0.73 us (1%)
    pallas_call x3, Pallas kernels, beams_call(): pl.pallas_call(functools.partial(beam_kernel, chunks, own, width, scale,...  20.8 us
    pallas_call x1, Pallas kernels, per_device(): pl.pallas_call(functools.partial(deblur_kernel, tiles), out_shape=(tile,...  6.71 us
    ppermute x3, starting transfers between devices, per_device(): lax.ppermute(blocks[k], 'sta', moves(k, groups))  5.68 us
    ppermute x3, waiting for transfers between devices, summed_over(): lax.ppermute(half, axis, moves(k, size))  4.54 us
    ppermute x3, starting transfers between devices, summed_over(): lax.ppermute(half, axis, moves(k, size))  4.52 us
    ppermute x4, starting transfers between devices, per_device(): lax.ppermute(narrow, 'grid', [(i, (i + shift) % tiles) for i in range(til...  3.05 us
    ppermute x4, waiting for transfers between devices, per_device(): lax.ppermute(narrow, 'grid', [(i, (i + shift) % tiles) for i in range(til...  3 us
    pallas_call x1, Pallas kernels, per_device(): pl.pallas_call(band_kernel, out_shape=[jax.ShapeDtypeStruct(shape, jnp.bf...  2.47 us
  transfers between devices with their start and end apart: 10, of which 5 were waited for; matrix products, arithmetic and copies ran while one was open for 0% of the time, Pallas kernels for 21%

profile of v8, /device:TPU:0, one launch (start us, length us, event | category | flops | bytes accessed | tf_op | source)
XLA Modules:
  0.0 54.3 jit_solution(7342918082187269989)
XLA Ops:
  0.6 1.9 %bundles.1 = (bf16[19,2,1536]{2,1,0:T(2,128)(2,1)}, bf16[19,2,1536]{2,1,0:T(2,128)(2,1)}, bf16[19,2,1536]{2,1,0:T(2,128)(2,1)}, bf16[19,2,1536]{2,1,0:T(2,128)(2,1)}) custom-call(s32[1]{0:T(128)} %bitcast.2.me_ref, bf16[64,2,1536]{2,1,0:T(2,128)(2,1)} %spectra_ref.1, s32[1,1536]{1,0:T(1,128)} %lag_ref.1, bf16[3,1536]{1,0:T(4,128)(2,1)} %bitcast.6), custom_call_target="tpu_custom_call" | custom-call | tf_op jit(solution)/shard_map/bundles/pallas_call | solution.py:408
  2.5 3.1 %collective-permute-start.2 = (bf16[19,2,1536]{2,1,0:T(2,128)(2,1)}, bf16[19,2,1536]{2,1,0:T(2,128)(2,1)S(1)}, u32[]{:S(2)}, u32[]{:S(2)}) collective-permute-start(bf16[19,2,1536]{2,1,0:T(2,128)(2,1)} %get-tuple-element.21), channel_id=1, source_target_pairs={{0,1},{1,0},{2,3},{3,2},{4,5},{5,4},{6,7},{7,6},{8,9},{9,8},{10,11... | collective-permute-start | bytes 350216 | tf_op jit(solution)/shard_map/ppermute | solution.py:421
  5.6 2.6 %collective-permute-start = (bf16[19,2,1536]{2,1,0:T(2,128)(2,1)}, bf16[19,2,1536]{2,1,0:T(2,128)(2,1)S(1)}, u32[]{:S(2)}, u32[]{:S(2)}) collective-permute-start(bf16[19,2,1536]{2,1,0:T(2,128)(2,1)} %get-tuple-element.19), channel_id=1, source_target_pairs={{0,2},{1,3},{2,0},{3,1},{4,6},{5,7},{6,4},{7,5},{8,10},{9,11},{10,... | collective-permute-start | bytes 350216 | tf_op jit(solution)/shard_map/ppermute | solution.py:421
  8.2 0.0 collective-permute-start.1
  8.2 0.9 %copy-done = bf16[19,2,1536]{2,1,0:T(2,128)(2,1)S(1)} copy-done((bf16[19,2,1536]{2,1,0:T(2,128)(2,1)S(1)}, bf16[19,2,1536]{2,1,0:T(2,128)(2,1)}, u32[]{:S(2)}) %copy-start) | copy-done | bytes 116760
  9.1 4.3 %beams_own.1.refs_1_ = f32[16,256,256]{2,1,0:T(8,128)S(1)} custom-call(s32[1]{0:T(128)} %bitcast.1.first_ref, bf16[19,2,1536]{2,1,0:T(2,128)(2,1)S(1)} %copy-done), custom_call_target="tpu_custom_call" | custom-call | bytes 8 | tf_op jit(solution)/shard_map/beams_own/pallas_call | solution.py:260
  13.4 4.5 %beams_more.1.refs_2_ = f32[16,256,256]{2,1,0:T(8,128)S(1)} custom-call(s32[1]{0:T(128)} %bitcast.1.first_ref, bf16[19,2,1536]{2,1,0:T(2,128)(2,1)S(1)} %collective-permute-done.2.refs_0_, f32[16,256,256]{2,1,0:T(8,128)S(1)} %beams_own.1.refs_1_), custom_call_target="tpu_custom_call" | custom-call | flops 6442450944 | bytes 8 | tf_op jit(solution)/shard_map/beams_more/pallas_call | solution.py:260
  17.9 0.0 copy-start.1
  17.9 0.0 collective-permute-done.1.refs_1_
  17.9 12.0 %beams_last.1 = f32[32,1024]{1,0:T(8,128)S(1)} custom-call(s32[1]{0:T(128)} %bitcast.1.first_ref, bf16[19,2,1536]{2,1,0:T(2,128)(2,1)S(1)} %collective-permute-done.refs_0_, bf16[19,2,1536]{2,1,0:T(2,128)(2,1)S(1)} %collective-permute-done.1.refs_1_, f32[16,256,256]{2,1,0:T(8,128)S(1)} %beams_more.1.refs_2_), custom_call_target="tpu_custom_call" | custom-call | flops 12884901888 | bytes 8 | tf_op jit(solution)/shard_map/beams_last/pallas_call | solution.py:260
  29.9 3.9 %collective-permute-start.5 = (f16[32,1024]{1,0:T(8,128)(2,1)S(1)}, f16[32,1024]{1,0:T(8,128)(2,1)S(1)}, u32[]{:S(2)}, u32[]{:S(2)}) collective-permute-start(f16[32,1024]{1,0:T(8,128)(2,1)S(1)} %convert_element_type.18), channel_id=1, source_target_pairs={{0,3},{1,2},{2,1},{3,0},{4,7},{5,6},{6,5},{7,4},{8,11},{9,10},{10,... | collective-permute-start | bytes 196616 | tf_op jit(solution)/shard_map/ppermute | solution.py:394
  33.8 0.6 %collective-permute-start.3 = (f16[32,1024]{1,0:T(8,128)(2,1)S(1)}, f16[32,1024]{1,0:T(8,128)(2,1)S(1)}, u32[]{:S(2)}, u32[]{:S(2)}) collective-permute-start(f16[32,1024]{1,0:T(8,128)(2,1)S(1)} %convert_element_type.18), channel_id=1, source_target_pairs={{0,1},{1,0},{2,3},{3,2},{4,5},{5,4},{6,7},{7,6},{8,9},{9,8},{10,11... | collective-permute-start | bytes 196616 | tf_op jit(solution)/shard_map/ppermute | solution.py:394
  34.5 1.8 %collective-permute-done.5 = f16[32,1024]{1,0:T(8,128)(2,1)S(1)} collective-permute-done((f16[32,1024]{1,0:T(8,128)(2,1)S(1)}, f16[32,1024]{1,0:T(8,128)(2,1)S(1)}, u32[]{:S(2)}, u32[]{:S(2)}) %collective-permute-start.5) | collective-permute-done | bytes 65568 | tf_op jit(solution)/shard_map/ppermute | solution.py:394
  36.3 2.7 %collective-permute-done.4 = f16[32,1024]{1,0:T(8,128)(2,1)S(1)} collective-permute-done((f16[32,1024]{1,0:T(8,128)(2,1)S(1)}, f16[32,1024]{1,0:T(8,128)(2,1)S(1)}, u32[]{:S(2)}, u32[]{:S(2)}) %collective-permute-start.4) | collective-permute-done | bytes 65568 | tf_op jit(solution)/shard_map/ppermute | solution.py:394
  39.0 0.0 collective-permute-done.3
  39.1 2.5 %collective-permute-start.9 = (bf16[32,1024]{1,0:T(8,128)(2,1)S(1)}, bf16[32,1024]{1,0:T(8,128)(2,1)S(1)}, u32[]{:S(2)}, u32[]{:S(2)}) collective-permute-start(bf16[32,1024]{1,0:T(8,128)(2,1)S(1)} %get-tuple-element.36), channel_id=1, source_target_pairs={{0,24},{4,28},{8,0},{12,4},{16,8},{20,12},{24,16},{28,20},{1,25},{... | collective-permute-start | bytes 196616 | tf_op jit(solution)/shard_map/ppermute | solution.py:445
  41.6 0.0 collective-permute-start.8
  41.6 0.5 collective-permute-start.7
  42.1 2.5 %bands.1 = (bf16[144,480]{1,0:T(8,128)(2,1)S(1)}, bf16[128,432]{1,0:T(8,128)(2,1)S(1)}, bf16[112,384]{1,0:T(8,128)(2,1)S(1)}, bf16[96,336]{1,0:T(8,128)(2,1)S(1)...) custom-call(f32[3,17]{1,0:T(4,128)S(1)} %copy-done.1), custom_call_target="tpu_custom_call" | custom-call | flops 10000000 | bytes 2000000 | tf_op jit(solution)/shard_map/bands/pallas_call | solution.py:432
  44.6 0.0 collective-permute-done.9.p2
  44.6 0.7 %collective-permute-done.8.p1 = bf16[32,1024]{1,0:T(8,128)(2,1)S(1)} collective-permute-done((bf16[32,1024]{1,0:T(8,128)(2,1)S(1)}, bf16[32,1024]{1,0:T(8,128)(2,1)S(1)}, u32[]{:S(2)}, u32[]{:S(2)}) %collective-permute-start.8) | collective-permute-done | bytes 65568 | tf_op jit(solution)/shard_map/ppermute | solution.py:445
  45.3 0.9 %collective-permute-done.7.m1 = bf16[32,1024]{1,0:T(8,128)(2,1)S(1)} collective-permute-done((bf16[32,1024]{1,0:T(8,128)(2,1)S(1)}, bf16[32,1024]{1,0:T(8,128)(2,1)S(1)}, u32[]{:S(2)}, u32[]{:S(2)}) %collective-permute-start.7) | collective-permute-done | bytes 65568 | tf_op jit(solution)/shard_map/ppermute | solution.py:445
  46.2 1.4 %collective-permute-done.6.m2 = bf16[32,1024]{1,0:T(8,128)(2,1)S(1)} collective-permute-done((bf16[32,1024]{1,0:T(8,128)(2,1)S(1)}, bf16[32,1024]{1,0:T(8,128)(2,1)S(1)}, u32[]{:S(2)}, u32[]{:S(2)}) %collective-permute-start.6) | collective-permute-done | bytes 65568 | tf_op jit(solution)/shard_map/ppermute | solution.py:445
  47.6 6.7 %deblur.1 = (f32[32,8,128]{2,1,0:T(8,128)}, f32[32,8,128]{2,1,0:T(8,128)}) custom-call(s32[1]{0:T(128)} %bitcast.at_ref, f32[3,17]{1,0:T(4,128)S(1)} %copy-done.1, f32[32,1024]{1,0:T(8,128)S(1)} %get-tuple-element.37.own_ref, bf16[32,1024]{1,0:T(8,128)(2,1)S(1)} %collective-permute-done.6.m2, bf16[32,1024]{1,0:T(8,128)(2,1)S(1)} %collective-permute-done.7.m1, ...), custom_call_target="tpu_custom_call" | custom-call | tf_op jit(solution)/shard_map/deblur/pallas_call | solution.py:447
  (8 shorter events, 0.1 us)
Async XLA Ops:
  2.5 10.9 %collective-permute-start.2 = (bf16[19,2,1536]{2,1,0:T(2,128)(2,1)}, bf16[19,2,1536]{2,1,0:T(2,128)(2,1)S(1)}, u32[]{:S(2)}, u32[]{:S(2)}) collective-permute-start(bf16[19,2,1536]{2,1,0:T(2,128)(2,1)} %get-tuple-element.21), channel_id=1, source_target_pairs={{0,1},{1,0},{2,3},{3,2},{4,5},{5,4},{6,7},{7,6},{8,9},{9,8},{10,11... | collective-permute-start | bytes 350216 | tf_op jit(solution)/shard_map/ppermute | solution.py:421
  5.6 12.3 %collective-permute-start = (bf16[19,2,1536]{2,1,0:T(2,128)(2,1)}, bf16[19,2,1536]{2,1,0:T(2,128)(2,1)S(1)}, u32[]{:S(2)}, u32[]{:S(2)}) collective-permute-start(bf16[19,2,1536]{2,1,0:T(2,128)(2,1)} %get-tuple-element.19), channel_id=1, source_target_pairs={{0,2},{1,3},{2,0},{3,1},{4,6},{5,7},{6,4},{7,5},{8,10},{9,11},{10,... | collective-permute-start | bytes 350216 | tf_op jit(solution)/shard_map/ppermute | solution.py:421
  8.2 9.7 %collective-permute-start.1 = (bf16[19,2,1536]{2,1,0:T(2,128)(2,1)}, bf16[19,2,1536]{2,1,0:T(2,128)(2,1)S(1)}, u32[]{:S(2)}, u32[]{:S(2)}) collective-permute-start(bf16[19,2,1536]{2,1,0:T(2,128)(2,1)} %get-tuple-element.20), channel_id=1, source_target_pairs={{0,3},{1,2},{2,1},{3,0},{4,7},{5,6},{6,5},{7,4},{8,11},{9,10},{10,... | collective-permute-start | bytes 350216 | tf_op jit(solution)/shard_map/ppermute | solution.py:421
  8.2 0.9 %copy-start = (bf16[19,2,1536]{2,1,0:T(2,128)(2,1)S(1)}, bf16[19,2,1536]{2,1,0:T(2,128)(2,1)}, u32[]{:S(2)}) copy-start(bf16[19,2,1536]{2,1,0:T(2,128)(2,1)} %get-tuple-element.22.refs_0_) | copy-start | bytes 350212
  17.9 24.2 %copy-start.1 = (f32[3,17]{1,0:T(4,128)S(1)}, f32[3,17]{1,0:T(4,128)}, u32[]{:S(2)}) copy-start(f32[3,17]{1,0:T(4,128)} %taps_ref.2) | copy-start | bytes 616
  29.9 6.3 %collective-permute-start.5 = (f16[32,1024]{1,0:T(8,128)(2,1)S(1)}, f16[32,1024]{1,0:T(8,128)(2,1)S(1)}, u32[]{:S(2)}, u32[]{:S(2)}) collective-permute-start(f16[32,1024]{1,0:T(8,128)(2,1)S(1)} %convert_element_type.18), channel_id=1, source_target_pairs={{0,3},{1,2},{2,1},{3,0},{4,7},{5,6},{6,5},{7,4},{8,11},{9,10},{10,... | collective-permute-start | bytes 196616 | tf_op jit(solution)/shard_map/ppermute | solution.py:394
  33.8 5.2 %collective-permute-start.4 = (f16[32,1024]{1,0:T(8,128)(2,1)S(1)}, f16[32,1024]{1,0:T(8,128)(2,1)S(1)}, u32[]{:S(2)}, u32[]{:S(2)}) collective-permute-start(f16[32,1024]{1,0:T(8,128)(2,1)S(1)} %convert_element_type.18), channel_id=1, source_target_pairs={{0,2},{1,3},{2,0},{3,1},{4,6},{5,7},{6,4},{7,5},{8,10},{9,11},{10,... | collective-permute-start | bytes 196616 | tf_op jit(solution)/shard_map/ppermute | solution.py:394
  33.8 5.2 %collective-permute-start.3 = (f16[32,1024]{1,0:T(8,128)(2,1)S(1)}, f16[32,1024]{1,0:T(8,128)(2,1)S(1)}, u32[]{:S(2)}, u32[]{:S(2)}) collective-permute-start(f16[32,1024]{1,0:T(8,128)(2,1)S(1)} %convert_element_type.18), channel_id=1, source_target_pairs={{0,1},{1,0},{2,3},{3,2},{4,5},{5,4},{6,7},{7,6},{8,9},{9,8},{10,11... | collective-permute-start | bytes 196616 | tf_op jit(solution)/shard_map/ppermute | solution.py:394
  39.1 5.5 %collective-permute-start.9 = (bf16[32,1024]{1,0:T(8,128)(2,1)S(1)}, bf16[32,1024]{1,0:T(8,128)(2,1)S(1)}, u32[]{:S(2)}, u32[]{:S(2)}) collective-permute-start(bf16[32,1024]{1,0:T(8,128)(2,1)S(1)} %get-tuple-element.36), channel_id=1, source_target_pairs={{0,24},{4,28},{8,0},{12,4},{16,8},{20,12},{24,16},{28,20},{1,25},{... | collective-permute-start | bytes 196616 | tf_op jit(solution)/shard_map/ppermute | solution.py:445
  41.6 3.7 %collective-permute-start.8 = (bf16[32,1024]{1,0:T(8,128)(2,1)S(1)}, bf16[32,1024]{1,0:T(8,128)(2,1)S(1)}, u32[]{:S(2)}, u32[]{:S(2)}) collective-permute-start(bf16[32,1024]{1,0:T(8,128)(2,1)S(1)} %get-tuple-element.36), channel_id=1, source_target_pairs={{0,28},{4,0},{8,4},{12,8},{16,12},{20,16},{24,20},{28,24},{1,29},{... | collective-permute-start | bytes 196616 | tf_op jit(solution)/shard_map/ppermute | solution.py:445
  41.6 4.6 %collective-permute-start.7 = (bf16[32,1024]{1,0:T(8,128)(2,1)S(1)}, bf16[32,1024]{1,0:T(8,128)(2,1)S(1)}, u32[]{:S(2)}, u32[]{:S(2)}) collective-permute-start(bf16[32,1024]{1,0:T(8,128)(2,1)S(1)} %get-tuple-element.36), channel_id=1, source_target_pairs={{0,4},{4,8},{8,12},{12,16},{16,20},{20,24},{24,28},{28,0},{1,5},{5... | collective-permute-start | bytes 196616 | tf_op jit(solution)/shard_map/ppermute | solution.py:445
  42.1 5.5 %collective-permute-start.6 = (bf16[32,1024]{1,0:T(8,128)(2,1)S(1)}, bf16[32,1024]{1,0:T(8,128)(2,1)S(1)}, u32[]{:S(2)}, u32[]{:S(2)}) collective-permute-start(bf16[32,1024]{1,0:T(8,128)(2,1)S(1)} %get-tuple-element.36), channel_id=1, source_target_pairs={{0,8},{4,12},{8,16},{12,20},{16,24},{20,28},{24,0},{28,4},{1,9},{5... | collective-permute-start | bytes 196616 | tf_op jit(solution)/shard_map/ppermute | solution.py:445

commit v9 on v8

--- a/solution.py
+++ b/solution.py
@@ -195,7 +195,7 @@
         for y, (re, im) in enumerate(butterfly(values, 3)):
             out_ref[:, y * CZ : (y + 1) * CZ] += re * re + im * im
 
-    batch = 8 if final else own
+    batch = own
     each = parts * batch // own
 
     def some(n, fn):
@@ -423,9 +423,9 @@
     at = (me * own).reshape(1)
     scale = SMALLER / (freqs * width * groups)
     held = beams_call(own, width, None, at, blocks[:1], None)
-    if groups > 2:
-        held = beams_call(own, width, None, at, blocks[1:2], held)
-    local = beams_call(own, width, scale, at, blocks[2 if groups > 2 else 1 :], held)
+    for block in blocks[1:-1]:
+        held = beams_call(own, width, None, at, [block], held)
+    local = beams_call(own, width, scale, at, blocks[-1:], held)
 
     half, taps = lax.optimization_barrier((local.astype(jnp.float16), spread_taps))
     shapes = [(m, 3 * n) for n, m in blur_rows()] + [(6 * CZ, 2 * CZ)]

time: 54.5 us -> 55.1 us (1.011)
    ppermute x3, waiting for transfers between devices: 0.01 us -> 0.96 us  [per_device(): lax.ppermute(blocks[k], 'sta', moves(k, groups))]
    pallas_call x3 -> x4, Pallas kernels: 20.8 us -> 20.8 us  [beams_call(): pl.pallas_call(functools.partial(beam_kernel, chunks, own, width, scale,...]
  transfers between devices with their start and end apart: 10 -> 10, of which waited for: 5 -> 6; matrix products, arithmetic and copies ran while one was open for 0% -> 0% of each run, Pallas kernels for 21% -> 28%
where the time goes in v9:
time: 55.1 us; the launch traced here: 54.9 us
  Pallas kernels  31.9 us (58%)
  starting transfers between devices  13.5 us (25%)
  waiting for transfers between devices  7.88 us (14%)
  local copies, waits for them, and re-layouts  0.9 us (2%)
  between operations  0.73 us (1%)
    pallas_call x4, Pallas kernels, beams_call(): pl.pallas_call(functools.partial(beam_kernel, chunks, own, width, scale,...  20.8 us
    pallas_call x1, Pallas kernels, per_device(): pl.pallas_call(functools.partial(deblur_kernel, tiles), out_shape=(tile,...  6.71 us
    ppermute x3, starting transfers between devices, per_device(): lax.ppermute(blocks[k], 'sta', moves(k, groups))  5.68 us
    ppermute x3, starting transfers between devices, summed_over(): lax.ppermute(half, axis, moves(k, size))  4.45 us
    ppermute x3, waiting for transfers between devices, summed_over(): lax.ppermute(half, axis, moves(k, size))  4.29 us
    ppermute x4, starting transfers between devices, per_device(): lax.ppermute(narrow, 'grid', [(i, (i + shift) % tiles) for i in range(til...  3.38 us
    ppermute x4, waiting for transfers between devices, per_device(): lax.ppermute(narrow, 'grid', [(i, (i + shift) % tiles) for i in range(til...  2.63 us
    pallas_call x1, Pallas kernels, per_device(): pl.pallas_call(band_kernel, out_shape=[jax.ShapeDtypeStruct(shape, jnp.bf...  2.47 us
  transfers between devices with their start and end apart: 10, of which 6 were waited for; matrix products, arithmetic and copies ran while one was open for 0% of the time, Pallas kernels for 28%

profile of v9, /device:TPU:0, one launch (start us, length us, event | category | flops | bytes accessed | tf_op | source)
XLA Modules:
  0.0 54.9 jit_solution(12449903940068949559)
XLA Ops:
  0.6 1.9 %bundles.1 = (bf16[19,2,1536]{2,1,0:T(2,128)(2,1)}, bf16[19,2,1536]{2,1,0:T(2,128)(2,1)}, bf16[19,2,1536]{2,1,0:T(2,128)(2,1)}, bf16[19,2,1536]{2,1,0:T(2,128)(2,1)}) custom-call(s32[1]{0:T(128)} %bitcast.2.me_ref, bf16[64,2,1536]{2,1,0:T(2,128)(2,1)} %spectra_ref.1, s32[1,1536]{1,0:T(1,128)} %lag_ref.1, bf16[3,1536]{1,0:T(4,128)(2,1)} %bitcast.6), custom_call_target="tpu_custom_call" | custom-call | tf_op jit(solution)/shard_map/bundles/pallas_call | solution.py:408
  2.5 3.1 %collective-permute-start.2 = (bf16[19,2,1536]{2,1,0:T(2,128)(2,1)}, bf16[19,2,1536]{2,1,0:T(2,128)(2,1)S(1)}, u32[]{:S(2)}, u32[]{:S(2)}) collective-permute-start(bf16[19,2,1536]{2,1,0:T(2,128)(2,1)} %get-tuple-element.21), channel_id=1, source_target_pairs={{0,1},{1,0},{2,3},{3,2},{4,5},{5,4},{6,7},{7,6},{8,9},{9,8},{10,11... | collective-permute-start | bytes 350216 | tf_op jit(solution)/shard_map/ppermute | solution.py:421
  5.6 2.5 %collective-permute-start = (bf16[19,2,1536]{2,1,0:T(2,128)(2,1)}, bf16[19,2,1536]{2,1,0:T(2,128)(2,1)S(1)}, u32[]{:S(2)}, u32[]{:S(2)}) collective-permute-start(bf16[19,2,1536]{2,1,0:T(2,128)(2,1)} %get-tuple-element.19), channel_id=1, source_target_pairs={{0,3},{1,2},{2,1},{3,0},{4,7},{5,6},{6,5},{7,4},{8,11},{9,10},{10,... | collective-permute-start | bytes 350216 | tf_op jit(solution)/shard_map/ppermute | solution.py:421
  8.1 0.1 collective-permute-start.1
  8.2 0.9 %copy-done = bf16[19,2,1536]{2,1,0:T(2,128)(2,1)S(1)} copy-done((bf16[19,2,1536]{2,1,0:T(2,128)(2,1)S(1)}, bf16[19,2,1536]{2,1,0:T(2,128)(2,1)}, u32[]{:S(2)}) %copy-start) | copy-done | bytes 116760
  9.1 4.3 %beams_own.1.refs_1_ = f32[16,256,256]{2,1,0:T(8,128)S(1)} custom-call(s32[1]{0:T(128)} %bitcast.1.first_ref, bf16[19,2,1536]{2,1,0:T(2,128)(2,1)S(1)} %copy-done), custom_call_target="tpu_custom_call" | custom-call | bytes 8 | tf_op jit(solution)/shard_map/beams_own/pallas_call | solution.py:260
  13.4 0.0 collective-permute-done.2.refs_0_
  13.4 4.5 %beams_more.2.refs_1_ = f32[16,256,256]{2,1,0:T(8,128)S(1)} custom-call(s32[1]{0:T(128)} %bitcast.1.first_ref, bf16[19,2,1536]{2,1,0:T(2,128)(2,1)S(1)} %collective-permute-done.2.refs_0_, f32[16,256,256]{2,1,0:T(8,128)S(1)} %beams_own.1.refs_1_), custom_call_target="tpu_custom_call" | custom-call | flops 6442450944 | bytes 8 | tf_op jit(solution)/shard_map/beams_more/pallas_call | solution.py:260
  17.9 1.0 %collective-permute-done.1.refs_0_ = bf16[19,2,1536]{2,1,0:T(2,128)(2,1)S(1)} collective-permute-done((bf16[19,2,1536]{2,1,0:T(2,128)(2,1)}, bf16[19,2,1536]{2,1,0:T(2,128)(2,1)S(1)}, u32[]{:S(2)}, u32[]{:S(2)}) %collective-permute-start.1) | collective-permute-done | bytes 116768 | tf_op jit(solution)/shard_map/ppermute | solution.py:421
  18.8 4.4 %beams_more.3.refs_1_ = f32[16,256,256]{2,1,0:T(8,128)S(1)} custom-call(s32[1]{0:T(128)} %bitcast.1.first_ref, bf16[19,2,1536]{2,1,0:T(2,128)(2,1)S(1)} %collective-permute-done.1.refs_0_, f32[16,256,256]{2,1,0:T(8,128)S(1)} %beams_more.2.refs_1_), custom_call_target="tpu_custom_call" | custom-call | flops 6442450944 | bytes 8 | tf_op jit(solution)/shard_map/beams_more/pallas_call | solution.py:260
  23.3 0.0 copy-start.1
  23.3 7.6 %beams_last.1 = f32[32,1024]{1,0:T(8,128)S(1)} custom-call(s32[1]{0:T(128)} %bitcast.1.first_ref, bf16[19,2,1536]{2,1,0:T(2,128)(2,1)S(1)} %collective-permute-done.refs_0_, f32[16,256,256]{2,1,0:T(8,128)S(1)} %beams_more.3.refs_1_), custom_call_target="tpu_custom_call" | custom-call | flops 6442450944 | bytes 8 | tf_op jit(solution)/shard_map/beams_last/pallas_call | solution.py:260
  30.9 2.7 %collective-permute-start.5 = (f16[32,1024]{1,0:T(8,128)(2,1)S(1)}, f16[32,1024]{1,0:T(8,128)(2,1)S(1)}, u32[]{:S(2)}, u32[]{:S(2)}) collective-permute-start(f16[32,1024]{1,0:T(8,128)(2,1)S(1)} %convert_element_type.18), channel_id=1, source_target_pairs={{0,3},{1,2},{2,1},{3,0},{4,7},{5,6},{6,5},{7,4},{8,11},{9,10},{10,... | collective-permute-start | bytes 196616 | tf_op jit(solution)/shard_map/ppermute | solution.py:394
  33.7 1.7 %collective-permute-start.3 = (f16[32,1024]{1,0:T(8,128)(2,1)S(1)}, f16[32,1024]{1,0:T(8,128)(2,1)S(1)}, u32[]{:S(2)}, u32[]{:S(2)}) collective-permute-start(f16[32,1024]{1,0:T(8,128)(2,1)S(1)} %convert_element_type.18), channel_id=1, source_target_pairs={{0,1},{1,0},{2,3},{3,2},{4,5},{5,4},{6,7},{7,6},{8,9},{9,8},{10,11... | collective-permute-start | bytes 196616 | tf_op jit(solution)/shard_map/ppermute | solution.py:394
  35.4 1.8 %collective-permute-done.5 = f16[32,1024]{1,0:T(8,128)(2,1)S(1)} collective-permute-done((f16[32,1024]{1,0:T(8,128)(2,1)S(1)}, f16[32,1024]{1,0:T(8,128)(2,1)S(1)}, u32[]{:S(2)}, u32[]{:S(2)}) %collective-permute-start.5) | collective-permute-done | bytes 65568 | tf_op jit(solution)/shard_map/ppermute | solution.py:394
  37.2 2.5 %collective-permute-done.4 = f16[32,1024]{1,0:T(8,128)(2,1)S(1)} collective-permute-done((f16[32,1024]{1,0:T(8,128)(2,1)S(1)}, f16[32,1024]{1,0:T(8,128)(2,1)S(1)}, u32[]{:S(2)}, u32[]{:S(2)}) %collective-permute-start.4) | collective-permute-done | bytes 65568 | tf_op jit(solution)/shard_map/ppermute | solution.py:394
  39.7 2.5 %collective-permute-start.9 = (bf16[32,1024]{1,0:T(8,128)(2,1)S(1)}, bf16[32,1024]{1,0:T(8,128)(2,1)S(1)}, u32[]{:S(2)}, u32[]{:S(2)}) collective-permute-start(bf16[32,1024]{1,0:T(8,128)(2,1)S(1)} %get-tuple-element.36), channel_id=1, source_target_pairs={{0,24},{4,28},{8,0},{12,4},{16,8},{20,12},{24,16},{28,20},{1,25},{... | collective-permute-start | bytes 196616 | tf_op jit(solution)/shard_map/ppermute | solution.py:445
  42.2 0.5 collective-permute-start.7
  42.7 0.4 collective-permute-start.6
  43.1 2.5 %bands.1 = (bf16[144,480]{1,0:T(8,128)(2,1)S(1)}, bf16[128,432]{1,0:T(8,128)(2,1)S(1)}, bf16[112,384]{1,0:T(8,128)(2,1)S(1)}, bf16[96,336]{1,0:T(8,128)(2,1)S(1)...) custom-call(f32[3,17]{1,0:T(4,128)S(1)} %copy-done.1), custom_call_target="tpu_custom_call" | custom-call | flops 10000000 | bytes 2000000 | tf_op jit(solution)/shard_map/bands/pallas_call | solution.py:432
  45.6 0.2 collective-permute-done.8.p1
  45.8 1.0 %collective-permute-done.7.m1 = bf16[32,1024]{1,0:T(8,128)(2,1)S(1)} collective-permute-done((bf16[32,1024]{1,0:T(8,128)(2,1)S(1)}, bf16[32,1024]{1,0:T(8,128)(2,1)S(1)}, u32[]{:S(2)}, u32[]{:S(2)}) %collective-permute-start.7) | collective-permute-done | bytes 65568 | tf_op jit(solution)/shard_map/ppermute | solution.py:445
  46.8 1.4 %collective-permute-done.6.m2 = bf16[32,1024]{1,0:T(8,128)(2,1)S(1)} collective-permute-done((bf16[32,1024]{1,0:T(8,128)(2,1)S(1)}, bf16[32,1024]{1,0:T(8,128)(2,1)S(1)}, u32[]{:S(2)}, u32[]{:S(2)}) %collective-permute-start.6) | collective-permute-done | bytes 65568 | tf_op jit(solution)/shard_map/ppermute | solution.py:445
  48.2 6.7 %deblur.1 = (f32[32,8,128]{2,1,0:T(8,128)}, f32[32,8,128]{2,1,0:T(8,128)}) custom-call(s32[1]{0:T(128)} %bitcast.at_ref, f32[3,17]{1,0:T(4,128)S(1)} %copy-done.1, f32[32,1024]{1,0:T(8,128)S(1)} %get-tuple-element.37.own_ref, bf16[32,1024]{1,0:T(8,128)(2,1)S(1)} %collective-permute-done.6.m2, bf16[32,1024]{1,0:T(8,128)(2,1)S(1)} %collective-permute-done.7.m1, ...), custom_call_target="tpu_custom_call" | custom-call | tf_op jit(solution)/shard_map/deblur/pallas_call | solution.py:447
  (9 shorter events, 0.1 us)
Async XLA Ops:
  2.5 10.8 %collective-permute-start.2 = (bf16[19,2,1536]{2,1,0:T(2,128)(2,1)}, bf16[19,2,1536]{2,1,0:T(2,128)(2,1)S(1)}, u32[]{:S(2)}, u32[]{:S(2)}) collective-permute-start(bf16[19,2,1536]{2,1,0:T(2,128)(2,1)} %get-tuple-element.21), channel_id=1, source_target_pairs={{0,1},{1,0},{2,3},{3,2},{4,5},{5,4},{6,7},{7,6},{8,9},{9,8},{10,11... | collective-permute-start | bytes 350216 | tf_op jit(solution)/shard_map/ppermute | solution.py:421
  5.6 17.7 %collective-permute-start = (bf16[19,2,1536]{2,1,0:T(2,128)(2,1)}, bf16[19,2,1536]{2,1,0:T(2,128)(2,1)S(1)}, u32[]{:S(2)}, u32[]{:S(2)}) collective-permute-start(bf16[19,2,1536]{2,1,0:T(2,128)(2,1)} %get-tuple-element.19), channel_id=1, source_target_pairs={{0,3},{1,2},{2,1},{3,0},{4,7},{5,6},{6,5},{7,4},{8,11},{9,10},{10,... | collective-permute-start | bytes 350216 | tf_op jit(solution)/shard_map/ppermute | solution.py:421
  8.1 10.7 %collective-permute-start.1 = (bf16[19,2,1536]{2,1,0:T(2,128)(2,1)}, bf16[19,2,1536]{2,1,0:T(2,128)(2,1)S(1)}, u32[]{:S(2)}, u32[]{:S(2)}) collective-permute-start(bf16[19,2,1536]{2,1,0:T(2,128)(2,1)} %get-tuple-element.20), channel_id=1, source_target_pairs={{0,2},{1,3},{2,0},{3,1},{4,6},{5,7},{6,4},{7,5},{8,10},{9,11},{10,... | collective-permute-start | bytes 350216 | tf_op jit(solution)/shard_map/ppermute | solution.py:421
  8.2 0.9 %copy-start = (bf16[19,2,1536]{2,1,0:T(2,128)(2,1)S(1)}, bf16[19,2,1536]{2,1,0:T(2,128)(2,1)}, u32[]{:S(2)}) copy-start(bf16[19,2,1536]{2,1,0:T(2,128)(2,1)} %get-tuple-element.22.refs_0_) | copy-start | bytes 350212
  23.3 19.8 %copy-start.1 = (f32[3,17]{1,0:T(4,128)S(1)}, f32[3,17]{1,0:T(4,128)}, u32[]{:S(2)}) copy-start(f32[3,17]{1,0:T(4,128)} %taps_ref.2) | copy-start | bytes 616
  30.9 6.3 %collective-permute-start.5 = (f16[32,1024]{1,0:T(8,128)(2,1)S(1)}, f16[32,1024]{1,0:T(8,128)(2,1)S(1)}, u32[]{:S(2)}, u32[]{:S(2)}) collective-permute-start(f16[32,1024]{1,0:T(8,128)(2,1)S(1)} %convert_element_type.18), channel_id=1, source_target_pairs={{0,3},{1,2},{2,1},{3,0},{4,7},{5,6},{6,5},{7,4},{8,11},{9,10},{10,... | collective-permute-start | bytes 196616 | tf_op jit(solution)/shard_map/ppermute | solution.py:394
  33.6 6.0 %collective-permute-start.4 = (f16[32,1024]{1,0:T(8,128)(2,1)S(1)}, f16[32,1024]{1,0:T(8,128)(2,1)S(1)}, u32[]{:S(2)}, u32[]{:S(2)}) collective-permute-start(f16[32,1024]{1,0:T(8,128)(2,1)S(1)} %convert_element_type.18), channel_id=1, source_target_pairs={{0,2},{1,3},{2,0},{3,1},{4,6},{5,7},{6,4},{7,5},{8,10},{9,11},{10,... | collective-permute-start | bytes 196616 | tf_op jit(solution)/shard_map/ppermute | solution.py:394
  33.7 6.0 %collective-permute-start.3 = (f16[32,1024]{1,0:T(8,128)(2,1)S(1)}, f16[32,1024]{1,0:T(8,128)(2,1)S(1)}, u32[]{:S(2)}, u32[]{:S(2)}) collective-permute-start(f16[32,1024]{1,0:T(8,128)(2,1)S(1)} %convert_element_type.18), channel_id=1, source_target_pairs={{0,1},{1,0},{2,3},{3,2},{4,5},{5,4},{6,7},{7,6},{8,9},{9,8},{10,11... | collective-permute-start | bytes 196616 | tf_op jit(solution)/shard_map/ppermute | solution.py:394
  39.7 5.9 %collective-permute-start.9 = (bf16[32,1024]{1,0:T(8,128)(2,1)S(1)}, bf16[32,1024]{1,0:T(8,128)(2,1)S(1)}, u32[]{:S(2)}, u32[]{:S(2)}) collective-permute-start(bf16[32,1024]{1,0:T(8,128)(2,1)S(1)} %get-tuple-element.36), channel_id=1, source_target_pairs={{0,24},{4,28},{8,0},{12,4},{16,8},{20,12},{24,16},{28,20},{1,25},{... | collective-permute-start | bytes 196616 | tf_op jit(solution)/shard_map/ppermute | solution.py:445
  42.2 3.6 %collective-permute-start.8 = (bf16[32,1024]{1,0:T(8,128)(2,1)S(1)}, bf16[32,1024]{1,0:T(8,128)(2,1)S(1)}, u32[]{:S(2)}, u32[]{:S(2)}) collective-permute-start(bf16[32,1024]{1,0:T(8,128)(2,1)S(1)} %get-tuple-element.36), channel_id=1, source_target_pairs={{0,28},{4,0},{8,4},{12,8},{16,12},{20,16},{24,20},{28,24},{1,29},{... | collective-permute-start | bytes 196616 | tf_op jit(solution)/shard_map/ppermute | solution.py:445
  42.2 4.6 %collective-permute-start.7 = (bf16[32,1024]{1,0:T(8,128)(2,1)S(1)}, bf16[32,1024]{1,0:T(8,128)(2,1)S(1)}, u32[]{:S(2)}, u32[]{:S(2)}) collective-permute-start(bf16[32,1024]{1,0:T(8,128)(2,1)S(1)} %get-tuple-element.36), channel_id=1, source_target_pairs={{0,4},{4,8},{8,12},{12,16},{16,20},{20,24},{24,28},{28,0},{1,5},{5... | collective-permute-start | bytes 196616 | tf_op jit(solution)/shard_map/ppermute | solution.py:445
  42.7 5.5 %collective-permute-start.6 = (bf16[32,1024]{1,0:T(8,128)(2,1)S(1)}, bf16[32,1024]{1,0:T(8,128)(2,1)S(1)}, u32[]{:S(2)}, u32[]{:S(2)}) collective-permute-start(bf16[32,1024]{1,0:T(8,128)(2,1)S(1)} %get-tuple-element.36), channel_id=1, source_target_pairs={{0,8},{4,12},{8,16},{12,20},{16,24},{20,28},{24,0},{28,4},{1,9},{5... | collective-permute-start | bytes 196616 | tf_op jit(solution)/shard_map/ppermute | solution.py:445
